TPU v7x, 128 devices: a whole 4x4x4 slice. The times are simulated.
128 devices in a mesh: band: 8 (over x_lo, y), grid: 16 (over z, x_hi, core).
Axes of the slice: x: 4 (x_hi: 2, x_lo: 2; x = x_hi * 2 + x_lo), y: 4, z: 4, core: 2. Of those that a mesh axis runs over, the one named last changes fastest.
Arguments:
- orbitals: float32 [8, 96, 9216], P('band', 'grid'), may hold values from -6.5 to 6.5
- blocks: float32 [128, 96, 9216], P('band', 'grid'), may hold values from -6.5 to 6.5
- owner: int32 [2], replicated, may hold values from 0 to 7, as said below
Outputs:
- local_exchange: float32 [8, 96, 9216], P('band', 'grid')
- block_exchange: float32 [2, 16, 96, 9216], P(None, 'band', 'grid')
Inputs may be any that keep to these rules, and one draw needn't show every extreme that they name: `owner`: the 2 rounds name different owners, and one of them is the last index of band.
All inputs are finite; a program needn't handle non-finite values.
Results may differ from a plain program's by a relative error of at most 0.0001.
Values sent between devices are 32-bit elements; how exact they have to be, the bound alone decides.
No kernel may reach another device: no remote copies, remote signals or barrier semaphores. Data moves between devices by JAX's collectives and lax.ppermute only.
A program may use at most 192 MiB of HBM per device.

v0:
```python
import math

import jax
import jax.numpy as jnp
from jax import lax
from jax.sharding import PartitionSpec as P

NX = 96
NY = 96
NZ = 96
ROUNDS = 2


mixing = 0.25
cell_length = 41.04
highest = lax.Precision.HIGHEST


def from_root(value, axis, source):
    kept = jnp.where(lax.axis_index(axis) == source, value, 0).astype(value.dtype)
    return lax.psum(kept, axis)


def angle_parts(length, sign_value):
    points = jnp.arange(length, dtype=jnp.int32)
    phase_index = points[:, None] * points[None, :] % length
    angles = phase_index.astype(jnp.float32) * (2.0 * math.pi / length)
    return (jnp.cos(angles), sign_value * jnp.sin(angles))


def fourier_table(length, sign_value):
    cosine, sine_part = angle_parts(length, sign_value)
    from_real = jnp.stack([cosine, sine_part], axis=-1)
    from_imag = jnp.stack([-sine_part, cosine], axis=-1)
    return jnp.stack([from_real, from_imag], axis=1)


def forward_z(values):
    length = values.shape[3]
    cosine, sine_part = angle_parts(length, -1.0)
    matrix = jnp.stack([cosine, sine_part], axis=1).reshape(length, 2 * length)
    result = jnp.dot(values, matrix, precision=highest)
    return result.reshape(values.shape[0], values.shape[1], values.shape[2], 2, length)


def inverse_z(values):
    length = values.shape[4]
    cosine, sine_part = angle_parts(length, 1.0)
    matrix = jnp.stack([cosine, -sine_part], axis=0).reshape(2 * length, length)
    flat_rows = values.reshape(values.shape[0], values.shape[1], values.shape[2], 2 * length)
    return jnp.dot(flat_rows, matrix, precision=highest)


def along_y(values, sign_value):
    return jnp.einsum(
        "axyqk,yqvs->axvsk", values, fourier_table(values.shape[2], sign_value), precision=highest
    )


def along_x(values, sign_value):
    return jnp.einsum(
        "axyqk,xqus->auysk", values, fourier_table(values.shape[1], sign_value), precision=highest
    )


def signed_index(points, length):
    return jnp.where(points < length // 2, points, points - length).astype(jnp.float32)


def coulomb(x_index, y_index):
    spacing = 2.0 * math.pi / cell_length
    wave_x = signed_index(x_index, NX) * spacing
    wave_y = signed_index(y_index, NY) * spacing
    wave_z = signed_index(jnp.arange(NZ, dtype=jnp.int32), NZ) * spacing
    squared = (
        wave_x[:, None, None] * wave_x[:, None, None]
        + wave_y[None, :, None] * wave_y[None, :, None]
        + wave_z[None, None, :] * wave_z[None, None, :]
    )
    safe = jnp.where(squared > 0, squared, jnp.float32(1.0))
    scaled = 4.0 * math.pi / (safe * float(NX * NY * NZ))
    return jnp.where(squared > 0, scaled, jnp.float32(0.0))


def potential_pencils(pair_field):
    pieces = pair_field.shape[0]
    slab_x = pair_field.shape[1]
    groups = lax.axis_size("grid")
    slab_y = NY // groups
    spectrum = along_y(forward_z(pair_field), -1.0)
    spectrum = lax.all_to_all(
        spectrum.reshape(pieces, slab_x, groups, slab_y * 2 * NZ),
        "grid",
        split_axis=2,
        concat_axis=1,
        tiled=True,
    )
    spectrum = spectrum.reshape(pieces, NX, slab_y, 2, NZ)
    y_index = lax.axis_index("grid") * slab_y + jnp.arange(slab_y, dtype=jnp.int32)
    kernel = coulomb(jnp.arange(NX, dtype=jnp.int32), y_index)
    spectrum = along_x(along_x(spectrum, -1.0) * kernel[:, :, None, :], 1.0)
    spectrum = lax.all_to_all(
        spectrum.reshape(pieces, NX, 1, slab_y * 2 * NZ),
        "grid",
        split_axis=1,
        concat_axis=2,
        tiled=True,
    )
    spectrum = spectrum.reshape(pieces, slab_x, NY, 2, NZ)
    return inverse_z(along_y(spectrum, 1.0))


def per_device(orbitals, blocks, owner):
    slab_x = orbitals.shape[1]
    flat_yz = orbitals.shape[2]
    batches = [[turn_index] for turn_index in range(ROUNDS)]
    partner_count = orbitals.shape[0]
    carried = jnp.zeros((partner_count, slab_x, flat_yz), jnp.float32)
    pieces_out = []
    for batch in batches:
        mine = jnp.stack([from_root(blocks, "band", owner[turn_index]) for turn_index in batch])
        depth = mine.shape[0]
        rows_used = mine.shape[1]
        pair_field = (mine[:, :, None] * orbitals[None, None]).reshape(
            depth * rows_used * partner_count, slab_x, NY, NZ
        )
        potential = potential_pencils(pair_field)
        potential = potential.reshape(depth, rows_used, partner_count, slab_x, flat_yz)
        carried = carried + jnp.sum(mine[:, :, None] * potential, axis=(0, 1))
        terms = jnp.sum(potential * orbitals[None, None], axis=2)
        pieces_out.append(
            -mixing * lax.psum_scatter(terms, "band", scatter_dimension=1, tiled=True)
        )
    return (-mixing * carried, jnp.concatenate(pieces_out, axis=0))


def solution(mesh):
    in_specs = (P("band", "grid", None), P("band", "grid", None), P())
    out_specs = (P("band", "grid", None), P(None, "band", "grid", None))
    return jax.shard_map(
        per_device, mesh=mesh, in_specs=in_specs, out_specs=out_specs, check_vma=False
    )
```

profile of v0, /device:TPU:28, one launch (start us, length us, event | category | flops | bytes accessed | tf_op | source)
XLA Modules:
  0.0 816.7 jit_solution(17382070433513569119)
XLA Ops:
  9.8 5.6 broadcast_select_fusion
  19.7 155.5 %all-reduce.9.cloned.1.call-done = (f32[16,6,9216]{2,0,1:T(8,128)}, f32[16,6,9216]{2,0,1:T(8,128)}) async-done(((f32[16,6,9216]{2,0,1:T(8,128)}, f32[16,6,9216]{2,0,1:T(8,128)}), (f32[16,6,9216]{2,0,1:T(8,128)}, f32[16,6,9216]{2,0,1:T(8,128)})) %all-reduce.9.cloned.1.call-update) | async-done | bytes 7077904 | tf_op jit(solution)/shard_map/psum | solution.py:21
  175.3 5.7 broadcast_multiply_fusion.2
  180.9 5.8 reshape.393
  186.7 10.1 %fusion.22 = f32[16,6,96,2,96]{4,2,3,1,0:T(8,128)S(1)} fusion(f32[96,1,96]{0,2,1:T(8,128)} %sine_multiply_fusion, f32[96,1,96]{0,2,1:T(8,128)} %fusion.76, f32[16,6,96,96]{3,2,0,1:T(8,128)} %reshape.393), kind=kOutput, calls=%fused_computation.24 | convolution fusion | flops 2038450176 | bytes 10690560 | tf_op jit(solution)/shard_map/dot_general | solution.py:42
  196.9 9.6 %fusion.37 = f32[16,6,96,2,96]{4,2,1,0,3:T(8,128)S(1)} fusion(f32[16,6,96,2,96]{4,2,3,1,0:T(8,128)S(1)} %fusion.22, f32[96,1,96,2]{0,2,1,3:T(8,128)S(1)} %copy-done.3, f32[96,1,96,2]{0,2,1,3:T(8,128)S(1)} %copy-done.5), kind=kOutput, calls=%fused_computation.35 | convolution fusion | flops 4076900352 | bytes 14303232 | tf_op jit(solution)/shard_map/axyqk,yqvs->axvsk/dot_general | solution.py:55
  206.5 11.1 %copy.92 = f32[16,6,96,2,96]{4,3,2,1,0:T(2,128)} copy(f32[16,6,96,2,96]{4,2,1,0,3:T(8,128)S(1)} %fusion.37) | data formatting | bytes 14155776 | tf_op jit(solution)/shard_map/axyqk,yqvs->axvsk/transpose | solution.py:55
  217.6 12.9 %reshape.394 = f32[16,6,16,1152]{3,2,1,0:T(8,128)} reshape(f32[16,6,96,2,96]{4,3,2,1,0:T(2,128)} %copy.92) | data formatting | bytes 14155776 | tf_op jit(solution)/shard_map/reshape | solution.py:92
  230.5 10.0 %copy.93 = f32[16,6,16,1152]{3,0,1,2:T(8,128)} copy(f32[16,6,16,1152]{3,2,1,0:T(8,128)} %reshape.394) | data formatting | bytes 14155776 | tf_op jit(solution)/shard_map/reshape | solution.py:92
  240.5 7.4 all-to-all-start.2
  247.9 3.6 reshape.386
  251.6 9.8 %fusion.24 = f32[16,6,96,2,96]{4,2,3,1,0:T(8,128)S(1)} fusion(f32[96,1,96]{0,2,1:T(8,128)} %sine_multiply_fusion, f32[96,1,96]{0,2,1:T(8,128)} %fusion.76, f32[16,6,96,96]{3,2,0,1:T(8,128)} %reshape.386), kind=kOutput, calls=%fused_computation.26 | convolution fusion | flops 2038450176 | bytes 10690560 | tf_op jit(solution)/shard_map/dot_general | solution.py:42
  261.4 9.6 %fusion.34 = f32[16,6,96,2,96]{4,2,1,0,3:T(8,128)S(1)} fusion(f32[16,6,96,2,96]{4,2,3,1,0:T(8,128)S(1)} %fusion.24, f32[96,1,96,2]{0,2,1,3:T(8,128)S(1)} %copy-done.4, f32[96,1,96,2]{0,2,1,3:T(8,128)S(1)} %copy-done.6), kind=kOutput, calls=%fused_computation.34 | convolution fusion | flops 4076900352 | bytes 14303232 | tf_op jit(solution)/shard_map/axyqk,yqvs->axvsk/dot_general | solution.py:55
  271.0 11.1 %copy.81 = f32[16,6,96,2,96]{4,3,2,1,0:T(2,128)} copy(f32[16,6,96,2,96]{4,2,1,0,3:T(8,128)S(1)} %fusion.34) | data formatting | bytes 14155776 | tf_op jit(solution)/shard_map/axyqk,yqvs->axvsk/transpose | solution.py:55
  282.1 13.2 %reshape.388 = f32[16,6,16,1152]{3,2,1,0:T(8,128)} reshape(f32[16,6,96,2,96]{4,3,2,1,0:T(2,128)} %copy.81) | data formatting | bytes 14155776 | tf_op jit(solution)/shard_map/reshape | solution.py:92
  295.3 10.1 %copy.82 = f32[16,6,16,1152]{3,0,1,2:T(8,128)} copy(f32[16,6,16,1152]{3,2,1,0:T(8,128)} %reshape.388) | data formatting | bytes 14155776 | tf_op jit(solution)/shard_map/reshape | solution.py:92
  305.3 22.7 %all-to-all-done.2 = f32[16,6,16,1152]{3,0,1,2:T(8,128)} async-done(((f32[16,6,16,1152]{3,0,1,2:T(8,128)}), f32[16,6,16,1152]{3,0,1,2:T(8,128)}, u32[]{:S(2)}, u32[]{:S(2)}) %all-to-all-start.2) | async-done | bytes 7077920 | tf_op jit(solution)/shard_map/all_to_all | solution.py:91
  328.0 7.5 all-to-all-start
  335.8 13.9 %reshape.395 = f32[16,96,6,2,96]{4,3,2,0,1:T(2,128)} reshape(f32[16,16,6,1,1152]{4,0,2,1,3:T(8,128)} %bitcast.55) | data formatting | bytes 14155776 | tf_op jit(solution)/shard_map/reshape | solution.py:98
  349.7 17.9 %fusion.9 = f32[96,2,16,6,96,1]{4,0,5,1,3,2:T(8,128)S(1)} fusion(f32[16,96,6,2,96,1]{4,3,2,0,1,5:T(2,128)} %bitcast.218, f32[96,1,96,2]{0,2,1,3:T(8,128)S(1)} %copy-done.4, f32[96,1,96,2]{0,2,1,3:T(8,128)S(1)} %copy-done.6), kind=kOutput, calls=%fused_computation.10 | convolution fusion | flops 4076900352 | bytes 14303232 | tf_op jit(solution)/shard_map/axyqk,xqus->auysk/dot_general | solution.py:61
  367.6 9.7 %fusion.31 = f32[16,96,6,2,96]{4,1,2,0,3:T(8,128)S(1)} fusion(f32[96,2,16,6,96,1]{4,0,5,1,3,2:T(8,128)S(1)} %fusion.9, f32[96,6,96]{2,0,1:T(8,128)S(1)} %fusion.52, f32[96,1,96,2]{0,2,3,1:T(8,128)S(1)} %copy-done.2, f32[96,1,96,2]{0,2,3,1:T(8,128)S(1)} %copy-done.1), kind=kOutput, calls=%fused_computation.33 | convolution fusion | flops 4078669824 | bytes 14524416 | tf_op jit(solution)/shard_map/axyqk,xqus->auysk/dot_general | solution.py:61
  377.4 11.8 %copy.149 = f32[16,96,6,2,96]{4,3,2,0,1:T(2,128)} copy(f32[16,96,6,2,96]{4,1,2,0,3:T(8,128)S(1)} %fusion.31) | data formatting | bytes 14155776 | tf_op jit(solution)/shard_map/reshape | solution.py:103
  389.1 13.2 %reshape.430 = f32[16,96,1,1152]{3,0,2,1:T(8,128)} reshape(f32[16,96,6,2,96]{4,3,2,0,1:T(2,128)} %copy.149) | data formatting | bytes 14155776 | tf_op jit(solution)/shard_map/reshape | solution.py:103
  402.3 13.3 %all-to-all-done = f32[16,6,16,1152]{3,0,1,2:T(8,128)} async-done(((f32[16,6,16,1152]{3,0,1,2:T(8,128)}), f32[16,6,16,1152]{3,0,1,2:T(8,128)}, u32[]{:S(2)}, u32[]{:S(2)}) %all-to-all-start) | async-done | bytes 7077920 | tf_op jit(solution)/shard_map/all_to_all | solution.py:91
  415.6 7.3 all-to-all-start.3
  422.8 13.9 %reshape.389 = f32[16,96,6,2,96]{4,3,2,0,1:T(2,128)} reshape(f32[16,16,6,1,1152]{4,0,2,1,3:T(8,128)} %bitcast.22) | data formatting | bytes 14155776 | tf_op jit(solution)/shard_map/reshape | solution.py:98
  436.7 17.8 %fusion.14 = f32[96,2,16,6,96,1]{4,0,5,1,3,2:T(8,128)S(1)} fusion(f32[16,96,6,2,96,1]{4,3,2,0,1,5:T(2,128)} %bitcast.216, f32[96,1,96,2]{0,2,1,3:T(8,128)S(1)} %copy-done.4, f32[96,1,96,2]{0,2,1,3:T(8,128)S(1)} %copy-done.6), kind=kOutput, calls=%fused_computation.16 | convolution fusion | flops 4076900352 | bytes 14303232 | tf_op jit(solution)/shard_map/axyqk,xqus->auysk/dot_general | solution.py:61
  454.5 9.7 %fusion.28 = f32[16,96,6,2,96]{4,1,2,0,3:T(8,128)S(1)} fusion(f32[96,2,16,6,96,1]{4,0,5,1,3,2:T(8,128)S(1)} %fusion.14, f32[96,6,96]{2,0,1:T(8,128)S(1)} %fusion.52, f32[96,1,96,2]{0,2,3,1:T(8,128)S(1)} %copy-done.2, f32[96,1,96,2]{0,2,3,1:T(8,128)S(1)} %copy-done.1), kind=kOutput, calls=%fused_computation.32 | convolution fusion | flops 4078669824 | bytes 14524416 | tf_op jit(solution)/shard_map/axyqk,xqus->auysk/dot_general | solution.py:61
  464.2 11.8 %copy.137 = f32[16,96,6,2,96]{4,3,2,0,1:T(2,128)} copy(f32[16,96,6,2,96]{4,1,2,0,3:T(8,128)S(1)} %fusion.28) | data formatting | bytes 14155776 | tf_op jit(solution)/shard_map/reshape | solution.py:103
  476.0 13.0 %reshape.428 = f32[16,96,1,1152]{3,0,2,1:T(8,128)} reshape(f32[16,96,6,2,96]{4,3,2,0,1:T(2,128)} %copy.137) | data formatting | bytes 14155776 | tf_op jit(solution)/shard_map/reshape | solution.py:103
  489.0 14.0 %all-to-all-done.3 = f32[16,96,1,1152]{3,0,2,1:T(8,128)} async-done(((f32[16,96,1,1152]{3,0,2,1:T(8,128)}), f32[16,96,1,1152]{3,0,2,1:T(8,128)}, u32[]{:S(2)}, u32[]{:S(2)}) %all-to-all-start.3) | async-done | bytes 7077920 | tf_op jit(solution)/shard_map/all_to_all | solution.py:102
  503.0 7.3 all-to-all-start.1
  510.7 10.1 %copy.98 = f32[16,6,16,1,1152]{4,2,1,0,3:T(8,128)} copy(f32[16,6,16,1,1152]{4,0,1,2,3:T(8,128)} %bitcast.65) | data formatting | bytes 14155776 | tf_op jit(solution)/shard_map/all_to_all | solution.py:102
  520.8 14.3 %reshape.397 = f32[16,6,96,2,96]{4,3,2,1,0:T(2,128)} reshape(f32[16,6,16,1,1152]{4,2,1,0,3:T(8,128)} %copy.98) | data formatting | bytes 14155776 | tf_op jit(solution)/shard_map/reshape | solution.py:109
  535.1 12.6 %fusion.43 = f32[16,6,96,2,96]{4,2,3,1,0:T(8,128)S(1)} fusion(f32[16,6,96,2,96,1]{4,3,2,1,0,5:T(2,128)} %bitcast.219, f32[96,1,96,2]{0,2,3,1:T(8,128)S(1)} %copy-done.2, f32[96,1,96,2]{0,2,3,1:T(8,128)S(1)} %copy-done.1), kind=kOutput, calls=%fused_computation.37 | convolution fusion | flops 4076900352 | bytes 14303232 | tf_op jit(solution)/shard_map/axyqk,yqvs->axvsk/dot_general | solution.py:55
  547.7 9.5 %fusion.49 = f32[16,6,96,96]{3,2,0,1:T(8,128)} fusion(f32[16,6,96,2,96]{4,2,3,1,0:T(8,128)S(1)} %fusion.43, f32[1,96,96]{2,1,0:T(8,128)S(1)} %sine_negate_fusion, f32[1,96,96]{2,1,0:T(8,128)S(1)} %fusion.73), kind=kOutput, calls=%fused_computation.39 | convolution fusion | flops 2038450176 | bytes 10690560 | tf_op jit(solution)/shard_map/dot_general | solution.py:51
  557.3 4.8 reshape.400
  562.1 28.3 %all-to-all-done.1 = f32[16,96,1,1152]{3,0,2,1:T(8,128)} async-done(((f32[16,96,1,1152]{3,0,2,1:T(8,128)}), f32[16,96,1,1152]{3,0,2,1:T(8,128)}, u32[]{:S(2)}, u32[]{:S(2)}) %all-to-all-start.1) | async-done | bytes 7077920 | tf_op jit(solution)/shard_map/all_to_all | solution.py:102
  590.4 10.0 %copy.87 = f32[16,6,16,1,1152]{4,2,1,0,3:T(8,128)} copy(f32[16,6,16,1,1152]{4,0,1,2,3:T(8,128)} %bitcast.32) | data formatting | bytes 14155776 | tf_op jit(solution)/shard_map/all_to_all | solution.py:102
  600.4 13.9 %reshape.391 = f32[16,6,96,2,96]{4,3,2,1,0:T(2,128)} reshape(f32[16,6,16,1,1152]{4,2,1,0,3:T(8,128)} %copy.87) | data formatting | bytes 14155776 | tf_op jit(solution)/shard_map/reshape | solution.py:109
  614.3 12.6 %fusion.40 = f32[16,6,96,2,96]{4,2,3,1,0:T(8,128)S(1)} fusion(f32[16,6,96,2,96,1]{4,3,2,1,0,5:T(2,128)} %bitcast.217, f32[96,1,96,2]{0,2,3,1:T(8,128)} %get-tuple-element.15, f32[96,1,96,2]{0,2,3,1:T(8,128)} %get-tuple-element.12), kind=kOutput, calls=%fused_computation.36 | convolution fusion | flops 4076900352 | bytes 14303232 | tf_op jit(solution)/shard_map/axyqk,yqvs->axvsk/dot_general | solution.py:55
  626.9 9.8 %fusion.46 = f32[16,6,96,96]{3,2,0,1:T(8,128)} fusion(f32[16,6,96,2,96]{4,2,3,1,0:T(8,128)S(1)} %fusion.40, f32[1,96,96]{2,1,0:T(8,128)S(1)} %copy-done.10, f32[1,96,96]{2,1,0:T(8,128)S(1)} %copy-done.8), kind=kOutput, calls=%fused_computation.38 | convolution fusion | flops 2038450176 | bytes 10690560 | tf_op jit(solution)/shard_map/dot_general | solution.py:51
  636.7 6.2 reshape.399
  642.9 5.5 broadcast_multiply_fusion.1
  649.9 6.1 reshape.398
  656.0 6.4 reshape.392
  662.5 5.9 multiply_reduce_fusion
  669.3 136.6 %all-reduce.7.cloned.1.call-done = (f32[1,16,6,9216]{3,1,2,0:T(8,128)}, f32[1,16,6,9216]{3,1,2,0:T(8,128)}) async-done(((f32[1,16,6,9216]{3,1,2,0:T(8,128)}, f32[1,16,6,9216]{3,1,2,0:T(8,128)}), (f32[1,16,6,9216]{3,1,2,0:T(8,128)}, f32[1,16,6,9216]{3,1,2,0:T(8,128)})) %all-reduce.7.cloned.1.call-update) | async-done | bytes 7077904
  (51 shorter events, 11.5 us)
Async XLA Ops:
  7.2 8.3 %copy-start.11 = (f32[1,6,9216]{2,0,1:T(1,128)S(1)}, f32[1,6,9216]{2,0,1:T(1,128)}, u32[]{:S(2)}) copy-start(f32[1,6,9216]{2,0,1:T(1,128)} %param.3) | copy-start | bytes 663556
  7.2 168.1 %all-reduce.9.cloned.1.call-start = ((), (), s32[]{:S(2)}) async-start(), calls=%async_computation.5 | async-start | bytes 14155776 | tf_op jit(solution)/shard_map/psum | solution.py:21
  186.7 10.1 %copy-start.3 = (f32[96,1,96,2]{0,2,1,3:T(8,128)S(1)}, f32[96,1,96,2]{0,2,1,3:T(8,128)}, u32[]{:S(2)}) copy-start(f32[96,1,96,2]{0,2,1,3:T(8,128)} %get-tuple-element.13) | copy-start | bytes 221188
  186.7 10.1 %copy-start.5 = (f32[96,1,96,2]{0,2,1,3:T(8,128)S(1)}, f32[96,1,96,2]{0,2,1,3:T(8,128)}, u32[]{:S(2)}) copy-start(f32[96,1,96,2]{0,2,1,3:T(8,128)} %get-tuple-element.14) | copy-start | bytes 221188
  240.5 87.5 %all-to-all-start.2 = ((f32[16,6,16,1152]{3,0,1,2:T(8,128)}), f32[16,6,16,1152]{3,0,1,2:T(8,128)}, u32[]{:S(2)}, u32[]{:S(2)}) async-start(f32[16,6,16,1152]{3,0,1,2:T(8,128)} %copy.93), calls=%async_computation.2 | async-start | bytes 14155776 | tf_op jit(solution)/shard_map/all_to_all | solution.py:91
  251.6 9.8 %copy-start.4 = (f32[96,1,96,2]{0,2,1,3:T(8,128)S(1)}, f32[96,1,96,2]{0,2,1,3:T(8,128)}, u32[]{:S(2)}) copy-start(f32[96,1,96,2]{0,2,1,3:T(8,128)} %get-tuple-element.13) | copy-start | bytes 221188
  251.6 9.8 %copy-start.6 = (f32[96,1,96,2]{0,2,1,3:T(8,128)S(1)}, f32[96,1,96,2]{0,2,1,3:T(8,128)}, u32[]{:S(2)}) copy-start(f32[96,1,96,2]{0,2,1,3:T(8,128)} %get-tuple-element.14) | copy-start | bytes 221188
  328.0 87.5 %all-to-all-start = ((f32[16,6,16,1152]{3,0,1,2:T(8,128)}), f32[16,6,16,1152]{3,0,1,2:T(8,128)}, u32[]{:S(2)}, u32[]{:S(2)}) async-start(f32[16,6,16,1152]{3,0,1,2:T(8,128)} %copy.82), calls=%async_computation | async-start | bytes 14155776 | tf_op jit(solution)/shard_map/all_to_all | solution.py:91
  349.7 17.9 %copy-start.1 = (f32[96,1,96,2]{0,2,3,1:T(8,128)S(1)}, f32[96,1,96,2]{0,2,3,1:T(8,128)}, u32[]{:S(2)}) copy-start(f32[96,1,96,2]{0,2,3,1:T(8,128)} %get-tuple-element.12) | copy-start | bytes 221188
  349.7 17.9 %copy-start.2 = (f32[96,1,96,2]{0,2,3,1:T(8,128)S(1)}, f32[96,1,96,2]{0,2,3,1:T(8,128)}, u32[]{:S(2)}) copy-start(f32[96,1,96,2]{0,2,3,1:T(8,128)} %get-tuple-element.15) | copy-start | bytes 221188
  415.6 87.4 %all-to-all-start.3 = ((f32[16,96,1,1152]{3,0,2,1:T(8,128)}), f32[16,96,1,1152]{3,0,2,1:T(8,128)}, u32[]{:S(2)}, u32[]{:S(2)}) async-start(f32[16,96,1,1152]{3,0,2,1:T(8,128)} %reshape.430), calls=%async_computation.3 | async-start | bytes 14155776 | tf_op jit(solution)/shard_map/all_to_all | solution.py:102
  503.0 87.4 %all-to-all-start.1 = ((f32[16,96,1,1152]{3,0,2,1:T(8,128)}), f32[16,96,1,1152]{3,0,2,1:T(8,128)}, u32[]{:S(2)}, u32[]{:S(2)}) async-start(f32[16,96,1,1152]{3,0,2,1:T(8,128)} %reshape.428), calls=%async_computation.1 | async-start | bytes 14155776 | tf_op jit(solution)/shard_map/all_to_all | solution.py:102
  510.3 295.7 %all-reduce.7.cloned.1.call-start = ((), (), s32[]{:S(2)}) async-start(), calls=%async_computation.4 | async-start | bytes 14155776
  510.5 37.2 %copy-start.7 = (f32[1,96,96]{2,1,0:T(8,128)}, f32[1,96,96]{2,1,0:T(8,128)S(1)}, u32[]{:S(2)}) copy-start(f32[1,96,96]{2,1,0:T(8,128)S(1)} %fusion.73) | copy-start | bytes 110596
  510.7 37.0 %copy-start.9 = (f32[1,96,96]{2,1,0:T(8,128)}, f32[1,96,96]{2,1,0:T(8,128)S(1)}, u32[]{:S(2)}) copy-start(f32[1,96,96]{2,1,0:T(8,128)S(1)} %sine_negate_fusion) | copy-start | bytes 110596
  614.3 12.6 %copy-start.8 = (f32[1,96,96]{2,1,0:T(8,128)S(1)}, f32[1,96,96]{2,1,0:T(8,128)}, u32[]{:S(2)}) copy-start(f32[1,96,96]{2,1,0:T(8,128)} %copy-done.7) | copy-start | bytes 110596
  614.3 12.7 %copy-start.10 = (f32[1,96,96]{2,1,0:T(8,128)S(1)}, f32[1,96,96]{2,1,0:T(8,128)}, u32[]{:S(2)}) copy-start(f32[1,96,96]{2,1,0:T(8,128)} %copy-done.9) | copy-start | bytes 110596
  642.9 5.5 copy-start.12
  648.4 14.1 %copy-start = (f32[16,6,9216]{2,0,1:T(8,128)S(1)}, f32[16,6,9216]{2,0,1:T(8,128)}, u32[]{:S(2)}) copy-start(f32[16,6,9216]{2,0,1:T(8,128)} %get-tuple-element.4) | copy-start | bytes 10616836
Sparse Core Ops, SparseCore 0:
  15.6 159.6 all-reduce.8
  648.5 157.3 all-reduce.6
where the time goes:
time: 829 us; the launch traced here: 817 us
  waiting for transfers between devices  370 us (45%)
  local copies, waits for them, and re-layouts  231 us (28%)
  matrix products  139 us (17%)
  other arithmetic  30.5 us (4%)
  starting transfers between devices  29.6 us (4%)
  between operations  16.8 us (2%)
    psum x1, waiting for transfers between devices, from_root(): return lax.psum(kept, axis)  156 us
    unnamed x3, waiting for transfers between devices  137 us
    dot_general x4, matrix products, along_x(): jnp.einsum('axyqk,xqus->auysk', values, fourier_table(values.shape[1], si...  55.1 us
    reshape x4, local copies, waits for them, and re-layouts, potential_pencils(): spectrum.reshape(pieces, NX, 1, slab_y * 2 * NZ)  49.7 us
    reshape x4, local copies, waits for them, and re-layouts, potential_pencils(): spectrum.reshape(pieces, slab_x, groups, slab_y * 2 * NZ)  46.2 us
    dot_general x4, matrix products, along_y(): jnp.einsum('axyqk,yqvs->axvsk', values, fourier_table(values.shape[2], si...  44.4 us
    all_to_all x2, waiting for transfers between devices, potential_pencils(): lax.all_to_all(spectrum.reshape(pieces, NX, 1, slab_y * 2 * NZ), 'grid',...  42.3 us
    all_to_all x2, waiting for transfers between devices, potential_pencils(): lax.all_to_all(spectrum.reshape(pieces, slab_x, groups, slab_y * 2 * NZ),...  36 us
  transfers between devices with their start and end apart: 6, of which 6 were waited for; matrix products, arithmetic and copies ran while one was open for 33% of the time, Pallas kernels for 0%

commit v1 on v0

v1 whole, which is shorter than its diff:
```python
import math

import jax
import jax.numpy as jnp
import ml_dtypes
import numpy as np
from jax import lax
from jax.experimental import pallas as pl
from jax.experimental.pallas import tpu as pltpu
from jax.sharding import Mesh, PartitionSpec as P

N = 96
LANES = 128
FOLD = 4
ROWS = N // FOLD
WIDTH = FOLD * N
ROUNDS = 2
mixing = 0.25
cell_length = 41.04
SCALE = -mixing * 4.0 * math.pi / ((2.0 * math.pi / cell_length) ** 2 * N**3)
f32 = jnp.float32
bf16 = jnp.bfloat16


def trig(rows, columns):
    angle = 2.0 * np.pi * ((rows[:, None] * columns[None, :]) % N) / N
    return np.cos(angle), np.sin(angle)


def two_parts(table):
    high = table.astype(ml_dtypes.bfloat16)
    low = (table - high.astype(np.float64)).astype(ml_dtypes.bfloat16)
    return high, low


def right_table(sign):
    points = np.arange(N)
    cosine, sine = trig(points, points)
    table = np.zeros((2 * LANES, 2 * LANES))
    table[:N, :N] = cosine
    table[:N, LANES : LANES + N] = sign * sine
    table[LANES : LANES + N, :N] = -sign * sine
    table[LANES : LANES + N, LANES : LANES + N] = cosine
    return two_parts(table)


def left_table(sign, out_points, in_points):
    cosine, sine = trig(out_points, in_points)
    table = np.block([[cosine, -sign * sine], [sign * sine, cosine]])
    high, low = two_parts(table)
    return np.concatenate([high, low], axis=0), high


natural = np.arange(N)
folded = (np.arange(N) % ROWS) * FOLD + np.arange(N) // ROWS
Z_FWD = right_table(-1.0)
Z_INV = right_table(1.0)
Y_FWD = left_table(-1.0, natural, folded)
Y_INV = left_table(1.0, folded, natural)
SUB = 6
PLANES = 4 * SUB
X_FWD = left_table(-1.0, natural, natural)
X_INV = left_table(1.0, natural, natural)


def split(value):
    high = value.astype(bf16)
    return high, (value - high.astype(f32)).astype(bf16)


def dot(a, b):
    return jnp.dot(a, b, preferred_element_type=f32)


def times_right(value, high_ref, low_ref):
    high, low = split(value)
    return dot(high, high_ref[...]) + dot(low, high_ref[...]) + dot(high, low_ref[...])


def times_left(both_ref, high_ref, value):
    high, low = split(value)
    first = dot(both_ref[...], high)
    return first[: 2 * N] + first[2 * N :] + dot(high_ref[...], low)


def unfold(plane):
    lane = lax.broadcasted_iota(jnp.int32, (ROWS, LANES), 1)
    a, b, c = plane[:, :128], plane[:, 128:256], plane[:, 256:]
    return jnp.concatenate(
        [
            a,
            pltpu.roll(jnp.where(lane >= 96, a, b), 32, 1),
            pltpu.roll(jnp.where(lane >= 64, b, c), 64, 1),
            pltpu.roll(c, 96, 1),
        ],
        axis=0,
    )


def fold(field):
    lane = lax.broadcasted_iota(jnp.int32, (ROWS, LANES), 1)
    parts = [field[i * ROWS : (i + 1) * ROWS] for i in range(FOLD)]
    second = pltpu.roll(parts[1], 96, 1)
    third = pltpu.roll(parts[2], 64, 1)
    return jnp.concatenate(
        [
            jnp.where(lane < 96, parts[0], second),
            jnp.where(lane < 64, second, third),
            jnp.where(lane < 32, third, pltpu.roll(parts[3], 32, 1)),
        ],
        axis=1,
    )


def pick(core, own, other):
    first = jnp.where(core == 0, own, other)
    second = jnp.where(core == 0, other, own)
    return first, second


def forward_kernel(ids, phi_ref, own, other, zh, zl, yb, yh, re_ref, im_ref):
    core = ids[0]
    for half in range(2):
        for p in range(SUB):
            reals = pick(core, own[0, 0, half, p], other[0, 0, half, p])
            imags = pick(core, own[0, 1, half, p], other[0, 1, half, p])
            rows = []
            for c in range(2):
                phi = phi_ref[0, 2 * half + c, p]
                rows.append(
                    jnp.concatenate([unfold(phi * reals[c]), unfold(phi * imags[c])], axis=1)
                )
            lines = times_right(jnp.concatenate(rows, axis=0), zh, zl)
            first, second = lines[:N], lines[N:]
            field = jnp.concatenate(
                [
                    jnp.concatenate([first[:, :LANES], second[:, :LANES]], axis=1),
                    jnp.concatenate([first[:, LANES:], second[:, LANES:]], axis=1),
                ],
                axis=0,
            )
            spectrum = times_left(yb, yh, field)
            for c in range(2):
                at = pl.ds((half * 2 + c) * SUB + p, N, stride=PLANES)
                lanes = slice(c * LANES, (c + 1) * LANES)
                re_ref[at, :] = spectrum[:N, lanes]
                im_ref[at, :] = spectrum[N:, lanes]


def middle_kernel(re_in, im_in, fb, fh, ib, ih, re_out, im_out):
    step = pl.program_id(0)
    rows = re_in.shape[1]
    x = lax.broadcasted_iota(jnp.int32, (N, 2 * LANES), 0)
    lane = lax.broadcasted_iota(jnp.int32, (N, 2 * LANES), 1)
    z = lane % LANES

    def wave(i):
        return jnp.where(i < N // 2, i, i - N)

    plane = wave(x) ** 2 + wave(z) ** 2
    for pair in range(rows // 2):
        value = jnp.concatenate(
            [
                jnp.concatenate([part[k, 2 * pair], part[k, 2 * pair + 1]], axis=1)
                for part in (re_in, im_in)
                for k in range(4)
            ],
            axis=0,
        )
        y = step * rows + 2 * pair + lane // LANES
        square = plane + wave(y) ** 2
        weight = jnp.where(square > 0, SCALE / jnp.maximum(square, 1).astype(f32), 0.0)
        spectrum = times_left(fb, fh, value)
        spectrum = jnp.concatenate([spectrum[:N] * weight, spectrum[N:] * weight], axis=0)
        value = times_left(ib, ih, spectrum)
        for i, part in enumerate((re_out, im_out)):
            for k in range(4):
                at = (4 * i + k) * PLANES
                for j in range(2):
                    part[k, 2 * pair + j] = value[
                        at : at + PLANES, j * LANES : (j + 1) * LANES
                    ]


def inverse_kernel(
    ids, phi_ref, own, other, re_ref, im_ref, yb, yh, zh, zl, keep, send, local_ref
):
    core = ids[0]
    for half in range(2):
        for p in range(SUB):
            loaded = []
            for c in range(2):
                at = pl.ds((half * 2 + c) * SUB + p, N, stride=PLANES)
                loaded.append((re_ref[at, :], im_ref[at, :]))
            value = jnp.concatenate(
                [
                    jnp.concatenate([loaded[0][0], loaded[1][0]], axis=1),
                    jnp.concatenate([loaded[0][1], loaded[1][1]], axis=1),
                ],
                axis=0,
            )
            value = times_left(yb, yh, value)
            lines = jnp.concatenate(
                [
                    jnp.concatenate([value[:N, :LANES], value[N:, :LANES]], axis=1),
                    jnp.concatenate([value[:N, LANES:], value[N:, LANES:]], axis=1),
                ],
                axis=0,
            )
            lines = times_right(lines, zh, zl)
            reals = pick(core, own[0, 0, half, p], other[0, 0, half, p])
            imags = pick(core, own[0, 1, half, p], other[0, 1, half, p])
            terms = []
            for c in range(2):
                real = fold(lines[c * N : (c + 1) * N, :LANES])
                imag = fold(lines[c * N : (c + 1) * N, LANES:])
                at = 2 * half + c
                phi = phi_ref[0, at, p]
                local_ref[at, 0, p] = reals[c] * real + imags[c] * imag
                terms.append((phi * real, phi * imag))
            for r in range(2):
                keep[0, r, half, p] = jnp.where(core == 0, terms[0][r], terms[1][r])
                send[0, r, half, p] = jnp.where(core == 0, terms[1][r], terms[0][r])


def whole(table):
    return pl.BlockSpec(table.shape, lambda *_: (0,) * table.ndim)


PARAMS = pltpu.CompilerParams(vmem_limit_bytes=56 * 2**20)
FLOPS = 2 * 3 * N * N * 4 * N * N * 2


PIECE = (2, 2, SUB, ROWS, WIDTH)


def piece_spec():
    return pl.BlockSpec((1, *PIECE), lambda i, ids: (i, 0, 0, 0, 0, 0))


def phi_spec():
    return pl.BlockSpec((1, 4, SUB, ROWS, WIDTH), lambda i, ids: ((ids[1] + i) & 3, 0, 0, 0, 0))


def spectrum_spec():
    return pl.BlockSpec((N * PLANES, LANES), lambda i, ids: (i, 0))


def forward_planes(ids, phi, own, other):
    tables = [jnp.asarray(t) for t in (*Z_FWD, *Y_FWD)]
    return pl.pallas_call(
        forward_kernel,
        grid_spec=pltpu.PrefetchScalarGridSpec(
            num_scalar_prefetch=1,
            grid=(4,),
            in_specs=[phi_spec(), piece_spec(), piece_spec()] + [whole(t) for t in tables],
            out_specs=[spectrum_spec()] * 2,
        ),
        out_shape=[jax.ShapeDtypeStruct((4 * N * PLANES, LANES), f32)] * 2,
        compiler_params=PARAMS,
        cost_estimate=pl.CostEstimate(
            flops=2 * FLOPS, bytes_accessed=20_000_000, transcendentals=0
        ),
    )(ids, phi, own, other, *tables)


def middle_lines(real, imag):
    per = 8
    tables = [jnp.asarray(t) for t in (*X_FWD, *X_INV)]
    shape = (4, N, PLANES, LANES)
    spec = pl.BlockSpec((4, per, PLANES, LANES), lambda i: (0, i, 0, 0))
    out = pl.pallas_call(
        middle_kernel,
        grid=(N // per,),
        in_specs=[spec] * 2 + [whole(t) for t in tables],
        out_specs=[spec] * 2,
        out_shape=[jax.ShapeDtypeStruct(shape, f32)] * 2,
        compiler_params=PARAMS,
        cost_estimate=pl.CostEstimate(
            flops=2 * FLOPS, bytes_accessed=20_000_000, transcendentals=0
        ),
    )(real.reshape(shape), imag.reshape(shape), *tables)
    return [part.reshape(4 * N * PLANES, LANES) for part in out]


def inverse_planes(ids, phi, own, other, real, imag):
    tables = [jnp.asarray(t) for t in (*Y_INV, *Z_INV)]
    return pl.pallas_call(
        inverse_kernel,
        grid_spec=pltpu.PrefetchScalarGridSpec(
            num_scalar_prefetch=1,
            grid=(4,),
            in_specs=[phi_spec(), piece_spec(), piece_spec()]
            + [spectrum_spec()] * 2
            + [whole(t) for t in tables],
            out_specs=[
                piece_spec(),
                piece_spec(),
                pl.BlockSpec((4, 1, SUB, ROWS, WIDTH), lambda i, ids: (0, i, 0, 0, 0)),
            ],
        ),
        out_shape=[jax.ShapeDtypeStruct((4, *PIECE), f32)] * 2
        + [jax.ShapeDtypeStruct((4, 4, SUB, ROWS, WIDTH), f32)],
        compiler_params=PARAMS,
        cost_estimate=pl.CostEstimate(
            flops=2 * FLOPS, bytes_accessed=30_000_000, transcendentals=0
        ),
    )(ids, phi, own, other, real, imag, *tables)


TURN_AXES = ("x_lo", "y", "z", "core")


def turn(value):
    pairs = []
    for a in range(2):
        for y in range(4):
            for z in range(4):
                for c in range(2):
                    source = ((a * 4 + y) * 4 + z) * 2 + c
                    target = ((c * 4 + z) * 4 + y) * 2 + a
                    pairs.append((source, target))
    return lax.ppermute(value, TURN_AXES, pairs)


def other_core(value):
    return lax.ppermute(value, "core", [(0, 1), (1, 0)])


LINE_X = ("x_lo", "x_hi")
RING = {"y": (0, 1, 2, 3), "z": (0, 1, 2, 3), LINE_X: (0, 2, 1, 3)}


def shifted(value, axis, step):
    ring = RING[axis]
    return lax.ppermute(value, axis, [(ring[i], ring[(i + step) % 4]) for i in range(4)])


def ahead(value, axis):
    return shifted(value, axis, 1)


def behind(value, axis):
    return shifted(value, axis, 3)


def halves_of(value):
    size = value.shape[0] // 2
    return value[:size], value[size:]


def gather_ring(mine, axis):
    before = ahead(mine, axis)
    after = behind(mine, axis)
    far = ahead(halves_of(before)[0], axis), behind(halves_of(after)[1], axis)
    return jnp.stack([mine, after, jnp.concatenate(far, axis=0), before])


def scatter_ring(parts, axis):
    first, second = halves_of(parts[2])
    first, second = ahead(first, axis), behind(second, axis)
    after, before = halves_of(parts[1]), halves_of(parts[3])
    after = jnp.concatenate([after[0] + first, after[1]], axis=0)
    before = jnp.concatenate([before[0], before[1] + second], axis=0)
    return parts[0] + ahead(after, axis) + behind(before, axis)


def per_device(orbitals, blocks, owner):
    core = lax.axis_index("core")
    y, z = lax.axis_index("y"), lax.axis_index("z")
    place = 2 * lax.axis_index("x_hi") + lax.axis_index("x_lo")
    ids = jnp.stack([core, z]).astype(jnp.int32)
    planes = orbitals.shape[1]

    phi = turn(orbitals.reshape(planes, ROWS, WIDTH))
    blocks = blocks.reshape(16, planes, ROWS, WIDTH)
    phi, blocks = lax.optimization_barrier((phi, blocks))
    phi = lax.all_gather(phi, ("y", "x_hi", "x_lo")).reshape(4, 4, planes, ROWS, WIDTH)

    blocks = lax.all_to_all(blocks, ("x_lo", "y", "x_hi"), 0, 0, tiled=True)
    blocks = blocks.reshape(8, 2, planes, ROWS, WIDTH)
    mine = jnp.stack(
        [lax.dynamic_index_in_dim(blocks, owner[r], 0, False) for r in range(ROUNDS)]
    )
    own = gather_ring(mine, "z")
    other = other_core(own)

    spectrum = forward_planes(ids, phi, own, other)
    spectrum = middle_lines(*spectrum)
    keep, send, local = inverse_planes(ids, phi, own, other, *spectrum)

    total = keep + other_core(send)
    total = [lax.dynamic_index_in_dim(total, (k - z) & 3, 0, False) for k in range(4)]
    total = lax.psum_scatter(jnp.stack(total), "z", scatter_dimension=0)
    total = lax.all_to_all(total, "x_hi", 1, 1, tiled=True)

    local = [lax.dynamic_index_in_dim(local, (k + place) & 3, 0, False) for k in range(4)]
    local = scatter_ring(local, LINE_X)
    local = [lax.dynamic_index_in_dim(local, (k + y - z) & 3, 0, False) for k in range(4)]
    local = turn(scatter_ring(local, "y"))
    return (
        local.reshape(1, planes, N * N),
        total.reshape(ROUNDS, 2, planes, N * N),
    )


def solution(mesh):
    fine = Mesh(mesh.devices.reshape(2, 4, 4, 2, 2), ("x_lo", "y", "z", "x_hi", "core"))
    band = ("x_lo", "y")
    grid = ("z", "x_hi", "core")
    return jax.shard_map(
        per_device,
        mesh=fine,
        in_specs=(P(band, grid, None), P(band, grid, None), P()),
        out_specs=(P(band, grid, None), P(None, band, grid, None)),
        check_vma=False,
    )
```

time: 829 us -> 275 us (0.33); the launches traced: 817 us -> 273 us
  waiting for transfers between devices: 370 us -> 138 us
  local copies, waits for them, and re-layouts: 231 us -> 12.3 us
  matrix products: 139 us -> 0 us
  Pallas kernels: 0 us -> 48 us
  other arithmetic: 30.5 us -> 11.7 us
  starting transfers between devices: 29.6 us -> 44.7 us
    reshape x18 -> x2, local copies, waits for them, and re-layouts: 185 us -> 2.33 us  [the longest x1 1.42 us: per_device(): total.reshape(ROUNDS, 2, planes, N * N)]
    psum x1 -> x0, waiting for transfers between devices: 156 us -> none  [from_root(): return lax.psum(kept, axis)]
    dot_general x12 -> x0, matrix products: 139 us -> none  [the longest x4 55.1 us: along_x(): jnp.einsum('axyqk,xqus->auysk', values, fourier_table(values.shape[1], si...]
    unnamed x3 -> x2, waiting for transfers between devices: 137 us -> 0.7 us
    ppermute x0 -> x16, waiting for transfers between devices: none -> 95.3 us  [the longest x12 62 us: shifted(): lax.ppermute(value, axis, [(ring[i], ring[(i + step) % 4]) for i in range...]
    pallas_call x0 -> x3, Pallas kernels: none -> 48 us  [the longest x1 16.8 us: middle_lines(): pl.pallas_call(middle_kernel, grid=(N // per,), in_specs=[spec] * 2 + [wh...]
    all_to_all x4 -> x2, waiting for transfers between devices: 78.3 us -> 42.4 us  [the longest x1 42.4 us: per_device(): blocks = lax.all_to_all(blocks, ('x_lo', 'y', 'x_hi'), 0, 0, tiled=True)]
    ppermute x0 -> x16, starting transfers between devices: none -> 32.2 us  [the longest x12 20.7 us: shifted(): lax.ppermute(value, axis, [(ring[i], ring[(i + step) % 4]) for i in range...]
  transfers between devices with their start and end apart: 6 -> 20, of which waited for: 6 -> 13; matrix products, arithmetic and copies ran while one was open for 33% -> 5% of each run, Pallas kernels for 0% -> 0%
where the time goes in v1:
time: 275 us; the launch traced here: 273 us
  waiting for transfers between devices  138 us (50%)
  Pallas kernels  48 us (17%)
  starting transfers between devices  44.7 us (16%)
  between operations  18.1 us (7%)
  local copies, waits for them, and re-layouts  12.3 us (4%)
  other arithmetic  11.7 us (4%)
    ppermute x12, waiting for transfers between devices, shifted(): lax.ppermute(value, axis, [(ring[i], ring[(i + step) % 4]) for i in range...  62 us
    all_to_all x1, waiting for transfers between devices, per_device(): blocks = lax.all_to_all(blocks, ('x_lo', 'y', 'x_hi'), 0, 0, tiled=True)  42.4 us
    ppermute x2, waiting for transfers between devices, turn(): return lax.ppermute(value, TURN_AXES, pairs)  21.5 us
    ppermute x12, starting transfers between devices, shifted(): lax.ppermute(value, axis, [(ring[i], ring[(i + step) % 4]) for i in range...  20.7 us
    pallas_call x1, Pallas kernels, middle_lines(): pl.pallas_call(middle_kernel, grid=(N // per,), in_specs=[spec] * 2 + [wh...  16.8 us
    pallas_call x1, Pallas kernels, inverse_planes(): pl.pallas_call(inverse_kernel, grid_spec=pltpu.PrefetchScalarGridSpec(num...  16.5 us
    pallas_call x1, Pallas kernels, forward_planes(): pl.pallas_call(forward_kernel, grid_spec=pltpu.PrefetchScalarGridSpec(num...  14.7 us
    ppermute x2, waiting for transfers between devices, other_core(): return lax.ppermute(value, 'core', [(0, 1), (1, 0)])  11.9 us
  transfers between devices with their start and end apart: 20, of which 13 were waited for; matrix products, arithmetic and copies ran while one was open for 5% of the time, Pallas kernels for 0%

profile of v1, /device:TPU:28, one launch (start us, length us, event | category | flops | bytes accessed | tf_op | source)
XLA Modules:
  0.0 273.1 jit_solution(14811612185880227757)
XLA Ops:
  7.2 1.5 reduce
  8.7 5.6 %collective-permute-start = (f32[6,24,384]{2,1,0:T(8,128)S(1)}, f32[6,24,384]{2,1,0:T(8,128)}, u32[]{:S(2)}, u32[]{:S(2)}) collective-permute-start(f32[6,24,384]{2,1,0:T(8,128)S(1)} %bitcast.78), channel_id=1, source_target_pairs={{0,0},{1,64},{4,16},{5,80},{8,32},{9,96},{12,48},{13,112},{16,4},{... | collective-permute-start | bytes 663560 | tf_op jit(solution)/shard_map/ppermute | solution.py:323
  14.3 2.6 copy.28
  16.9 10.1 %collective-permute-done = f32[6,24,384]{2,1,0:T(8,128)} collective-permute-done((f32[6,24,384]{2,1,0:T(8,128)S(1)}, f32[6,24,384]{2,1,0:T(8,128)}, u32[]{:S(2)}, u32[]{:S(2)}) %collective-permute-start) | collective-permute-done | bytes 221216 | tf_op jit(solution)/shard_map/ppermute | solution.py:323
  27.0 2.0 copy.23
  29.1 7.6 %all-to-all-start = ((f32[16,6,24,384]{3,2,1,0:T(8,128)}), f32[16,6,24,384]{3,2,1,0:T(8,128)S(1)}, u32[]{:S(2)}, u32[]{:S(2)}) async-start(f32[16,6,24,384]{3,2,1,0:T(8,128)} %copy.23), calls=%async_computation | async-start | bytes 7077888 | tf_op jit(solution)/shard_map/all_to_all | solution.py:380
  36.7 0.7 all-gather.3.cloned.1.call-update
  37.5 0.6 fusion.7
  42.0 42.4 %all-to-all-done = f32[16,6,24,384]{3,2,1,0:T(8,128)S(1)} async-done(((f32[16,6,24,384]{3,2,1,0:T(8,128)}), f32[16,6,24,384]{3,2,1,0:T(8,128)S(1)}, u32[]{:S(2)}, u32[]{:S(2)}) %all-to-all-start) | async-done | bytes 3538976 | tf_op jit(solution)/shard_map/all_to_all | solution.py:380
  84.4 0.1 fusion.6
  84.5 0.5 collective-permute-start.2
  85.0 2.8 %collective-permute-start.1 = (f32[2,2,6,24,384]{4,3,2,1,0:T(8,128)S(1)}, f32[2,2,6,24,384]{4,3,2,1,0:T(8,128)S(1)}, u32[]{:S(2)}, u32[]{:S(2)}) collective-permute-start(f32[2,2,6,24,384]{4,3,2,1,0:T(8,128)S(1)} %get-tuple-element.45), channel_id=1, source_target_pairs={{0,12},{4,0},{8,4},{12,8},{1,13},{5,1},{9,5},{13,9},{2,14},{6,2},{... | collective-permute-start | bytes 2654216 | tf_op jit(solution)/shard_map/ppermute | solution.py:336
  87.8 17.0 %collective-permute-done.2 = f32[2,2,6,24,384]{4,3,2,1,0:T(8,128)S(1)} collective-permute-done((f32[2,2,6,24,384]{4,3,2,1,0:T(8,128)S(1)}, f32[2,2,6,24,384]{4,3,2,1,0:T(8,128)S(1)}, u32[]{:S(2)}, u32[]{:S(2)}) %collective-permute-start.2) | collective-permute-done | bytes 884768 | tf_op jit(solution)/shard_map/ppermute | solution.py:336
  104.9 3.3 %collective-permute-start.4 = (f32[1,2,6,24,384]{4,3,2,1,0:T(8,128)S(1)}, f32[1,2,6,24,384]{4,3,2,1,0:T(8,128)S(1)}, u32[]{:S(2)}, u32[]{:S(2)}) collective-permute-start(f32[1,2,6,24,384]{4,3,2,1,0:T(8,128)S(1)} %slice.113), channel_id=1, source_target_pairs={{0,12},{4,0},{8,4},{12,8},{1,13},{5,1},{9,5},{13,9},{2,14},{6,2},{... | collective-permute-start | bytes 1327112 | tf_op jit(solution)/shard_map/ppermute | solution.py:336
  108.2 6.5 %collective-permute-done.3 = f32[1,2,6,24,384]{4,3,2,1,0:T(8,128)S(1)} collective-permute-done((f32[1,2,6,24,384]{4,3,2,1,0:T(8,128)S(1)}, f32[1,2,6,24,384]{4,3,2,1,0:T(8,128)S(1)}, u32[]{:S(2)}, u32[]{:S(2)}) %collective-permute-start.3) | collective-permute-done | bytes 442400 | tf_op jit(solution)/shard_map/ppermute | solution.py:336
  114.8 0.2 pad_maximum_fusion.own
  115.1 0.8 pad_add_fusion.ids
  115.9 5.6 %collective-permute-done.5.other = f32[4,2,2,6,24,384]{5,4,3,2,1,0:T(8,128)} collective-permute-done((f32[4,2,2,6,24,384]{5,4,3,2,1,0:T(8,128)S(1)}, f32[4,2,2,6,24,384]{5,4,3,2,1,0:T(8,128)}, u32[]{:S(2)}, u32[]{:S(2)}) %collective-permute-start.5) | collective-permute-done | bytes 3538976 | tf_op jit(solution)/shard_map/ppermute | solution.py:327
  121.5 14.7 %shard_map.158 = (f32[9216,128]{1,0:T(8,128)}, f32[9216,128]{1,0:T(8,128)}) custom-call(s32[2]{0:T(128)} %pad_add_fusion.ids, f32[4,4,6,24,384]{4,3,2,1,0:T(8,128)} %bitcast.79, f32[4,2,2,6,24,384]{5,4,3,2,1,0:T(8,128)} %copy-done, f32[4,2,2,6,24,384]{5,4,3,2,1,0:T(8,128)} %collective-permute-done.5.other, bf16[256,256]{1,0:T(8,128)(2,1)} %constant.89.clone.zh, ...), custom_call_target="tpu_custom_call" | custom-call | flops 8153726976 | bytes 20000000 | tf_op jit(solution)/shard_map/pallas_call | solution.py:251
  136.1 16.8 %shard_map.159 = (f32[4,96,24,128]{3,2,1,0:T(8,128)}, f32[4,96,24,128]{3,2,1,0:T(8,128)}) custom-call(f32[4,96,24,128]{3,2,1,0:T(8,128)} %bitcast.83, f32[4,96,24,128]{3,2,1,0:T(8,128)} %bitcast.84, bf16[384,192]{1,0:T(8,128)(2,1)} %constant.93.clone.fb, bf16[192,192]{1,0:T(8,128)(2,1)} %constant.94.clone.fh, bf16[384,192]{1,0:T(8,128)(2,1)} %constant.95.clone.ib, ...), custom_call_target="tpu_custom_call" | custom-call | flops 8153726976 | bytes 20000000 | tf_op jit(solution)/shard_map/pallas_call | solution.py:272
  152.9 16.5 %shard_map.160 = (f32[4,2,2,6,24,384]{5,4,3,2,1,0:T(8,128)}, f32[4,2,2,6,24,384]{5,4,3,2,1,0:T(8,128)}, f32[4,4,6,24,384]{4,3,2,1,0:T(8,128)}) custom-call(s32[2]{0:T(128)} %pad_add_fusion.ids, f32[4,4,6,24,384]{4,3,2,1,0:T(8,128)} %bitcast.80, f32[4,2,2,6,24,384]{5,4,3,2,1,0:T(8,128)} %copy-done, f32[4,2,2,6,24,384]{5,4,3,2,1,0:T(8,128)} %collective-permute-done.5.other, ...), custom_call_target="tpu_custom_call" | custom-call | flops 8153726976 | bytes 30000000 | tf_op jit(solution)/shard_map/pallas_call | solution.py:288
  169.4 0.1 collective-permute-start.15
  169.6 6.3 %collective-permute-done.15 = f32[4,2,2,6,24,384]{5,4,3,2,1,0:T(8,128)S(1)} collective-permute-done((f32[4,2,2,6,24,384]{5,4,3,2,1,0:T(8,128)}, f32[4,2,2,6,24,384]{5,4,3,2,1,0:T(8,128)S(1)}, u32[]{:S(2)}, u32[]{:S(2)}) %collective-permute-start.15) | collective-permute-done | bytes 3538976 | tf_op jit(solution)/shard_map/ppermute | solution.py:327
  175.9 2.4 add.121
  178.2 0.2 constant_dynamic-slice_fusion.3
  178.5 2.0 pad_maximum_fusion.1
  180.5 2.0 copy-done.1
  182.6 3.6 %collective-permute-start.6 = (f32[2,6,24,384]{3,2,1,0:T(8,128)S(1)}, f32[2,6,24,384]{3,2,1,0:T(8,128)S(1)}, u32[]{:S(2)}, u32[]{:S(2)}) collective-permute-start(f32[2,6,24,384]{3,2,1,0:T(8,128)S(1)} %get-tuple-element.32), channel_id=1, source_target_pairs={{0,64},{64,2},{2,66},{66,0},{1,65},{65,3},{3,67},{67,1},{4,68},{68... | collective-permute-start | bytes 1327112 | tf_op jit(solution)/shard_map/ppermute | solution.py:336
  186.2 9.7 %collective-permute-done.6 = f32[2,6,24,384]{3,2,1,0:T(8,128)S(1)} collective-permute-done((f32[2,6,24,384]{3,2,1,0:T(8,128)S(1)}, f32[2,6,24,384]{3,2,1,0:T(8,128)S(1)}, u32[]{:S(2)}, u32[]{:S(2)}) %collective-permute-start.6) | collective-permute-done | bytes 442400 | tf_op jit(solution)/shard_map/ppermute | solution.py:336
  195.9 2.2 collective-permute-done.8
  198.2 1.0 pad_maximum_fusion.3
  199.3 1.8 collective-permute-start.7
  201.0 1.0 pad_maximum_fusion.4
  202.0 0.3 collective-permute-start.9
  202.3 17.9 %collective-permute-done.7 = f32[4,6,24,384]{3,2,1,0:T(8,128)} collective-permute-done((f32[4,6,24,384]{3,2,1,0:T(8,128)}, f32[4,6,24,384]{3,2,1,0:T(8,128)}, u32[]{:S(2)}, u32[]{:S(2)}) %collective-permute-start.7) | collective-permute-done | bytes 884768 | tf_op jit(solution)/shard_map/ppermute | solution.py:336
  220.1 2.8 %collective-permute-done.9 = f32[4,6,24,384]{3,2,1,0:T(8,128)} collective-permute-done((f32[4,6,24,384]{3,2,1,0:T(8,128)}, f32[4,6,24,384]{3,2,1,0:T(8,128)}, u32[]{:S(2)}, u32[]{:S(2)}) %collective-permute-start.9) | collective-permute-done | bytes 884768 | tf_op jit(solution)/shard_map/ppermute | solution.py:336
  222.9 1.6 fusion
  224.5 6.3 %collective-permute-start.10 = (f32[3,24,384]{2,1,0:T(8,128)S(1)}, f32[3,24,384]{2,1,0:T(8,128)S(1)}, u32[]{:S(2)}, u32[]{:S(2)}) collective-permute-start(f32[3,24,384]{2,1,0:T(8,128)S(1)} %get-tuple-element.40), channel_id=1, source_target_pairs={{0,16},{16,32},{32,48},{48,0},{1,17},{17,33},{33,49},{49,1},{2,18}... | collective-permute-start | bytes 331784 | tf_op jit(solution)/shard_map/ppermute | solution.py:336
  230.8 2.3 collective-permute-done.10
  233.2 3.6 %collective-permute-done.12 = f32[3,24,384]{2,1,0:T(8,128)S(1)} collective-permute-done((f32[3,24,384]{2,1,0:T(8,128)S(1)}, f32[3,24,384]{2,1,0:T(8,128)S(1)}, u32[]{:S(2)}, u32[]{:S(2)}) %collective-permute-start.12) | collective-permute-done | bytes 110624 | tf_op jit(solution)/shard_map/ppermute | solution.py:336
  236.9 2.1 collective-permute-start.13
  239.0 2.1 copy.24
  241.2 4.8 %all-to-all-start.1 = ((f32[2,2,6,24,384]{4,3,2,0,1:T(8,128)}), f32[2,2,6,24,384]{4,3,2,0,1:T(8,128)S(1)}, u32[]{:S(2)}, u32[]{:S(2)}) async-start(f32[2,2,6,24,384]{4,3,2,0,1:T(8,128)} %copy.24), calls=%async_computation.2 | async-start | bytes 1769472 | tf_op jit(solution)/shard_map/all_to_all | solution.py:395
  246.0 1.0 fusion.3
  246.9 5.6 %collective-permute-start.14 = (f32[6,24,384]{2,1,0:T(8,128)S(1)}, f32[6,24,384]{2,1,0:T(8,128)S(1)}, u32[]{:S(2)}, u32[]{:S(2)}) collective-permute-start(f32[6,24,384]{2,1,0:T(8,128)S(1)} %fusion.3), channel_id=1, source_target_pairs={{0,0},{1,64},{4,16},{5,80},{8,32},{9,96},{12,48},{13,112},{16,4},{... | collective-permute-start | bytes 663560 | tf_op jit(solution)/shard_map/ppermute | solution.py:323
  252.6 11.3 %collective-permute-done.14 = f32[6,24,384]{2,1,0:T(8,128)S(1)} collective-permute-done((f32[6,24,384]{2,1,0:T(8,128)S(1)}, f32[6,24,384]{2,1,0:T(8,128)S(1)}, u32[]{:S(2)}, u32[]{:S(2)}) %collective-permute-start.14) | collective-permute-done | bytes 221216 | tf_op jit(solution)/shard_map/ppermute | solution.py:323
  263.9 0.9 reshape.58
  264.9 1.4 reshape.55
  (34 shorter events, 1.0 us)
Async XLA Ops:
  8.7 18.4 %collective-permute-start = (f32[6,24,384]{2,1,0:T(8,128)S(1)}, f32[6,24,384]{2,1,0:T(8,128)}, u32[]{:S(2)}, u32[]{:S(2)}) collective-permute-start(f32[6,24,384]{2,1,0:T(8,128)S(1)} %bitcast.78), channel_id=1, source_target_pairs={{0,0},{1,64},{4,16},{5,80},{8,32},{9,96},{12,48},{13,112},{16,4},{... | collective-permute-start | bytes 663560 | tf_op jit(solution)/shard_map/ppermute | solution.py:323
  29.1 8.4 %copy-start.3 = (s32[2]{0:T(128)S(1)}, s32[2]{0:T(128)}, u32[]{:S(2)}) copy-start(s32[2]{0:T(128)} %param.17) | copy-start | bytes 28
  29.1 55.2 %all-to-all-start = ((f32[16,6,24,384]{3,2,1,0:T(8,128)}), f32[16,6,24,384]{3,2,1,0:T(8,128)S(1)}, u32[]{:S(2)}, u32[]{:S(2)}) async-start(f32[16,6,24,384]{3,2,1,0:T(8,128)} %copy.23), calls=%async_computation | async-start | bytes 7077888 | tf_op jit(solution)/shard_map/all_to_all | solution.py:380
  36.7 79.2 %all-gather.3.cloned.1.call-start = ((), (), s32[]{:S(2)}) async-start(), calls=%async_computation.4 | async-start | bytes 3760128 | tf_op jit(solution)/shard_map/all_gather | solution.py:378
  37.4 201.6 %reduce-scatter.2.cloned.1.call-start = ((), (), s32[]{:S(2)}) async-start(), calls=%async_computation.3 | async-start | bytes 4423680 | tf_op jit(solution)/shard_map/reduce_scatter | solution.py:394
  84.5 20.3 %collective-permute-start.2 = (f32[2,2,6,24,384]{4,3,2,1,0:T(8,128)S(1)}, f32[2,2,6,24,384]{4,3,2,1,0:T(8,128)S(1)}, u32[]{:S(2)}, u32[]{:S(2)}) collective-permute-start(f32[2,2,6,24,384]{4,3,2,1,0:T(8,128)S(1)} %get-tuple-element.45), channel_id=1, source_target_pairs={{0,4},{4,8},{8,12},{12,0},{1,5},{5,9},{9,13},{13,1},{2,6},{6,10},{... | collective-permute-start | bytes 2654216 | tf_op jit(solution)/shard_map/ppermute | solution.py:336
  85.0 19.9 %collective-permute-start.1 = (f32[2,2,6,24,384]{4,3,2,1,0:T(8,128)S(1)}, f32[2,2,6,24,384]{4,3,2,1,0:T(8,128)S(1)}, u32[]{:S(2)}, u32[]{:S(2)}) collective-permute-start(f32[2,2,6,24,384]{4,3,2,1,0:T(8,128)S(1)} %get-tuple-element.45), channel_id=1, source_target_pairs={{0,12},{4,0},{8,4},{12,8},{1,13},{5,1},{9,5},{13,9},{2,14},{6,2},{... | collective-permute-start | bytes 2654216 | tf_op jit(solution)/shard_map/ppermute | solution.py:336
  104.8 9.9 %collective-permute-start.3 = (f32[1,2,6,24,384]{4,3,2,1,0:T(8,128)S(1)}, f32[1,2,6,24,384]{4,3,2,1,0:T(8,128)S(1)}, u32[]{:S(2)}, u32[]{:S(2)}) collective-permute-start(f32[1,2,6,24,384]{4,3,2,1,0:T(8,128)S(1)} %slice.112), channel_id=1, source_target_pairs={{0,4},{4,8},{8,12},{12,0},{1,5},{5,9},{9,13},{13,1},{2,6},{6,10},{... | collective-permute-start | bytes 1327112 | tf_op jit(solution)/shard_map/ppermute | solution.py:336
  104.9 9.8 %collective-permute-start.4 = (f32[1,2,6,24,384]{4,3,2,1,0:T(8,128)S(1)}, f32[1,2,6,24,384]{4,3,2,1,0:T(8,128)S(1)}, u32[]{:S(2)}, u32[]{:S(2)}) collective-permute-start(f32[1,2,6,24,384]{4,3,2,1,0:T(8,128)S(1)} %slice.113), channel_id=1, source_target_pairs={{0,12},{4,0},{8,4},{12,8},{1,13},{5,1},{9,5},{13,9},{2,14},{6,2},{... | collective-permute-start | bytes 1327112 | tf_op jit(solution)/shard_map/ppermute | solution.py:336
  115.0 6.4 %copy-start = (f32[4,2,2,6,24,384]{5,4,3,2,1,0:T(8,128)}, f32[4,2,2,6,24,384]{5,4,3,2,1,0:T(8,128)S(1)}, u32[]{:S(2)}) copy-start(f32[4,2,2,6,24,384]{5,4,3,2,1,0:T(8,128)S(1)} %pad_maximum_fusion.own) | copy-start | bytes 10616836
  115.0 6.4 %collective-permute-start.5 = (f32[4,2,2,6,24,384]{5,4,3,2,1,0:T(8,128)S(1)}, f32[4,2,2,6,24,384]{5,4,3,2,1,0:T(8,128)}, u32[]{:S(2)}, u32[]{:S(2)}) collective-permute-start(f32[4,2,2,6,24,384]{5,4,3,2,1,0:T(8,128)S(1)} %pad_maximum_fusion.own), channel_id=1, source_target_pairs={{0,1},{1,0},{2,3},{3,2},{4,5},{5,4},{6,7},{7,6},{8,9},{9,8},{10,11... | collective-permute-start | bytes 10616840 | tf_op jit(solution)/shard_map/ppermute | solution.py:327
  169.4 6.4 %collective-permute-start.15 = (f32[4,2,2,6,24,384]{5,4,3,2,1,0:T(8,128)}, f32[4,2,2,6,24,384]{5,4,3,2,1,0:T(8,128)S(1)}, u32[]{:S(2)}, u32[]{:S(2)}) collective-permute-start(f32[4,2,2,6,24,384]{5,4,3,2,1,0:T(8,128)} %get-tuple-element.19), channel_id=1, source_target_pairs={{0,1},{1,0},{2,3},{3,2},{4,5},{5,4},{6,7},{7,6},{8,9},{9,8},{10,11... | collective-permute-start | bytes 10616840 | tf_op jit(solution)/shard_map/ppermute | solution.py:327
  180.5 2.0 copy-start.1
  182.6 13.3 %collective-permute-start.6 = (f32[2,6,24,384]{3,2,1,0:T(8,128)S(1)}, f32[2,6,24,384]{3,2,1,0:T(8,128)S(1)}, u32[]{:S(2)}, u32[]{:S(2)}) collective-permute-start(f32[2,6,24,384]{3,2,1,0:T(8,128)S(1)} %get-tuple-element.32), channel_id=1, source_target_pairs={{0,64},{64,2},{2,66},{66,0},{1,65},{65,3},{3,67},{67,1},{4,68},{68... | collective-permute-start | bytes 1327112 | tf_op jit(solution)/shard_map/ppermute | solution.py:336
  186.2 11.9 %collective-permute-start.8 = (f32[2,6,24,384]{3,2,1,0:T(8,128)S(1)}, f32[2,6,24,384]{3,2,1,0:T(8,128)S(1)}, u32[]{:S(2)}, u32[]{:S(2)}) collective-permute-start(f32[2,6,24,384]{3,2,1,0:T(8,128)S(1)} %get-tuple-element.34), channel_id=1, source_target_pairs={{0,66},{64,0},{2,64},{66,2},{1,67},{65,1},{3,65},{67,3},{4,70},{68... | collective-permute-start | bytes 1327112 | tf_op jit(solution)/shard_map/ppermute | solution.py:336
  199.3 20.9 %collective-permute-start.7 = (f32[4,6,24,384]{3,2,1,0:T(8,128)}, f32[4,6,24,384]{3,2,1,0:T(8,128)}, u32[]{:S(2)}, u32[]{:S(2)}) collective-permute-start(f32[4,6,24,384]{3,2,1,0:T(8,128)} %pad_maximum_fusion.3), channel_id=1, source_target_pairs={{0,64},{64,2},{2,66},{66,0},{1,65},{65,3},{3,67},{67,1},{4,68},{68... | collective-permute-start | bytes 2654216 | tf_op jit(solution)/shard_map/ppermute | solution.py:336
  202.0 20.9 %collective-permute-start.9 = (f32[4,6,24,384]{3,2,1,0:T(8,128)}, f32[4,6,24,384]{3,2,1,0:T(8,128)}, u32[]{:S(2)}, u32[]{:S(2)}) collective-permute-start(f32[4,6,24,384]{3,2,1,0:T(8,128)} %pad_maximum_fusion.4), channel_id=1, source_target_pairs={{0,66},{64,0},{2,64},{66,2},{1,67},{65,1},{3,65},{67,3},{4,70},{68... | collective-permute-start | bytes 2654216 | tf_op jit(solution)/shard_map/ppermute | solution.py:336
  224.4 12.3 %copy-start.2 = (f32[4,6,24,384]{3,2,1,0:T(8,128)}, f32[4,6,24,384]{3,2,1,0:T(8,128)S(1)}, u32[]{:S(2)}) copy-start(f32[4,6,24,384]{3,2,1,0:T(8,128)S(1)} %fusion) | copy-start | bytes 2654212
  224.5 8.6 %collective-permute-start.10 = (f32[3,24,384]{2,1,0:T(8,128)S(1)}, f32[3,24,384]{2,1,0:T(8,128)S(1)}, u32[]{:S(2)}, u32[]{:S(2)}) collective-permute-start(f32[3,24,384]{2,1,0:T(8,128)S(1)} %get-tuple-element.40), channel_id=1, source_target_pairs={{0,16},{16,32},{32,48},{48,0},{1,17},{17,33},{33,49},{49,1},{2,18}... | collective-permute-start | bytes 331784 | tf_op jit(solution)/shard_map/ppermute | solution.py:336
  230.8 6.0 %collective-permute-start.12 = (f32[3,24,384]{2,1,0:T(8,128)S(1)}, f32[3,24,384]{2,1,0:T(8,128)S(1)}, u32[]{:S(2)}, u32[]{:S(2)}) collective-permute-start(f32[3,24,384]{2,1,0:T(8,128)S(1)} %get-tuple-element.42), channel_id=1, source_target_pairs={{0,48},{16,0},{32,16},{48,32},{1,49},{17,1},{33,17},{49,33},{2,50}... | collective-permute-start | bytes 331784 | tf_op jit(solution)/shard_map/ppermute | solution.py:336
  236.8 9.1 %collective-permute-start.11 = (f32[6,24,384]{2,1,0:T(8,128)S(1)}, f32[6,24,384]{2,1,0:T(8,128)S(1)}, u32[]{:S(2)}, u32[]{:S(2)}) collective-permute-start(f32[6,24,384]{2,1,0:T(8,128)S(1)} %pad_maximum_fusion.5), channel_id=1, source_target_pairs={{0,16},{16,32},{32,48},{48,0},{1,17},{17,33},{33,49},{49,1},{2,18}... | collective-permute-start | bytes 663560 | tf_op jit(solution)/shard_map/ppermute | solution.py:336
  236.9 9.0 %collective-permute-start.13 = (f32[6,24,384]{2,1,0:T(8,128)S(1)}, f32[6,24,384]{2,1,0:T(8,128)S(1)}, u32[]{:S(2)}, u32[]{:S(2)}) collective-permute-start(f32[6,24,384]{2,1,0:T(8,128)S(1)} %pad_maximum_fusion.6), channel_id=1, source_target_pairs={{0,48},{16,0},{32,16},{48,32},{1,49},{17,1},{33,17},{49,33},{2,50}... | collective-permute-start | bytes 663560 | tf_op jit(solution)/shard_map/ppermute | solution.py:336
  241.2 23.7 %all-to-all-start.1 = ((f32[2,2,6,24,384]{4,3,2,0,1:T(8,128)}), f32[2,2,6,24,384]{4,3,2,0,1:T(8,128)S(1)}, u32[]{:S(2)}, u32[]{:S(2)}) async-start(f32[2,2,6,24,384]{4,3,2,0,1:T(8,128)} %copy.24), calls=%async_computation.2 | async-start | bytes 1769472 | tf_op jit(solution)/shard_map/all_to_all | solution.py:395
  246.9 17.0 %collective-permute-start.14 = (f32[6,24,384]{2,1,0:T(8,128)S(1)}, f32[6,24,384]{2,1,0:T(8,128)S(1)}, u32[]{:S(2)}, u32[]{:S(2)}) collective-permute-start(f32[6,24,384]{2,1,0:T(8,128)S(1)} %fusion.3), channel_id=1, source_target_pairs={{0,0},{1,64},{4,16},{5,80},{8,32},{9,96},{12,48},{13,112},{16,4},{... | collective-permute-start | bytes 663560 | tf_op jit(solution)/shard_map/ppermute | solution.py:323
Sparse Core Ops, SparseCore 0:
  39.7 71.9 all-gather.2
  180.6 48.0 reduce-scatter.1

commit v2 on v1

v2 whole, which is shorter than its diff:
```python
import math

import jax
import jax.numpy as jnp
import ml_dtypes
import numpy as np
from jax import lax
from jax.experimental import pallas as pl
from jax.experimental.pallas import tpu as pltpu
from jax.sharding import Mesh, PartitionSpec as P

N = 96
LANES = 128
FOLD = 4
ROWS = N // FOLD
WIDTH = FOLD * N
ROUNDS = 2
mixing = 0.25
cell_length = 41.04
SCALE = -mixing * 4.0 * math.pi / ((2.0 * math.pi / cell_length) ** 2 * N**3)
f32 = jnp.float32
bf16 = jnp.bfloat16


def trig(rows, columns):
    angle = 2.0 * np.pi * ((rows[:, None] * columns[None, :]) % N) / N
    return np.cos(angle), np.sin(angle)


def two_parts(table):
    high = table.astype(ml_dtypes.bfloat16)
    low = (table - high.astype(np.float64)).astype(ml_dtypes.bfloat16)
    return np.concatenate([high, low], axis=0)


def right_table(sign):
    points = np.arange(N)
    cosine, sine = trig(points, points)
    table = np.zeros((2 * LANES, 2 * LANES))
    table[:N, :N] = cosine
    table[:N, LANES : LANES + N] = sign * sine
    table[LANES : LANES + N, :N] = -sign * sine
    table[LANES : LANES + N, LANES : LANES + N] = cosine
    return two_parts(table)


def left_table(sign, out_points, in_points):
    cosine, sine = trig(out_points, in_points)
    return two_parts(np.block([[cosine, -sign * sine], [sign * sine, cosine]]))


natural = np.arange(N)
folded = (np.arange(N) % ROWS) * FOLD + np.arange(N) // ROWS
RIGHT = np.stack([right_table(-1.0), right_table(1.0)])
Z_FWD, Z_INV = 0, 1
LEFT = np.stack(
    [
        left_table(-1.0, natural, folded),
        left_table(1.0, folded, natural),
        left_table(-1.0, natural, natural),
        left_table(1.0, natural, natural),
    ]
)
Y_FWD, Y_INV, X_FWD, X_INV = 0, 1, 2, 3
SUB = 6
PLANES = 4 * SUB


def split(value):
    high = value.astype(bf16)
    return high, (value - high.astype(f32)).astype(bf16)


def dot(a, b):
    return jnp.dot(a, b, preferred_element_type=f32)


def times_right(value, table):
    high, low = split(value)
    above, below = table[: 2 * LANES, :], table[2 * LANES :, :]
    return dot(high, above) + dot(low, above) + dot(high, below)


def times_left(table, value):
    high, low = split(value)
    first = dot(table[...], high)
    return first[: 2 * N] + first[2 * N :] + dot(table[: 2 * N, :], low)


def unfold(plane):
    lane = lax.broadcasted_iota(jnp.int32, (ROWS, LANES), 1)
    a, b, c = plane[:, :128], plane[:, 128:256], plane[:, 256:]
    return jnp.concatenate(
        [
            a,
            pltpu.roll(jnp.where(lane >= 96, a, b), 32, 1),
            pltpu.roll(jnp.where(lane >= 64, b, c), 64, 1),
            pltpu.roll(c, 96, 1),
        ],
        axis=0,
    )


def fold(field):
    lane = lax.broadcasted_iota(jnp.int32, (ROWS, LANES), 1)
    parts = [field[i * ROWS : (i + 1) * ROWS] for i in range(FOLD)]
    second = pltpu.roll(parts[1], 96, 1)
    third = pltpu.roll(parts[2], 64, 1)
    return jnp.concatenate(
        [
            jnp.where(lane < 96, parts[0], second),
            jnp.where(lane < 64, second, third),
            jnp.where(lane < 32, third, pltpu.roll(parts[3], 32, 1)),
        ],
        axis=1,
    )


def pick(core, own, other):
    first = jnp.where(core == 0, own, other)
    second = jnp.where(core == 0, other, own)
    return first, second


FORWARD = 8
MIDDLE = 12
INVERSE = 8
LINES = N // MIDDLE
HELD = N * PLANES


def field_kernel(
    ids, phi_ref, own, other, right, left,
    keep, send, local_ref, re_ref, im_ref
):
    core = ids[0]
    step = pl.program_id(0)

    def forward(near, half):
        base = near * HELD + half * 2 * SUB
        for p in range(SUB):
            reals = pick(core, own[0, 0, 0, p], other[0, 0, 0, p])
            imags = pick(core, own[0, 1, 0, p], other[0, 1, 0, p])
            rows = []
            for c in range(2):
                phi = phi_ref[0, 2 * half + c, p]
                rows.append(
                    jnp.concatenate([unfold(phi * reals[c]), unfold(phi * imags[c])], axis=1)
                )
            lines = times_right(jnp.concatenate(rows, axis=0), right.at[Z_FWD])
            first, second = lines[:N], lines[N:]
            field = jnp.concatenate(
                [
                    jnp.concatenate([first[:, :LANES], second[:, :LANES]], axis=1),
                    jnp.concatenate([first[:, LANES:], second[:, LANES:]], axis=1),
                ],
                axis=0,
            )
            spectrum = times_left(left.at[Y_FWD], field)
            for c in range(2):
                at = pl.ds(base + c * SUB + p, N, stride=PLANES)
                lanes = slice(c * LANES, (c + 1) * LANES)
                re_ref[at, :] = spectrum[:N, lanes]
                im_ref[at, :] = spectrum[N:, lanes]

    def middle(block):
        x = lax.broadcasted_iota(jnp.int32, (N, 2 * LANES), 0)
        lane = lax.broadcasted_iota(jnp.int32, (N, 2 * LANES), 1)

        def wave(i):
            return jnp.where(i < N // 2, i, i - N)

        plane = wave(x) ** 2 + wave(lane % LANES) ** 2

        def at(k, ky):
            return pl.ds(pl.multiple_of(k * HELD + ky * PLANES, 8), PLANES)

        for pair in range(LINES // 2):
            ky = block * LINES + 2 * pair
            value = jnp.concatenate(
                [
                    jnp.concatenate([part[at(k, ky), :], part[at(k, ky + 1), :]], axis=1)
                    for part in (re_ref, im_ref)
                    for k in range(4)
                ],
                axis=0,
            )
            square = plane + wave(ky + lane // LANES) ** 2
            weight = jnp.where(square > 0, SCALE / jnp.maximum(square, 1).astype(f32), 0.0)
            spectrum = times_left(left.at[X_FWD], value)
            spectrum = jnp.concatenate([spectrum[:N] * weight, spectrum[N:] * weight], axis=0)
            value = times_left(left.at[X_INV], spectrum)
            for i, part in enumerate((re_ref, im_ref)):
                for k in range(4):
                    first = (4 * i + k) * PLANES
                    for j in range(2):
                        part[at(k, ky + j), :] = value[
                            first : first + PLANES, j * LANES : (j + 1) * LANES
                        ]

    def inverse(near, half):
        base = near * HELD + half * 2 * SUB
        for p in range(SUB):
            loaded = []
            for c in range(2):
                at = pl.ds(base + c * SUB + p, N, stride=PLANES)
                loaded.append((re_ref[at, :], im_ref[at, :]))
            value = jnp.concatenate(
                [
                    jnp.concatenate([loaded[0][0], loaded[1][0]], axis=1),
                    jnp.concatenate([loaded[0][1], loaded[1][1]], axis=1),
                ],
                axis=0,
            )
            value = times_left(left.at[Y_INV], value)
            lines = jnp.concatenate(
                [
                    jnp.concatenate([value[:N, :LANES], value[N:, :LANES]], axis=1),
                    jnp.concatenate([value[:N, LANES:], value[N:, LANES:]], axis=1),
                ],
                axis=0,
            )
            lines = times_right(lines, right.at[Z_INV])
            reals = pick(core, own[0, 0, 0, p], other[0, 0, 0, p])
            imags = pick(core, own[0, 1, 0, p], other[0, 1, 0, p])
            terms = []
            for c in range(2):
                real = fold(lines[c * N : (c + 1) * N, :LANES])
                imag = fold(lines[c * N : (c + 1) * N, LANES:])
                at = 2 * half + c
                phi = phi_ref[0, at, p]
                local_ref[at, 0, p] = reals[c] * real + imags[c] * imag
                terms.append((phi * real, phi * imag))
            for r in range(2):
                keep[0, r, 0, p] = jnp.where(core == 0, terms[0][r], terms[1][r])
                send[0, r, 0, p] = jnp.where(core == 0, terms[1][r], terms[0][r])

    @pl.when(step < FORWARD)
    def _():
        forward(step // 2, step % 2)

    @pl.when((step >= FORWARD) & (step < FORWARD + MIDDLE))
    def _():
        middle(step - FORWARD)

    @pl.when(step >= FORWARD + MIDDLE)
    def _():
        last = step - (FORWARD + MIDDLE)
        inverse(last // 2, last % 2)


def whole(table):
    return pl.BlockSpec(table.shape, lambda *_: (0,) * table.ndim)


def in_place(step):
    last = step - (FORWARD + MIDDLE)
    at = jnp.where(step < FORWARD, step, jnp.maximum(last, 0))
    return at // 2, at % 2


def out_place(step):
    at = jnp.maximum(step - (FORWARD + MIDDLE), 0)
    return at // 2, at % 2


PIECE = (2, 2, SUB, ROWS, WIDTH)


def solve(ids, phi, own, other):
    tables = [jnp.asarray(RIGHT), jnp.asarray(LEFT)]
    block = (1, 2, 1, SUB, ROWS, WIDTH)

    def phi_at(step, ids):
        return ((ids[1] + in_place(step)[0]) & 3, 0, 0, 0, 0)

    def block_at(step, ids):
        near, half = in_place(step)
        return (near, 0, half, 0, 0, 0)

    def term_at(step, ids):
        near, half = out_place(step)
        return (near, 0, half, 0, 0, 0)

    def local_at(step, ids):
        return (0, (ids[2] + out_place(step)[0]) & 3, 0, 0, 0)

    return pl.pallas_call(
        field_kernel,
        grid_spec=pltpu.PrefetchScalarGridSpec(
            num_scalar_prefetch=1,
            grid=(FORWARD + MIDDLE + INVERSE,),
            in_specs=[
                pl.BlockSpec((1, 4, SUB, ROWS, WIDTH), phi_at),
                pl.BlockSpec(block, block_at),
                pl.BlockSpec(block, block_at),
            ]
            + [whole(t) for t in tables],
            out_specs=[
                pl.BlockSpec(block, term_at),
                pl.BlockSpec(block, term_at),
                pl.BlockSpec((4, 1, SUB, ROWS, WIDTH), local_at),
            ],
            scratch_shapes=[pltpu.VMEM((4 * HELD, LANES), f32)] * 2,
        ),
        out_shape=[jax.ShapeDtypeStruct((4, *PIECE), f32)] * 2
        + [jax.ShapeDtypeStruct((4, 4, SUB, ROWS, WIDTH), f32)],
        compiler_params=pltpu.CompilerParams(vmem_limit_bytes=48 * 2**20),
        cost_estimate=pl.CostEstimate(
            flops=2 * 3 * 6 * (2 * N) ** 2 * N * N, bytes_accessed=35_000_000, transcendentals=0
        ),
    )(ids, phi, own, other, *tables)


TURN_AXES = ("x_lo", "y", "z", "core")


def turn(value):
    pairs = []
    for a in range(2):
        for y in range(4):
            for z in range(4):
                for c in range(2):
                    source = ((a * 4 + y) * 4 + z) * 2 + c
                    target = ((c * 4 + z) * 4 + y) * 2 + a
                    pairs.append((source, target))
    return lax.ppermute(value, TURN_AXES, pairs)


def other_core(value):
    return lax.ppermute(value, "core", [(0, 1), (1, 0)])


LINE_X = ("x_lo", "x_hi")
RING = {"y": (0, 1, 2, 3), "z": (0, 1, 2, 3), LINE_X: (0, 2, 1, 3)}


def shifted(value, axis, step):
    ring = RING[axis]
    return lax.ppermute(value, axis, [(ring[i], ring[(i + step) % 4]) for i in range(4)])


def ahead(value, axis):
    return shifted(value, axis, 1)


def behind(value, axis):
    return shifted(value, axis, 3)


def halves_of(value):
    size = (value.shape[0] + 1) // 2
    return value[:size], value[size:]


def gather_ring(mine, axis):
    before = ahead(mine, axis)
    after = behind(mine, axis)
    far = ahead(halves_of(before)[0], axis), behind(halves_of(after)[1], axis)
    return jnp.stack([mine, after, jnp.concatenate(far, axis=0), before])


def scatter_ring(parts, axis):
    first, second = halves_of(parts[2])
    first, second = ahead(first, axis), behind(second, axis)
    after, before = halves_of(parts[1]), halves_of(parts[3])
    after = jnp.concatenate([after[0] + first, after[1]], axis=0)
    before = jnp.concatenate([before[0], before[1] + second], axis=0)
    return parts[0] + ahead(after, axis) + behind(before, axis)


def per_device(orbitals, blocks, owner):
    core, y, z = (lax.axis_index(name) for name in ("core", "y", "z"))
    ids = jnp.stack([core, z, (z - y) & 3]).astype(jnp.int32)
    planes = orbitals.shape[1]

    phi = turn(orbitals.reshape(planes, ROWS, WIDTH))
    blocks = blocks.reshape(16, planes, ROWS, WIDTH)
    phi, blocks = lax.optimization_barrier((phi, blocks))
    phi = lax.all_gather(phi, ("y", "x_hi", "x_lo")).reshape(4, 4, planes, ROWS, WIDTH)

    blocks = lax.all_to_all(blocks, ("x_lo", "y", "x_hi"), 0, 0, tiled=True)
    blocks = blocks.reshape(8, 2, planes, ROWS, WIDTH)
    mine = jnp.stack(
        [lax.dynamic_index_in_dim(blocks, owner[r], 0, False) for r in range(ROUNDS)]
    )
    own = gather_ring(mine, "z")
    other = other_core(own)

    keep, send, local = solve(ids, phi, own, other)

    local = lax.psum_scatter(local, ("x_hi", "x_lo"), scatter_dimension=0)
    total = scatter_ring(keep + other_core(send), "z")
    total, local = lax.optimization_barrier((total, local))
    local = scatter_ring(local, "y")
    total = lax.all_to_all(total, "x_hi", 1, 1, tiled=True)
    local = turn(local)
    return (
        local.reshape(1, planes, N * N),
        total.reshape(ROUNDS, 2, planes, N * N),
    )


def solution(mesh):
    fine = Mesh(mesh.devices.reshape(2, 4, 4, 2, 2), ("x_lo", "y", "z", "x_hi", "core"))
    band = ("x_lo", "y")
    grid = ("z", "x_hi", "core")
    return jax.shard_map(
        per_device,
        mesh=fine,
        in_specs=(P(band, grid, None), P(band, grid, None), P()),
        out_specs=(P(band, grid, None), P(None, band, grid, None)),
        check_vma=False,
    )
```

time: 275 us -> 263 us (0.956)
  other arithmetic: 11.7 us -> 4.8 us
  Pallas kernels: 48 us -> 44 us
  waiting for transfers between devices: 138 us -> 142 us
  starting transfers between devices: 44.7 us -> 41 us
    pallas_call x3 -> x1, Pallas kernels: 48 us -> 44 us  [solve(): pl.pallas_call(field_kernel, grid_spec=pltpu.PrefetchScalarGridSpec(num_s...]
    all_to_all x1, waiting for transfers between devices: 0.01 us -> 3.47 us  [per_device(): total = lax.all_to_all(total, 'x_hi', 1, 1, tiled=True)]
    ppermute x2, starting transfers between devices: 11.2 us -> 8.46 us  [turn(): return lax.ppermute(value, TURN_AXES, pairs)]
  transfers between devices with their start and end apart: 20 -> 20, of which waited for: 13 -> 14; matrix products, arithmetic and copies ran while one was open for 5% -> 3% of each run, Pallas kernels for 0% -> 0%
where the time goes in v2:
time: 263 us; the launch traced here: 262 us
  waiting for transfers between devices  142 us (54%)
  Pallas kernels  44 us (17%)
  starting transfers between devices  41 us (16%)
  between operations  18.1 us (7%)
  local copies, waits for them, and re-layouts  12.1 us (5%)
  other arithmetic  4.8 us (2%)
    ppermute x12, waiting for transfers between devices, shifted(): lax.ppermute(value, axis, [(ring[i], ring[(i + step) % 4]) for i in range...  64 us
    pallas_call x1, Pallas kernels, solve(): pl.pallas_call(field_kernel, grid_spec=pltpu.PrefetchScalarGridSpec(num_s...  44 us
    all_to_all x1, waiting for transfers between devices, per_device(): blocks = lax.all_to_all(blocks, ('x_lo', 'y', 'x_hi'), 0, 0, tiled=True)  42.4 us
    ppermute x12, starting transfers between devices, shifted(): lax.ppermute(value, axis, [(ring[i], ring[(i + step) % 4]) for i in range...  19.8 us
    ppermute x2, waiting for transfers between devices, turn(): return lax.ppermute(value, TURN_AXES, pairs)  18.8 us
    ppermute x2, waiting for transfers between devices, other_core(): return lax.ppermute(value, 'core', [(0, 1), (1, 0)])  12.6 us
    ppermute x2, starting transfers between devices, turn(): return lax.ppermute(value, TURN_AXES, pairs)  8.46 us
    all_to_all x1, starting transfers between devices, per_device(): blocks = lax.all_to_all(blocks, ('x_lo', 'y', 'x_hi'), 0, 0, tiled=True)  7.61 us
  transfers between devices with their start and end apart: 20, of which 14 were waited for; matrix products, arithmetic and copies ran while one was open for 3% of the time, Pallas kernels for 0%

profile of v2, /device:TPU:28, one launch (start us, length us, event | category | flops | bytes accessed | tf_op | source)
XLA Modules:
  0.0 261.9 jit_solution(10263387977090132912)
XLA Ops:
  7.2 1.5 reduce
  8.7 5.6 %collective-permute-start = (f32[6,24,384]{2,1,0:T(8,128)S(1)}, f32[6,24,384]{2,1,0:T(8,128)}, u32[]{:S(2)}, u32[]{:S(2)}) collective-permute-start(f32[6,24,384]{2,1,0:T(8,128)S(1)} %bitcast.75), channel_id=1, source_target_pairs={{0,0},{1,64},{4,16},{5,80},{8,32},{9,96},{12,48},{13,112},{16,4},{... | collective-permute-start | bytes 663560 | tf_op jit(solution)/shard_map/ppermute | solution.py:327
  14.3 2.6 copy.18
  16.9 10.1 %collective-permute-done = f32[6,24,384]{2,1,0:T(8,128)} collective-permute-done((f32[6,24,384]{2,1,0:T(8,128)S(1)}, f32[6,24,384]{2,1,0:T(8,128)}, u32[]{:S(2)}, u32[]{:S(2)}) %collective-permute-start) | collective-permute-done | bytes 221216 | tf_op jit(solution)/shard_map/ppermute | solution.py:327
  27.0 2.0 copy.13
  29.1 7.6 %all-to-all-start = ((f32[16,6,24,384]{3,2,1,0:T(8,128)}), f32[16,6,24,384]{3,2,1,0:T(8,128)S(1)}, u32[]{:S(2)}, u32[]{:S(2)}) async-start(f32[16,6,24,384]{3,2,1,0:T(8,128)} %copy.13), calls=%async_computation | async-start | bytes 7077888 | tf_op jit(solution)/shard_map/all_to_all | solution.py:382
  36.7 0.7 all-gather.3.cloned.1.call-update
  37.5 0.6 fusion.6
  42.0 42.4 %all-to-all-done = f32[16,6,24,384]{3,2,1,0:T(8,128)S(1)} async-done(((f32[16,6,24,384]{3,2,1,0:T(8,128)}), f32[16,6,24,384]{3,2,1,0:T(8,128)S(1)}, u32[]{:S(2)}, u32[]{:S(2)}) %all-to-all-start) | async-done | bytes 3538976 | tf_op jit(solution)/shard_map/all_to_all | solution.py:382
  84.4 0.1 fusion.5
  84.5 1.4 collective-permute-start.1
  85.9 0.7 collective-permute-start.2
  86.6 17.6 %collective-permute-done.1 = f32[2,2,6,24,384]{4,3,2,1,0:T(8,128)S(1)} collective-permute-done((f32[2,2,6,24,384]{4,3,2,1,0:T(8,128)S(1)}, f32[2,2,6,24,384]{4,3,2,1,0:T(8,128)S(1)}, u32[]{:S(2)}, u32[]{:S(2)}) %collective-permute-start.1) | collective-permute-done | bytes 884768 | tf_op jit(solution)/shard_map/ppermute | solution.py:340
  104.2 1.4 collective-permute-start.4
  105.6 0.8 collective-permute-start.3
  106.4 6.6 %collective-permute-done.4 = f32[1,2,6,24,384]{4,3,2,1,0:T(8,128)S(1)} collective-permute-done((f32[1,2,6,24,384]{4,3,2,1,0:T(8,128)S(1)}, f32[1,2,6,24,384]{4,3,2,1,0:T(8,128)S(1)}, u32[]{:S(2)}, u32[]{:S(2)}) %collective-permute-start.4) | collective-permute-done | bytes 442400 | tf_op jit(solution)/shard_map/ppermute | solution.py:340
  113.0 2.2 collective-permute-done.3
  115.3 0.2 pad_maximum_fusion.own
  115.5 0.1 collective-permute-start.5
  115.7 6.3 %collective-permute-done.5.other = f32[4,2,2,6,24,384]{5,4,3,2,1,0:T(8,128)} collective-permute-done((f32[4,2,2,6,24,384]{5,4,3,2,1,0:T(8,128)S(1)}, f32[4,2,2,6,24,384]{5,4,3,2,1,0:T(8,128)}, u32[]{:S(2)}, u32[]{:S(2)}) %collective-permute-start.5) | collective-permute-done | bytes 3538976 | tf_op jit(solution)/shard_map/ppermute | solution.py:331
  122.0 1.1 copy-done
  123.1 1.0 copy-done.1
  124.1 44.0 %shard_map.68 = (f32[4,2,2,6,24,384]{5,4,3,2,1,0:T(8,128)S(1)}, f32[4,2,2,6,24,384]{5,4,3,2,1,0:T(8,128)}, f32[4,4,6,24,384]{4,3,2,1,0:T(8,128)}) custom-call(s32[3]{0:T(128)S(1)} %pad_add_fusion.ids, f32[4,4,6,24,384]{4,3,2,1,0:T(8,128)} %bitcast.76, f32[4,2,2,6,24,384]{5,4,3,2,1,0:T(8,128)} %copy-done.2, ...), custom_call_target="tpu_custom_call" | custom-call | flops 12230590464 | bytes 35000000 | tf_op jit(solution)/shard_map/pallas_call | solution.py:288
  168.1 0.2 collective-permute-start.6
  168.3 6.3 %collective-permute-done.6 = f32[4,2,2,6,24,384]{5,4,3,2,1,0:T(8,128)S(1)} collective-permute-done((f32[4,2,2,6,24,384]{5,4,3,2,1,0:T(8,128)}, f32[4,2,2,6,24,384]{5,4,3,2,1,0:T(8,128)S(1)}, u32[]{:S(2)}, u32[]{:S(2)}) %collective-permute-start.6) | collective-permute-done | bytes 3538976 | tf_op jit(solution)/shard_map/ppermute | solution.py:331
  174.6 0.5 add.38
  175.1 0.1 slice_bitcast_fusion.5
  175.3 3.2 %collective-permute-start.9 = (f32[1,2,6,24,384]{4,3,2,1,0:T(8,128)S(1)}, f32[1,2,6,24,384]{4,3,2,1,0:T(8,128)S(1)}, u32[]{:S(2)}, u32[]{:S(2)}) collective-permute-start(f32[1,2,6,24,384]{4,3,2,1,0:T(8,128)S(1)} %get-tuple-element.25), channel_id=1, source_target_pairs={{0,12},{4,0},{8,4},{12,8},{1,13},{5,1},{9,5},{13,9},{2,14},{6,2},{... | collective-permute-start | bytes 1327112 | tf_op jit(solution)/shard_map/ppermute | solution.py:340
  178.5 10.2 %collective-permute-done.7 = f32[1,2,6,24,384]{4,3,2,1,0:T(8,128)S(1)} collective-permute-done((f32[1,2,6,24,384]{4,3,2,1,0:T(8,128)S(1)}, f32[1,2,6,24,384]{4,3,2,1,0:T(8,128)S(1)}, u32[]{:S(2)}, u32[]{:S(2)}) %collective-permute-start.7) | collective-permute-done | bytes 442400 | tf_op jit(solution)/shard_map/ppermute | solution.py:340
  188.7 0.1 fusion.3
  188.9 3.0 %collective-permute-start.10 = (f32[2,2,6,24,384]{4,3,2,1,0:T(8,128)S(1)}, f32[2,2,6,24,384]{4,3,2,1,0:T(8,128)S(1)}, u32[]{:S(2)}, u32[]{:S(2)}) collective-permute-start(f32[2,2,6,24,384]{4,3,2,1,0:T(8,128)S(1)} %pad_maximum_fusion.3), channel_id=1, source_target_pairs={{0,12},{4,0},{8,4},{12,8},{1,13},{5,1},{9,5},{13,9},{2,14},{6,2},{... | collective-permute-start | bytes 2654216 | tf_op jit(solution)/shard_map/ppermute | solution.py:340
  192.1 17.9 %collective-permute-done.10 = f32[2,2,6,24,384]{4,3,2,1,0:T(8,128)S(1)} collective-permute-done((f32[2,2,6,24,384]{4,3,2,1,0:T(8,128)S(1)}, f32[2,2,6,24,384]{4,3,2,1,0:T(8,128)S(1)}, u32[]{:S(2)}, u32[]{:S(2)}) %collective-permute-start.10) | collective-permute-done | bytes 884768 | tf_op jit(solution)/shard_map/ppermute | solution.py:340
  210.0 3.6 %collective-permute-done.8 = f32[2,2,6,24,384]{4,3,2,1,0:T(8,128)S(1)} collective-permute-done((f32[2,2,6,24,384]{4,3,2,1,0:T(8,128)S(1)}, f32[2,2,6,24,384]{4,3,2,1,0:T(8,128)S(1)}, u32[]{:S(2)}, u32[]{:S(2)}) %collective-permute-start.8) | collective-permute-done | bytes 884768 | tf_op jit(solution)/shard_map/ppermute | solution.py:340
  213.6 0.1 fusion.1
  213.7 1.1 slice_bitcast_fusion.10
  214.8 5.7 %collective-permute-start.11 = (f32[3,24,384]{2,1,0:T(8,128)S(1)}, f32[3,24,384]{2,1,0:T(8,128)S(1)}, u32[]{:S(2)}, u32[]{:S(2)}) collective-permute-start(f32[3,24,384]{2,1,0:T(8,128)S(1)} %get-tuple-element.32), channel_id=1, source_target_pairs={{0,16},{16,32},{32,48},{48,0},{1,17},{17,33},{33,49},{49,1},{2,18}... | collective-permute-start | bytes 331784 | tf_op jit(solution)/shard_map/ppermute | solution.py:340
  220.6 2.6 %collective-permute-done.11 = f32[3,24,384]{2,1,0:T(8,128)S(1)} collective-permute-done((f32[3,24,384]{2,1,0:T(8,128)S(1)}, f32[3,24,384]{2,1,0:T(8,128)S(1)}, u32[]{:S(2)}, u32[]{:S(2)}) %collective-permute-start.11) | collective-permute-done | bytes 110624 | tf_op jit(solution)/shard_map/ppermute | solution.py:340
  223.2 3.3 %collective-permute-done.13 = f32[3,24,384]{2,1,0:T(8,128)S(1)} collective-permute-done((f32[3,24,384]{2,1,0:T(8,128)S(1)}, f32[3,24,384]{2,1,0:T(8,128)S(1)}, u32[]{:S(2)}, u32[]{:S(2)}) %collective-permute-start.13) | collective-permute-done | bytes 110624 | tf_op jit(solution)/shard_map/ppermute | solution.py:340
  226.5 1.0 bitcast_add_fusion.2
  227.6 3.3 %collective-permute-start.12 = (f32[6,24,384]{2,1,0:T(8,128)S(1)}, f32[6,24,384]{2,1,0:T(8,128)S(1)}, u32[]{:S(2)}, u32[]{:S(2)}) collective-permute-start(f32[6,24,384]{2,1,0:T(8,128)S(1)} %pad_maximum_fusion.4), channel_id=1, source_target_pairs={{0,16},{16,32},{32,48},{48,0},{1,17},{17,33},{33,49},{49,1},{2,18}... | collective-permute-start | bytes 663560 | tf_op jit(solution)/shard_map/ppermute | solution.py:340
  230.9 1.0 copy.14
  231.9 4.8 %all-to-all-start.1 = ((f32[2,2,6,24,384]{4,3,2,0,1:T(8,128)}), f32[2,2,6,24,384]{4,3,2,0,1:T(8,128)S(1)}, u32[]{:S(2)}, u32[]{:S(2)}) async-start(f32[2,2,6,24,384]{4,3,2,0,1:T(8,128)} %copy.14), calls=%async_computation.2 | async-start | bytes 1769472 | tf_op jit(solution)/shard_map/all_to_all | solution.py:396
  236.7 1.0 fusion.4
  237.6 2.9 %collective-permute-start.15 = (f32[6,24,384]{2,1,0:T(8,128)S(1)}, f32[6,24,384]{2,1,0:T(8,128)S(1)}, u32[]{:S(2)}, u32[]{:S(2)}) collective-permute-start(f32[6,24,384]{2,1,0:T(8,128)S(1)} %fusion.4), channel_id=1, source_target_pairs={{0,0},{1,64},{4,16},{5,80},{8,32},{9,96},{12,48},{13,112},{16,4},{... | collective-permute-start | bytes 663560 | tf_op jit(solution)/shard_map/ppermute | solution.py:327
  240.5 3.5 %all-to-all-done.1 = f32[2,2,6,24,384]{4,3,2,0,1:T(8,128)S(1)} async-done(((f32[2,2,6,24,384]{4,3,2,0,1:T(8,128)}), f32[2,2,6,24,384]{4,3,2,0,1:T(8,128)S(1)}, u32[]{:S(2)}, u32[]{:S(2)}) %all-to-all-start.1) | async-done | bytes 884768 | tf_op jit(solution)/shard_map/all_to_all | solution.py:396
  244.0 1.4 reshape.39
  245.5 8.7 %collective-permute-done.15 = f32[6,24,384]{2,1,0:T(8,128)S(1)} collective-permute-done((f32[6,24,384]{2,1,0:T(8,128)S(1)}, f32[6,24,384]{2,1,0:T(8,128)S(1)}, u32[]{:S(2)}, u32[]{:S(2)}) %collective-permute-start.15) | collective-permute-done | bytes 221216 | tf_op jit(solution)/shard_map/ppermute | solution.py:327
  254.2 0.9 reshape.42
  (30 shorter events, 0.9 us)
Async XLA Ops:
  8.7 18.4 %collective-permute-start = (f32[6,24,384]{2,1,0:T(8,128)S(1)}, f32[6,24,384]{2,1,0:T(8,128)}, u32[]{:S(2)}, u32[]{:S(2)}) collective-permute-start(f32[6,24,384]{2,1,0:T(8,128)S(1)} %bitcast.75), channel_id=1, source_target_pairs={{0,0},{1,64},{4,16},{5,80},{8,32},{9,96},{12,48},{13,112},{16,4},{... | collective-permute-start | bytes 663560 | tf_op jit(solution)/shard_map/ppermute | solution.py:327
  29.1 8.4 %copy-start.3 = (s32[2]{0:T(128)S(1)}, s32[2]{0:T(128)}, u32[]{:S(2)}) copy-start(s32[2]{0:T(128)} %param.7) | copy-start | bytes 28
  29.1 55.2 %all-to-all-start = ((f32[16,6,24,384]{3,2,1,0:T(8,128)}), f32[16,6,24,384]{3,2,1,0:T(8,128)S(1)}, u32[]{:S(2)}, u32[]{:S(2)}) async-start(f32[16,6,24,384]{3,2,1,0:T(8,128)} %copy.13), calls=%async_computation | async-start | bytes 7077888 | tf_op jit(solution)/shard_map/all_to_all | solution.py:382
  36.7 79.0 %all-gather.3.cloned.1.call-start = ((), (), s32[]{:S(2)}) async-start(), calls=%async_computation.4 | async-start | bytes 3760128 | tf_op jit(solution)/shard_map/all_gather | solution.py:380
  37.4 176.3 %reduce-scatter.2.cloned.1.call-start = ((), (), s32[]{:S(2)}) async-start(), calls=%async_computation.3 | async-start | bytes 4423680 | tf_op jit(solution)/shard_map/reduce_scatter | solution.py:392
  84.5 19.7 %collective-permute-start.1 = (f32[2,2,6,24,384]{4,3,2,1,0:T(8,128)S(1)}, f32[2,2,6,24,384]{4,3,2,1,0:T(8,128)S(1)}, u32[]{:S(2)}, u32[]{:S(2)}) collective-permute-start(f32[2,2,6,24,384]{4,3,2,1,0:T(8,128)S(1)} %get-tuple-element.37), channel_id=1, source_target_pairs={{0,12},{4,0},{8,4},{12,8},{1,13},{5,1},{9,5},{13,9},{2,14},{6,2},{... | collective-permute-start | bytes 2654216 | tf_op jit(solution)/shard_map/ppermute | solution.py:340
  85.9 19.7 %collective-permute-start.2 = (f32[2,2,6,24,384]{4,3,2,1,0:T(8,128)S(1)}, f32[2,2,6,24,384]{4,3,2,1,0:T(8,128)S(1)}, u32[]{:S(2)}, u32[]{:S(2)}) collective-permute-start(f32[2,2,6,24,384]{4,3,2,1,0:T(8,128)S(1)} %get-tuple-element.37), channel_id=1, source_target_pairs={{0,4},{4,8},{8,12},{12,0},{1,5},{5,9},{9,13},{13,1},{2,6},{6,10},{... | collective-permute-start | bytes 2654216 | tf_op jit(solution)/shard_map/ppermute | solution.py:340
  104.2 8.8 %collective-permute-start.4 = (f32[1,2,6,24,384]{4,3,2,1,0:T(8,128)S(1)}, f32[1,2,6,24,384]{4,3,2,1,0:T(8,128)S(1)}, u32[]{:S(2)}, u32[]{:S(2)}) collective-permute-start(f32[1,2,6,24,384]{4,3,2,1,0:T(8,128)S(1)} %slice.139), channel_id=1, source_target_pairs={{0,12},{4,0},{8,4},{12,8},{1,13},{5,1},{9,5},{13,9},{2,14},{6,2},{... | collective-permute-start | bytes 1327112 | tf_op jit(solution)/shard_map/ppermute | solution.py:340
  105.6 9.6 %collective-permute-start.3 = (f32[1,2,6,24,384]{4,3,2,1,0:T(8,128)S(1)}, f32[1,2,6,24,384]{4,3,2,1,0:T(8,128)S(1)}, u32[]{:S(2)}, u32[]{:S(2)}) collective-permute-start(f32[1,2,6,24,384]{4,3,2,1,0:T(8,128)S(1)} %slice.138), channel_id=1, source_target_pairs={{0,4},{4,8},{8,12},{12,0},{1,5},{5,9},{9,13},{13,1},{2,6},{6,10},{... | collective-permute-start | bytes 1327112 | tf_op jit(solution)/shard_map/ppermute | solution.py:340
  115.5 6.4 %copy-start.2 = (f32[4,2,2,6,24,384]{5,4,3,2,1,0:T(8,128)}, f32[4,2,2,6,24,384]{5,4,3,2,1,0:T(8,128)S(1)}, u32[]{:S(2)}) copy-start(f32[4,2,2,6,24,384]{5,4,3,2,1,0:T(8,128)S(1)} %pad_maximum_fusion.own) | copy-start | bytes 10616836
  115.5 6.4 %collective-permute-start.5 = (f32[4,2,2,6,24,384]{5,4,3,2,1,0:T(8,128)S(1)}, f32[4,2,2,6,24,384]{5,4,3,2,1,0:T(8,128)}, u32[]{:S(2)}, u32[]{:S(2)}) collective-permute-start(f32[4,2,2,6,24,384]{5,4,3,2,1,0:T(8,128)S(1)} %pad_maximum_fusion.own), channel_id=1, source_target_pairs={{0,1},{1,0},{2,3},{3,2},{4,5},{5,4},{6,7},{7,6},{8,9},{9,8},{10,11... | collective-permute-start | bytes 10616840 | tf_op jit(solution)/shard_map/ppermute | solution.py:331
  122.0 1.1 copy-start
  123.1 1.0 copy-start.1
  168.1 6.5 %collective-permute-start.6 = (f32[4,2,2,6,24,384]{5,4,3,2,1,0:T(8,128)}, f32[4,2,2,6,24,384]{5,4,3,2,1,0:T(8,128)S(1)}, u32[]{:S(2)}, u32[]{:S(2)}) collective-permute-start(f32[4,2,2,6,24,384]{5,4,3,2,1,0:T(8,128)} %get-tuple-element.12), channel_id=1, source_target_pairs={{0,1},{1,0},{2,3},{3,2},{4,5},{5,4},{6,7},{7,6},{8,9},{9,8},{10,11... | collective-permute-start | bytes 10616840 | tf_op jit(solution)/shard_map/ppermute | solution.py:331
  175.2 13.5 %collective-permute-start.7 = (f32[1,2,6,24,384]{4,3,2,1,0:T(8,128)S(1)}, f32[1,2,6,24,384]{4,3,2,1,0:T(8,128)S(1)}, u32[]{:S(2)}, u32[]{:S(2)}) collective-permute-start(f32[1,2,6,24,384]{4,3,2,1,0:T(8,128)S(1)} %get-tuple-element.24), channel_id=1, source_target_pairs={{0,4},{4,8},{8,12},{12,0},{1,5},{5,9},{9,13},{13,1},{2,6},{6,10},{... | collective-permute-start | bytes 1327112 | tf_op jit(solution)/shard_map/ppermute | solution.py:340
  175.3 13.4 %collective-permute-start.9 = (f32[1,2,6,24,384]{4,3,2,1,0:T(8,128)S(1)}, f32[1,2,6,24,384]{4,3,2,1,0:T(8,128)S(1)}, u32[]{:S(2)}, u32[]{:S(2)}) collective-permute-start(f32[1,2,6,24,384]{4,3,2,1,0:T(8,128)S(1)} %get-tuple-element.25), channel_id=1, source_target_pairs={{0,12},{4,0},{8,4},{12,8},{1,13},{5,1},{9,5},{13,9},{2,14},{6,2},{... | collective-permute-start | bytes 1327112 | tf_op jit(solution)/shard_map/ppermute | solution.py:340
  188.9 21.1 %collective-permute-start.10 = (f32[2,2,6,24,384]{4,3,2,1,0:T(8,128)S(1)}, f32[2,2,6,24,384]{4,3,2,1,0:T(8,128)S(1)}, u32[]{:S(2)}, u32[]{:S(2)}) collective-permute-start(f32[2,2,6,24,384]{4,3,2,1,0:T(8,128)S(1)} %pad_maximum_fusion.3), channel_id=1, source_target_pairs={{0,12},{4,0},{8,4},{12,8},{1,13},{5,1},{9,5},{13,9},{2,14},{6,2},{... | collective-permute-start | bytes 2654216 | tf_op jit(solution)/shard_map/ppermute | solution.py:340
  192.0 21.5 %collective-permute-start.8 = (f32[2,2,6,24,384]{4,3,2,1,0:T(8,128)S(1)}, f32[2,2,6,24,384]{4,3,2,1,0:T(8,128)S(1)}, u32[]{:S(2)}, u32[]{:S(2)}) collective-permute-start(f32[2,2,6,24,384]{4,3,2,1,0:T(8,128)S(1)} %pad_maximum_fusion.2), channel_id=1, source_target_pairs={{0,4},{4,8},{8,12},{12,0},{1,5},{5,9},{9,13},{13,1},{2,6},{6,10},{... | collective-permute-start | bytes 2654216 | tf_op jit(solution)/shard_map/ppermute | solution.py:340
  214.8 8.4 %collective-permute-start.11 = (f32[3,24,384]{2,1,0:T(8,128)S(1)}, f32[3,24,384]{2,1,0:T(8,128)S(1)}, u32[]{:S(2)}, u32[]{:S(2)}) collective-permute-start(f32[3,24,384]{2,1,0:T(8,128)S(1)} %get-tuple-element.32), channel_id=1, source_target_pairs={{0,16},{16,32},{32,48},{48,0},{1,17},{17,33},{33,49},{49,1},{2,18}... | collective-permute-start | bytes 331784 | tf_op jit(solution)/shard_map/ppermute | solution.py:340
  220.5 6.0 %collective-permute-start.13 = (f32[3,24,384]{2,1,0:T(8,128)S(1)}, f32[3,24,384]{2,1,0:T(8,128)S(1)}, u32[]{:S(2)}, u32[]{:S(2)}) collective-permute-start(f32[3,24,384]{2,1,0:T(8,128)S(1)} %get-tuple-element.33), channel_id=1, source_target_pairs={{0,48},{16,0},{32,16},{48,32},{1,49},{17,1},{33,17},{49,33},{2,50}... | collective-permute-start | bytes 331784 | tf_op jit(solution)/shard_map/ppermute | solution.py:340
  227.5 9.2 %collective-permute-start.14 = (f32[6,24,384]{2,1,0:T(8,128)S(1)}, f32[6,24,384]{2,1,0:T(8,128)S(1)}, u32[]{:S(2)}, u32[]{:S(2)}) collective-permute-start(f32[6,24,384]{2,1,0:T(8,128)S(1)} %pad_maximum_fusion.5), channel_id=1, source_target_pairs={{0,48},{16,0},{32,16},{48,32},{1,49},{17,1},{33,17},{49,33},{2,50}... | collective-permute-start | bytes 663560 | tf_op jit(solution)/shard_map/ppermute | solution.py:340
  227.6 9.1 %collective-permute-start.12 = (f32[6,24,384]{2,1,0:T(8,128)S(1)}, f32[6,24,384]{2,1,0:T(8,128)S(1)}, u32[]{:S(2)}, u32[]{:S(2)}) collective-permute-start(f32[6,24,384]{2,1,0:T(8,128)S(1)} %pad_maximum_fusion.4), channel_id=1, source_target_pairs={{0,16},{16,32},{32,48},{48,0},{1,17},{17,33},{33,49},{49,1},{2,18}... | collective-permute-start | bytes 663560 | tf_op jit(solution)/shard_map/ppermute | solution.py:340
  231.9 12.1 %all-to-all-start.1 = ((f32[2,2,6,24,384]{4,3,2,0,1:T(8,128)}), f32[2,2,6,24,384]{4,3,2,0,1:T(8,128)S(1)}, u32[]{:S(2)}, u32[]{:S(2)}) async-start(f32[2,2,6,24,384]{4,3,2,0,1:T(8,128)} %copy.14), calls=%async_computation.2 | async-start | bytes 1769472 | tf_op jit(solution)/shard_map/all_to_all | solution.py:396
  237.6 16.5 %collective-permute-start.15 = (f32[6,24,384]{2,1,0:T(8,128)S(1)}, f32[6,24,384]{2,1,0:T(8,128)S(1)}, u32[]{:S(2)}, u32[]{:S(2)}) collective-permute-start(f32[6,24,384]{2,1,0:T(8,128)S(1)} %fusion.4), channel_id=1, source_target_pairs={{0,0},{1,64},{4,16},{5,80},{8,32},{9,96},{12,48},{13,112},{16,4},{... | collective-permute-start | bytes 663560 | tf_op jit(solution)/shard_map/ppermute | solution.py:327
Sparse Core Ops, SparseCore 0:
  39.7 71.9 all-gather.2
  168.3 44.3 reduce-scatter.1

commit v3 on v2

--- a/solution.py
+++ b/solution.py
@@ -122,9 +122,9 @@
     return first, second
 
 
-FORWARD = 8
-MIDDLE = 12
-INVERSE = 8
+FORWARD = 4
+MIDDLE = 3
+INVERSE = 4
 LINES = N // MIDDLE
 HELD = N * PLANES
 
@@ -139,8 +139,8 @@
     def forward(near, half):
         base = near * HELD + half * 2 * SUB
         for p in range(SUB):
-            reals = pick(core, own[0, 0, 0, p], other[0, 0, 0, p])
-            imags = pick(core, own[0, 1, 0, p], other[0, 1, 0, p])
+            reals = pick(core, own[0, 0, half, p], other[0, 0, half, p])
+            imags = pick(core, own[0, 1, half, p], other[0, 1, half, p])
             rows = []
             for c in range(2):
                 phi = phi_ref[0, 2 * half + c, p]
@@ -221,8 +221,8 @@
                 axis=0,
             )
             lines = times_right(lines, right.at[Z_INV])
-            reals = pick(core, own[0, 0, 0, p], other[0, 0, 0, p])
-            imags = pick(core, own[0, 1, 0, p], other[0, 1, 0, p])
+            reals = pick(core, own[0, 0, half, p], other[0, 0, half, p])
+            imags = pick(core, own[0, 1, half, p], other[0, 1, half, p])
             terms = []
             for c in range(2):
                 real = fold(lines[c * N : (c + 1) * N, :LANES])
@@ -232,12 +232,13 @@
                 local_ref[at, 0, p] = reals[c] * real + imags[c] * imag
                 terms.append((phi * real, phi * imag))
             for r in range(2):
-                keep[0, r, 0, p] = jnp.where(core == 0, terms[0][r], terms[1][r])
-                send[0, r, 0, p] = jnp.where(core == 0, terms[1][r], terms[0][r])
+                keep[0, r, half, p] = jnp.where(core == 0, terms[0][r], terms[1][r])
+                send[0, r, half, p] = jnp.where(core == 0, terms[1][r], terms[0][r])
 
     @pl.when(step < FORWARD)
     def _():
-        forward(step // 2, step % 2)
+        for half in range(2):
+            forward(step, half)
 
     @pl.when((step >= FORWARD) & (step < FORWARD + MIDDLE))
     def _():
@@ -245,8 +246,8 @@
 
     @pl.when(step >= FORWARD + MIDDLE)
     def _():
-        last = step - (FORWARD + MIDDLE)
-        inverse(last // 2, last % 2)
+        for half in range(2):
+            inverse(step - (FORWARD + MIDDLE), half)
 
 
 def whole(table):
@@ -254,14 +255,11 @@
 
 
 def in_place(step):
-    last = step - (FORWARD + MIDDLE)
-    at = jnp.where(step < FORWARD, step, jnp.maximum(last, 0))
-    return at // 2, at % 2
+    return jnp.where(step < FORWARD, step, out_place(step))
 
 
 def out_place(step):
-    at = jnp.maximum(step - (FORWARD + MIDDLE), 0)
-    return at // 2, at % 2
+    return jnp.maximum(step - (FORWARD + MIDDLE), 0)
 
 
 PIECE = (2, 2, SUB, ROWS, WIDTH)
@@ -269,21 +267,19 @@
 
 def solve(ids, phi, own, other):
     tables = [jnp.asarray(RIGHT), jnp.asarray(LEFT)]
-    block = (1, 2, 1, SUB, ROWS, WIDTH)
+    block = (1, 2, 2, SUB, ROWS, WIDTH)
 
     def phi_at(step, ids):
-        return ((ids[1] + in_place(step)[0]) & 3, 0, 0, 0, 0)
+        return ((ids[1] + in_place(step)) & 3, 0, 0, 0, 0)
 
     def block_at(step, ids):
-        near, half = in_place(step)
-        return (near, 0, half, 0, 0, 0)
+        return (in_place(step), 0, 0, 0, 0, 0)
 
     def term_at(step, ids):
-        near, half = out_place(step)
-        return (near, 0, half, 0, 0, 0)
+        return (out_place(step), 0, 0, 0, 0, 0)
 
     def local_at(step, ids):
-        return (0, (ids[2] + out_place(step)[0]) & 3, 0, 0, 0)
+        return (0, (ids[2] + out_place(step)) & 3, 0, 0, 0)
 
     return pl.pallas_call(
         field_kernel,

time: 263 us -> 252 us (0.958)
  Pallas kernels: 44 us -> 33.4 us
    pallas_call x1, Pallas kernels: 44 us -> 33.4 us  [solve(): pl.pallas_call(field_kernel, grid_spec=pltpu.PrefetchScalarGridSpec(num_s...]
where the time goes in v3:
time: 252 us
  waiting for transfers between devices  142 us (56%)
  starting transfers between devices  41.2 us (16%)
  Pallas kernels  33.4 us (13%)
  between operations  18.1 us (7%)
  local copies, waits for them, and re-layouts  12.1 us (5%)
  other arithmetic  4.8 us (2%)
    ppermute x12, waiting for transfers between devices, shifted(): lax.ppermute(value, axis, [(ring[i], ring[(i + step) % 4]) for i in range...  64 us
    all_to_all x1, waiting for transfers between devices, per_device(): blocks = lax.all_to_all(blocks, ('x_lo', 'y', 'x_hi'), 0, 0, tiled=True)  42.4 us
    pallas_call x1, Pallas kernels, solve(): pl.pallas_call(field_kernel, grid_spec=pltpu.PrefetchScalarGridSpec(num_s...  33.4 us
    ppermute x12, starting transfers between devices, shifted(): lax.ppermute(value, axis, [(ring[i], ring[(i + step) % 4]) for i in range...  19.8 us
    ppermute x2, waiting for transfers between devices, turn(): return lax.ppermute(value, TURN_AXES, pairs)  18.8 us
    ppermute x2, waiting for transfers between devices, other_core(): return lax.ppermute(value, 'core', [(0, 1), (1, 0)])  12.5 us
    ppermute x2, starting transfers between devices, turn(): return lax.ppermute(value, TURN_AXES, pairs)  8.46 us
    all_to_all x1, starting transfers between devices, per_device(): blocks = lax.all_to_all(blocks, ('x_lo', 'y', 'x_hi'), 0, 0, tiled=True)  7.61 us
  transfers between devices with their start and end apart: 20, of which 14 were waited for; matrix products, arithmetic and copies ran while one was open for 3% of the time, Pallas kernels for 0%

profile of v3, /device:TPU:28, one launch (start us, length us, event | category | flops | bytes accessed | tf_op | source)
XLA Modules:
  0.0 251.6 jit_solution(1466194613933567945)
XLA Ops:
  7.2 1.5 reduce
  8.7 5.6 %collective-permute-start = (f32[6,24,384]{2,1,0:T(8,128)S(1)}, f32[6,24,384]{2,1,0:T(8,128)}, u32[]{:S(2)}, u32[]{:S(2)}) collective-permute-start(f32[6,24,384]{2,1,0:T(8,128)S(1)} %bitcast.75), channel_id=1, source_target_pairs={{0,0},{1,64},{4,16},{5,80},{8,32},{9,96},{12,48},{13,112},{16,4},{... | collective-permute-start | bytes 663560 | tf_op jit(solution)/shard_map/ppermute | solution.py:323
  14.3 2.6 %copy.18 = f32[12,8,24,384]{3,2,1,0:T(8,128)S(1)} copy(f32[12,8,24,384]{3,1,2,0:T(8,128)} %bitcast.68) | data formatting | bytes 7077888
  16.9 10.1 %collective-permute-done = f32[6,24,384]{2,1,0:T(8,128)} collective-permute-done((f32[6,24,384]{2,1,0:T(8,128)S(1)}, f32[6,24,384]{2,1,0:T(8,128)}, u32[]{:S(2)}, u32[]{:S(2)}) %collective-permute-start) | collective-permute-done | bytes 221216 | tf_op jit(solution)/shard_map/ppermute | solution.py:323
  27.0 2.0 copy.13
  29.1 7.6 %all-to-all-start = ((f32[16,6,24,384]{3,2,1,0:T(8,128)}), f32[16,6,24,384]{3,2,1,0:T(8,128)S(1)}, u32[]{:S(2)}, u32[]{:S(2)}) async-start(f32[16,6,24,384]{3,2,1,0:T(8,128)} %copy.13), calls=%async_computation | async-start | bytes 7077888 | tf_op jit(solution)/shard_map/all_to_all | solution.py:378
  36.7 0.7 all-gather.3.cloned.1.call-update
  37.5 0.6 fusion.6
  42.0 42.4 %all-to-all-done = f32[16,6,24,384]{3,2,1,0:T(8,128)S(1)} async-done(((f32[16,6,24,384]{3,2,1,0:T(8,128)}), f32[16,6,24,384]{3,2,1,0:T(8,128)S(1)}, u32[]{:S(2)}, u32[]{:S(2)}) %all-to-all-start) | async-done | bytes 3538976 | tf_op jit(solution)/shard_map/all_to_all | solution.py:378
  84.4 0.1 fusion.5
  84.5 1.4 collective-permute-start.1
  85.9 0.7 collective-permute-start.2
  86.6 17.6 %collective-permute-done.1 = f32[2,2,6,24,384]{4,3,2,1,0:T(8,128)S(1)} collective-permute-done((f32[2,2,6,24,384]{4,3,2,1,0:T(8,128)S(1)}, f32[2,2,6,24,384]{4,3,2,1,0:T(8,128)S(1)}, u32[]{:S(2)}, u32[]{:S(2)}) %collective-permute-start.1) | collective-permute-done | bytes 884768 | tf_op jit(solution)/shard_map/ppermute | solution.py:336
  104.2 1.4 collective-permute-start.4
  105.6 0.8 collective-permute-start.3
  106.4 6.6 %collective-permute-done.4 = f32[1,2,6,24,384]{4,3,2,1,0:T(8,128)S(1)} collective-permute-done((f32[1,2,6,24,384]{4,3,2,1,0:T(8,128)S(1)}, f32[1,2,6,24,384]{4,3,2,1,0:T(8,128)S(1)}, u32[]{:S(2)}, u32[]{:S(2)}) %collective-permute-start.4) | collective-permute-done | bytes 442400 | tf_op jit(solution)/shard_map/ppermute | solution.py:336
  113.0 2.2 collective-permute-done.3
  115.3 0.2 pad_maximum_fusion.own
  115.5 0.1 collective-permute-start.5
  115.7 6.3 %collective-permute-done.5.other = f32[4,2,2,6,24,384]{5,4,3,2,1,0:T(8,128)} collective-permute-done((f32[4,2,2,6,24,384]{5,4,3,2,1,0:T(8,128)S(1)}, f32[4,2,2,6,24,384]{5,4,3,2,1,0:T(8,128)}, u32[]{:S(2)}, u32[]{:S(2)}) %collective-permute-start.5) | collective-permute-done | bytes 3538976 | tf_op jit(solution)/shard_map/ppermute | solution.py:327
  122.0 1.1 copy-done
  123.1 1.0 copy-done.1
  124.1 33.4 %shard_map.68 = (f32[4,2,2,6,24,384]{5,4,3,2,1,0:T(8,128)S(1)}, f32[4,2,2,6,24,384]{5,4,3,2,1,0:T(8,128)}, f32[4,4,6,24,384]{4,3,2,1,0:T(8,128)}) custom-call(s32[3]{0:T(128)S(1)} %pad_add_fusion.ids, f32[4,4,6,24,384]{4,3,2,1,0:T(8,128)} %bitcast.76, f32[4,2,2,6,24,384]{5,4,3,2,1,0:T(8,128)} %copy-done.2, ...), custom_call_target="tpu_custom_call" | custom-call | flops 12230590464 | bytes 35000000 | tf_op jit(solution)/shard_map/pallas_call | solution.py:284
  157.6 0.4 collective-permute-start.6
  158.0 6.3 %collective-permute-done.6 = f32[4,2,2,6,24,384]{5,4,3,2,1,0:T(8,128)S(1)} collective-permute-done((f32[4,2,2,6,24,384]{5,4,3,2,1,0:T(8,128)}, f32[4,2,2,6,24,384]{5,4,3,2,1,0:T(8,128)S(1)}, u32[]{:S(2)}, u32[]{:S(2)}) %collective-permute-start.6) | collective-permute-done | bytes 3538976 | tf_op jit(solution)/shard_map/ppermute | solution.py:327
  164.3 0.5 add.38
  164.7 0.1 slice_bitcast_fusion.5
  164.9 3.2 %collective-permute-start.9 = (f32[1,2,6,24,384]{4,3,2,1,0:T(8,128)S(1)}, f32[1,2,6,24,384]{4,3,2,1,0:T(8,128)S(1)}, u32[]{:S(2)}, u32[]{:S(2)}) collective-permute-start(f32[1,2,6,24,384]{4,3,2,1,0:T(8,128)S(1)} %get-tuple-element.25), channel_id=1, source_target_pairs={{0,12},{4,0},{8,4},{12,8},{1,13},{5,1},{9,5},{13,9},{2,14},{6,2},{... | collective-permute-start | bytes 1327112 | tf_op jit(solution)/shard_map/ppermute | solution.py:336
  168.1 10.2 %collective-permute-done.7 = f32[1,2,6,24,384]{4,3,2,1,0:T(8,128)S(1)} collective-permute-done((f32[1,2,6,24,384]{4,3,2,1,0:T(8,128)S(1)}, f32[1,2,6,24,384]{4,3,2,1,0:T(8,128)S(1)}, u32[]{:S(2)}, u32[]{:S(2)}) %collective-permute-start.7) | collective-permute-done | bytes 442400 | tf_op jit(solution)/shard_map/ppermute | solution.py:336
  178.3 0.1 fusion.3
  178.5 3.0 %collective-permute-start.10 = (f32[2,2,6,24,384]{4,3,2,1,0:T(8,128)S(1)}, f32[2,2,6,24,384]{4,3,2,1,0:T(8,128)S(1)}, u32[]{:S(2)}, u32[]{:S(2)}) collective-permute-start(f32[2,2,6,24,384]{4,3,2,1,0:T(8,128)S(1)} %pad_maximum_fusion.3), channel_id=1, source_target_pairs={{0,12},{4,0},{8,4},{12,8},{1,13},{5,1},{9,5},{13,9},{2,14},{6,2},{... | collective-permute-start | bytes 2654216 | tf_op jit(solution)/shard_map/ppermute | solution.py:336
  181.7 17.9 %collective-permute-done.10 = f32[2,2,6,24,384]{4,3,2,1,0:T(8,128)S(1)} collective-permute-done((f32[2,2,6,24,384]{4,3,2,1,0:T(8,128)S(1)}, f32[2,2,6,24,384]{4,3,2,1,0:T(8,128)S(1)}, u32[]{:S(2)}, u32[]{:S(2)}) %collective-permute-start.10) | collective-permute-done | bytes 884768 | tf_op jit(solution)/shard_map/ppermute | solution.py:336
  199.6 3.6 %collective-permute-done.8 = f32[2,2,6,24,384]{4,3,2,1,0:T(8,128)S(1)} collective-permute-done((f32[2,2,6,24,384]{4,3,2,1,0:T(8,128)S(1)}, f32[2,2,6,24,384]{4,3,2,1,0:T(8,128)S(1)}, u32[]{:S(2)}, u32[]{:S(2)}) %collective-permute-start.8) | collective-permute-done | bytes 884768 | tf_op jit(solution)/shard_map/ppermute | solution.py:336
  203.2 0.1 fusion.1
  203.3 1.1 slice_bitcast_fusion.10
  204.4 5.7 %collective-permute-start.11 = (f32[3,24,384]{2,1,0:T(8,128)S(1)}, f32[3,24,384]{2,1,0:T(8,128)S(1)}, u32[]{:S(2)}, u32[]{:S(2)}) collective-permute-start(f32[3,24,384]{2,1,0:T(8,128)S(1)} %get-tuple-element.32), channel_id=1, source_target_pairs={{0,16},{16,32},{32,48},{48,0},{1,17},{17,33},{33,49},{49,1},{2,18}... | collective-permute-start | bytes 331784 | tf_op jit(solution)/shard_map/ppermute | solution.py:336
  210.2 2.6 %collective-permute-done.11 = f32[3,24,384]{2,1,0:T(8,128)S(1)} collective-permute-done((f32[3,24,384]{2,1,0:T(8,128)S(1)}, f32[3,24,384]{2,1,0:T(8,128)S(1)}, u32[]{:S(2)}, u32[]{:S(2)}) %collective-permute-start.11) | collective-permute-done | bytes 110624 | tf_op jit(solution)/shard_map/ppermute | solution.py:336
  212.8 3.3 %collective-permute-done.13 = f32[3,24,384]{2,1,0:T(8,128)S(1)} collective-permute-done((f32[3,24,384]{2,1,0:T(8,128)S(1)}, f32[3,24,384]{2,1,0:T(8,128)S(1)}, u32[]{:S(2)}, u32[]{:S(2)}) %collective-permute-start.13) | collective-permute-done | bytes 110624 | tf_op jit(solution)/shard_map/ppermute | solution.py:336
  216.1 1.0 bitcast_add_fusion.2
  217.2 3.3 %collective-permute-start.12 = (f32[6,24,384]{2,1,0:T(8,128)S(1)}, f32[6,24,384]{2,1,0:T(8,128)S(1)}, u32[]{:S(2)}, u32[]{:S(2)}) collective-permute-start(f32[6,24,384]{2,1,0:T(8,128)S(1)} %pad_maximum_fusion.4), channel_id=1, source_target_pairs={{0,16},{16,32},{32,48},{48,0},{1,17},{17,33},{33,49},{49,1},{2,18}... | collective-permute-start | bytes 663560 | tf_op jit(solution)/shard_map/ppermute | solution.py:336
  220.5 1.0 copy.14
  221.5 4.8 %all-to-all-start.1 = ((f32[2,2,6,24,384]{4,3,2,0,1:T(8,128)}), f32[2,2,6,24,384]{4,3,2,0,1:T(8,128)S(1)}, u32[]{:S(2)}, u32[]{:S(2)}) async-start(f32[2,2,6,24,384]{4,3,2,0,1:T(8,128)} %copy.14), calls=%async_computation.2 | async-start | bytes 1769472 | tf_op jit(solution)/shard_map/all_to_all | solution.py:392
  226.3 1.0 fusion.4
  227.3 2.9 %collective-permute-start.15 = (f32[6,24,384]{2,1,0:T(8,128)S(1)}, f32[6,24,384]{2,1,0:T(8,128)S(1)}, u32[]{:S(2)}, u32[]{:S(2)}) collective-permute-start(f32[6,24,384]{2,1,0:T(8,128)S(1)} %fusion.4), channel_id=1, source_target_pairs={{0,0},{1,64},{4,16},{5,80},{8,32},{9,96},{12,48},{13,112},{16,4},{... | collective-permute-start | bytes 663560 | tf_op jit(solution)/shard_map/ppermute | solution.py:323
  230.1 3.5 %all-to-all-done.1 = f32[2,2,6,24,384]{4,3,2,0,1:T(8,128)S(1)} async-done(((f32[2,2,6,24,384]{4,3,2,0,1:T(8,128)}), f32[2,2,6,24,384]{4,3,2,0,1:T(8,128)S(1)}, u32[]{:S(2)}, u32[]{:S(2)}) %all-to-all-start.1) | async-done | bytes 884768 | tf_op jit(solution)/shard_map/all_to_all | solution.py:392
  233.7 1.4 reshape.39
  235.1 8.7 %collective-permute-done.15 = f32[6,24,384]{2,1,0:T(8,128)S(1)} collective-permute-done((f32[6,24,384]{2,1,0:T(8,128)S(1)}, f32[6,24,384]{2,1,0:T(8,128)S(1)}, u32[]{:S(2)}, u32[]{:S(2)}) %collective-permute-start.15) | collective-permute-done | bytes 221216 | tf_op jit(solution)/shard_map/ppermute | solution.py:323
  243.8 0.9 reshape.42
  (30 shorter events, 0.9 us)
Async XLA Ops:
  8.7 18.4 %collective-permute-start = (f32[6,24,384]{2,1,0:T(8,128)S(1)}, f32[6,24,384]{2,1,0:T(8,128)}, u32[]{:S(2)}, u32[]{:S(2)}) collective-permute-start(f32[6,24,384]{2,1,0:T(8,128)S(1)} %bitcast.75), channel_id=1, source_target_pairs={{0,0},{1,64},{4,16},{5,80},{8,32},{9,96},{12,48},{13,112},{16,4},{... | collective-permute-start | bytes 663560 | tf_op jit(solution)/shard_map/ppermute | solution.py:323
  29.1 8.4 %copy-start.3 = (s32[2]{0:T(128)S(1)}, s32[2]{0:T(128)}, u32[]{:S(2)}) copy-start(s32[2]{0:T(128)} %param.7) | copy-start | bytes 28
  29.1 55.2 %all-to-all-start = ((f32[16,6,24,384]{3,2,1,0:T(8,128)}), f32[16,6,24,384]{3,2,1,0:T(8,128)S(1)}, u32[]{:S(2)}, u32[]{:S(2)}) async-start(f32[16,6,24,384]{3,2,1,0:T(8,128)} %copy.13), calls=%async_computation | async-start | bytes 7077888 | tf_op jit(solution)/shard_map/all_to_all | solution.py:378
  36.7 79.0 %all-gather.3.cloned.1.call-start = ((), (), s32[]{:S(2)}) async-start(), calls=%async_computation.4 | async-start | bytes 3760128 | tf_op jit(solution)/shard_map/all_gather | solution.py:376
  37.4 165.9 %reduce-scatter.2.cloned.1.call-start = ((), (), s32[]{:S(2)}) async-start(), calls=%async_computation.3 | async-start | bytes 4423680 | tf_op jit(solution)/shard_map/reduce_scatter | solution.py:388
  84.5 19.7 %collective-permute-start.1 = (f32[2,2,6,24,384]{4,3,2,1,0:T(8,128)S(1)}, f32[2,2,6,24,384]{4,3,2,1,0:T(8,128)S(1)}, u32[]{:S(2)}, u32[]{:S(2)}) collective-permute-start(f32[2,2,6,24,384]{4,3,2,1,0:T(8,128)S(1)} %get-tuple-element.37), channel_id=1, source_target_pairs={{0,12},{4,0},{8,4},{12,8},{1,13},{5,1},{9,5},{13,9},{2,14},{6,2},{... | collective-permute-start | bytes 2654216 | tf_op jit(solution)/shard_map/ppermute | solution.py:336
  85.9 19.7 %collective-permute-start.2 = (f32[2,2,6,24,384]{4,3,2,1,0:T(8,128)S(1)}, f32[2,2,6,24,384]{4,3,2,1,0:T(8,128)S(1)}, u32[]{:S(2)}, u32[]{:S(2)}) collective-permute-start(f32[2,2,6,24,384]{4,3,2,1,0:T(8,128)S(1)} %get-tuple-element.37), channel_id=1, source_target_pairs={{0,4},{4,8},{8,12},{12,0},{1,5},{5,9},{9,13},{13,1},{2,6},{6,10},{... | collective-permute-start | bytes 2654216 | tf_op jit(solution)/shard_map/ppermute | solution.py:336
  104.2 8.8 %collective-permute-start.4 = (f32[1,2,6,24,384]{4,3,2,1,0:T(8,128)S(1)}, f32[1,2,6,24,384]{4,3,2,1,0:T(8,128)S(1)}, u32[]{:S(2)}, u32[]{:S(2)}) collective-permute-start(f32[1,2,6,24,384]{4,3,2,1,0:T(8,128)S(1)} %slice.139), channel_id=1, source_target_pairs={{0,12},{4,0},{8,4},{12,8},{1,13},{5,1},{9,5},{13,9},{2,14},{6,2},{... | collective-permute-start | bytes 1327112 | tf_op jit(solution)/shard_map/ppermute | solution.py:336
  105.6 9.6 %collective-permute-start.3 = (f32[1,2,6,24,384]{4,3,2,1,0:T(8,128)S(1)}, f32[1,2,6,24,384]{4,3,2,1,0:T(8,128)S(1)}, u32[]{:S(2)}, u32[]{:S(2)}) collective-permute-start(f32[1,2,6,24,384]{4,3,2,1,0:T(8,128)S(1)} %slice.138), channel_id=1, source_target_pairs={{0,4},{4,8},{8,12},{12,0},{1,5},{5,9},{9,13},{13,1},{2,6},{6,10},{... | collective-permute-start | bytes 1327112 | tf_op jit(solution)/shard_map/ppermute | solution.py:336
  115.5 6.4 %copy-start.2 = (f32[4,2,2,6,24,384]{5,4,3,2,1,0:T(8,128)}, f32[4,2,2,6,24,384]{5,4,3,2,1,0:T(8,128)S(1)}, u32[]{:S(2)}) copy-start(f32[4,2,2,6,24,384]{5,4,3,2,1,0:T(8,128)S(1)} %pad_maximum_fusion.own) | copy-start | bytes 10616836
  115.5 6.4 %collective-permute-start.5 = (f32[4,2,2,6,24,384]{5,4,3,2,1,0:T(8,128)S(1)}, f32[4,2,2,6,24,384]{5,4,3,2,1,0:T(8,128)}, u32[]{:S(2)}, u32[]{:S(2)}) collective-permute-start(f32[4,2,2,6,24,384]{5,4,3,2,1,0:T(8,128)S(1)} %pad_maximum_fusion.own), channel_id=1, source_target_pairs={{0,1},{1,0},{2,3},{3,2},{4,5},{5,4},{6,7},{7,6},{8,9},{9,8},{10,11... | collective-permute-start | bytes 10616840 | tf_op jit(solution)/shard_map/ppermute | solution.py:327
  122.0 1.1 copy-start
  123.1 1.0 copy-start.1
  157.6 6.7 %collective-permute-start.6 = (f32[4,2,2,6,24,384]{5,4,3,2,1,0:T(8,128)}, f32[4,2,2,6,24,384]{5,4,3,2,1,0:T(8,128)S(1)}, u32[]{:S(2)}, u32[]{:S(2)}) collective-permute-start(f32[4,2,2,6,24,384]{5,4,3,2,1,0:T(8,128)} %get-tuple-element.12), channel_id=1, source_target_pairs={{0,1},{1,0},{2,3},{3,2},{4,5},{5,4},{6,7},{7,6},{8,9},{9,8},{10,11... | collective-permute-start | bytes 10616840 | tf_op jit(solution)/shard_map/ppermute | solution.py:327
  164.8 13.5 %collective-permute-start.7 = (f32[1,2,6,24,384]{4,3,2,1,0:T(8,128)S(1)}, f32[1,2,6,24,384]{4,3,2,1,0:T(8,128)S(1)}, u32[]{:S(2)}, u32[]{:S(2)}) collective-permute-start(f32[1,2,6,24,384]{4,3,2,1,0:T(8,128)S(1)} %get-tuple-element.24), channel_id=1, source_target_pairs={{0,4},{4,8},{8,12},{12,0},{1,5},{5,9},{9,13},{13,1},{2,6},{6,10},{... | collective-permute-start | bytes 1327112 | tf_op jit(solution)/shard_map/ppermute | solution.py:336
  164.9 13.4 %collective-permute-start.9 = (f32[1,2,6,24,384]{4,3,2,1,0:T(8,128)S(1)}, f32[1,2,6,24,384]{4,3,2,1,0:T(8,128)S(1)}, u32[]{:S(2)}, u32[]{:S(2)}) collective-permute-start(f32[1,2,6,24,384]{4,3,2,1,0:T(8,128)S(1)} %get-tuple-element.25), channel_id=1, source_target_pairs={{0,12},{4,0},{8,4},{12,8},{1,13},{5,1},{9,5},{13,9},{2,14},{6,2},{... | collective-permute-start | bytes 1327112 | tf_op jit(solution)/shard_map/ppermute | solution.py:336
  178.5 21.1 %collective-permute-start.10 = (f32[2,2,6,24,384]{4,3,2,1,0:T(8,128)S(1)}, f32[2,2,6,24,384]{4,3,2,1,0:T(8,128)S(1)}, u32[]{:S(2)}, u32[]{:S(2)}) collective-permute-start(f32[2,2,6,24,384]{4,3,2,1,0:T(8,128)S(1)} %pad_maximum_fusion.3), channel_id=1, source_target_pairs={{0,12},{4,0},{8,4},{12,8},{1,13},{5,1},{9,5},{13,9},{2,14},{6,2},{... | collective-permute-start | bytes 2654216 | tf_op jit(solution)/shard_map/ppermute | solution.py:336
  181.6 21.5 %collective-permute-start.8 = (f32[2,2,6,24,384]{4,3,2,1,0:T(8,128)S(1)}, f32[2,2,6,24,384]{4,3,2,1,0:T(8,128)S(1)}, u32[]{:S(2)}, u32[]{:S(2)}) collective-permute-start(f32[2,2,6,24,384]{4,3,2,1,0:T(8,128)S(1)} %pad_maximum_fusion.2), channel_id=1, source_target_pairs={{0,4},{4,8},{8,12},{12,0},{1,5},{5,9},{9,13},{13,1},{2,6},{6,10},{... | collective-permute-start | bytes 2654216 | tf_op jit(solution)/shard_map/ppermute | solution.py:336
  204.4 8.4 %collective-permute-start.11 = (f32[3,24,384]{2,1,0:T(8,128)S(1)}, f32[3,24,384]{2,1,0:T(8,128)S(1)}, u32[]{:S(2)}, u32[]{:S(2)}) collective-permute-start(f32[3,24,384]{2,1,0:T(8,128)S(1)} %get-tuple-element.32), channel_id=1, source_target_pairs={{0,16},{16,32},{32,48},{48,0},{1,17},{17,33},{33,49},{49,1},{2,18}... | collective-permute-start | bytes 331784 | tf_op jit(solution)/shard_map/ppermute | solution.py:336
  210.2 6.0 %collective-permute-start.13 = (f32[3,24,384]{2,1,0:T(8,128)S(1)}, f32[3,24,384]{2,1,0:T(8,128)S(1)}, u32[]{:S(2)}, u32[]{:S(2)}) collective-permute-start(f32[3,24,384]{2,1,0:T(8,128)S(1)} %get-tuple-element.33), channel_id=1, source_target_pairs={{0,48},{16,0},{32,16},{48,32},{1,49},{17,1},{33,17},{49,33},{2,50}... | collective-permute-start | bytes 331784 | tf_op jit(solution)/shard_map/ppermute | solution.py:336
  217.1 9.2 %collective-permute-start.14 = (f32[6,24,384]{2,1,0:T(8,128)S(1)}, f32[6,24,384]{2,1,0:T(8,128)S(1)}, u32[]{:S(2)}, u32[]{:S(2)}) collective-permute-start(f32[6,24,384]{2,1,0:T(8,128)S(1)} %pad_maximum_fusion.5), channel_id=1, source_target_pairs={{0,48},{16,0},{32,16},{48,32},{1,49},{17,1},{33,17},{49,33},{2,50}... | collective-permute-start | bytes 663560 | tf_op jit(solution)/shard_map/ppermute | solution.py:336
  217.2 9.1 %collective-permute-start.12 = (f32[6,24,384]{2,1,0:T(8,128)S(1)}, f32[6,24,384]{2,1,0:T(8,128)S(1)}, u32[]{:S(2)}, u32[]{:S(2)}) collective-permute-start(f32[6,24,384]{2,1,0:T(8,128)S(1)} %pad_maximum_fusion.4), channel_id=1, source_target_pairs={{0,16},{16,32},{32,48},{48,0},{1,17},{17,33},{33,49},{49,1},{2,18}... | collective-permute-start | bytes 663560 | tf_op jit(solution)/shard_map/ppermute | solution.py:336
  221.5 12.1 %all-to-all-start.1 = ((f32[2,2,6,24,384]{4,3,2,0,1:T(8,128)}), f32[2,2,6,24,384]{4,3,2,0,1:T(8,128)S(1)}, u32[]{:S(2)}, u32[]{:S(2)}) async-start(f32[2,2,6,24,384]{4,3,2,0,1:T(8,128)} %copy.14), calls=%async_computation.2 | async-start | bytes 1769472 | tf_op jit(solution)/shard_map/all_to_all | solution.py:392
  227.3 16.5 %collective-permute-start.15 = (f32[6,24,384]{2,1,0:T(8,128)S(1)}, f32[6,24,384]{2,1,0:T(8,128)S(1)}, u32[]{:S(2)}, u32[]{:S(2)}) collective-permute-start(f32[6,24,384]{2,1,0:T(8,128)S(1)} %fusion.4), channel_id=1, source_target_pairs={{0,0},{1,64},{4,16},{5,80},{8,32},{9,96},{12,48},{13,112},{16,4},{... | collective-permute-start | bytes 663560 | tf_op jit(solution)/shard_map/ppermute | solution.py:323
Sparse Core Ops, SparseCore 0:
  39.7 71.9 all-gather.2
  157.7 44.3 reduce-scatter.1

commit v4 on v3

--- a/solution.py
+++ b/solution.py
@@ -123,24 +123,29 @@
 
 
 FORWARD = 4
-MIDDLE = 3
+MIDDLE = 2
 INVERSE = 4
 LINES = N // MIDDLE
 HELD = N * PLANES
 
 
 def field_kernel(
-    ids, phi_ref, own, other, right, left,
+    ids, phi_ref, own, other, own_far, other_far, right, left,
     keep, send, local_ref, re_ref, im_ref
 ):
     core = ids[0]
     step = pl.program_id(0)
 
+    def block_planes(far, r, half, p):
+        mine = jnp.where(far, own_far[r, half, p], own[0, r, half, p])
+        theirs = jnp.where(far, other_far[r, half, p], other[0, r, half, p])
+        return pick(core, mine, theirs)
+
     def forward(near, half):
         base = near * HELD + half * 2 * SUB
         for p in range(SUB):
-            reals = pick(core, own[0, 0, half, p], other[0, 0, half, p])
-            imags = pick(core, own[0, 1, half, p], other[0, 1, half, p])
+            reals = block_planes(near == FAR, 0, half, p)
+            imags = block_planes(near == FAR, 1, half, p)
             rows = []
             for c in range(2):
                 phi = phi_ref[0, 2 * half + c, p]
@@ -221,8 +226,8 @@
                 axis=0,
             )
             lines = times_right(lines, right.at[Z_INV])
-            reals = pick(core, own[0, 0, half, p], other[0, 0, half, p])
-            imags = pick(core, own[0, 1, half, p], other[0, 1, half, p])
+            reals = block_planes(near == FAR, 0, half, p)
+            imags = block_planes(near == FAR, 1, half, p)
             terms = []
             for c in range(2):
                 real = fold(lines[c * N : (c + 1) * N, :LANES])
@@ -238,7 +243,7 @@
     @pl.when(step < FORWARD)
     def _():
         for half in range(2):
-            forward(step, half)
+            forward(in_place(step), half)
 
     @pl.when((step >= FORWARD) & (step < FORWARD + MIDDLE))
     def _():
@@ -247,25 +252,40 @@
     @pl.when(step >= FORWARD + MIDDLE)
     def _():
         for half in range(2):
-            inverse(step - (FORWARD + MIDDLE), half)
+            inverse(out_place(step), half)
 
 
 def whole(table):
     return pl.BlockSpec(table.shape, lambda *_: (0,) * table.ndim)
 
 
+FAR = 2
+
+
+def order(step):
+    return step ^ (step >> 1)
+
+
+def in_step(step):
+    return jnp.where(step < FORWARD, step, out_step(step))
+
+
+def out_step(step):
+    return jnp.maximum(step - (FORWARD + MIDDLE), 0)
+
+
 def in_place(step):
-    return jnp.where(step < FORWARD, step, out_place(step))
+    return order(in_step(step))
 
 
 def out_place(step):
-    return jnp.maximum(step - (FORWARD + MIDDLE), 0)
+    return order(out_step(step))
 
 
 PIECE = (2, 2, SUB, ROWS, WIDTH)
 
 
-def solve(ids, phi, own, other):
+def solve(ids, phi, own, other, own_far, other_far):
     tables = [jnp.asarray(RIGHT), jnp.asarray(LEFT)]
     block = (1, 2, 2, SUB, ROWS, WIDTH)
 
@@ -273,7 +293,7 @@
         return ((ids[1] + in_place(step)) & 3, 0, 0, 0, 0)
 
     def block_at(step, ids):
-        return (in_place(step), 0, 0, 0, 0, 0)
+        return (jnp.minimum(in_step(step), 2), 0, 0, 0, 0, 0)
 
     def term_at(step, ids):
         return (out_place(step), 0, 0, 0, 0, 0)
@@ -290,6 +310,8 @@
                 pl.BlockSpec((1, 4, SUB, ROWS, WIDTH), phi_at),
                 pl.BlockSpec(block, block_at),
                 pl.BlockSpec(block, block_at),
+                whole(own_far),
+                whole(other_far),
             ]
             + [whole(t) for t in tables],
             out_specs=[
@@ -297,7 +319,7 @@
                 pl.BlockSpec(block, term_at),
                 pl.BlockSpec((4, 1, SUB, ROWS, WIDTH), local_at),
             ],
-            scratch_shapes=[pltpu.VMEM((4 * HELD, LANES), f32)] * 2,
+            scratch_shapes=[pltpu.VMEM((4 * HELD + PLANES, LANES), f32)] * 2,
         ),
         out_shape=[jax.ShapeDtypeStruct((4, *PIECE), f32)] * 2
         + [jax.ShapeDtypeStruct((4, 4, SUB, ROWS, WIDTH), f32)],
@@ -305,7 +327,7 @@
         cost_estimate=pl.CostEstimate(
             flops=2 * 3 * 6 * (2 * N) ** 2 * N * N, bytes_accessed=35_000_000, transcendentals=0
         ),
-    )(ids, phi, own, other, *tables)
+    )(ids, phi, own, other, own_far, other_far, *tables)
 
 
 TURN_AXES = ("x_lo", "y", "z", "core")
@@ -353,7 +375,7 @@
     before = ahead(mine, axis)
     after = behind(mine, axis)
     far = ahead(halves_of(before)[0], axis), behind(halves_of(after)[1], axis)
-    return jnp.stack([mine, after, jnp.concatenate(far, axis=0), before])
+    return jnp.stack([mine, after, before]), jnp.concatenate(far, axis=0)
 
 
 def scatter_ring(parts, axis):
@@ -380,10 +402,10 @@
     mine = jnp.stack(
         [lax.dynamic_index_in_dim(blocks, owner[r], 0, False) for r in range(ROUNDS)]
     )
-    own = gather_ring(mine, "z")
-    other = other_core(own)
-
-    keep, send, local = solve(ids, phi, own, other)
+    own, own_far = gather_ring(mine, "z")
+    other, other_far = other_core(own), other_core(own_far)
+
+    keep, send, local = solve(ids, phi, own, other, own_far, other_far)
 
     local = lax.psum_scatter(local, ("x_hi", "x_lo"), scatter_dimension=0)
     total = scatter_ring(keep + other_core(send), "z")

time: 252 us -> 251 us (level)
    ppermute x2 -> x3, waiting for transfers between devices: 12.5 us -> 8.76 us  [other_core(): return lax.ppermute(value, 'core', [(0, 1), (1, 0)])]
  transfers between devices with their start and end apart: 20 -> 21, of which waited for: 14 -> 15; matrix products, arithmetic and copies ran while one was open for 3% -> 3% of each run, Pallas kernels for 0% -> 0%
where the time goes in v4:
time: 251 us
  waiting for transfers between devices  140 us (56%)
  starting transfers between devices  42.6 us (17%)
  Pallas kernels  33.4 us (13%)
  between operations  18.1 us (7%)
  local copies, waits for them, and re-layouts  12.2 us (5%)
  other arithmetic  4.68 us (2%)
    ppermute x12, waiting for transfers between devices, shifted(): lax.ppermute(value, axis, [(ring[i], ring[(i + step) % 4]) for i in range...  65.1 us
    all_to_all x1, waiting for transfers between devices, per_device(): blocks = lax.all_to_all(blocks, ('x_lo', 'y', 'x_hi'), 0, 0, tiled=True)  42.4 us
    pallas_call x1, Pallas kernels, solve(): pl.pallas_call(field_kernel, grid_spec=pltpu.PrefetchScalarGridSpec(num_s...  33.4 us
    ppermute x12, starting transfers between devices, shifted(): lax.ppermute(value, axis, [(ring[i], ring[(i + step) % 4]) for i in range...  20.1 us
    ppermute x2, waiting for transfers between devices, turn(): return lax.ppermute(value, TURN_AXES, pairs)  17.9 us
    ppermute x3, waiting for transfers between devices, other_core(): return lax.ppermute(value, 'core', [(0, 1), (1, 0)])  8.76 us
    ppermute x2, starting transfers between devices, turn(): return lax.ppermute(value, TURN_AXES, pairs)  8.52 us
    all_to_all x1, starting transfers between devices, per_device(): blocks = lax.all_to_all(blocks, ('x_lo', 'y', 'x_hi'), 0, 0, tiled=True)  7.61 us
  transfers between devices with their start and end apart: 21, of which 15 were waited for; matrix products, arithmetic and copies ran while one was open for 3% of the time, Pallas kernels for 0%

profile of v4, /device:TPU:28, one launch (start us, length us, event | category | flops | bytes accessed | tf_op | source)
XLA Modules:
  0.0 250.6 jit_solution(6629195285456962194)
XLA Ops:
  7.2 1.5 reduce
  8.7 5.6 %collective-permute-start = (f32[6,24,384]{2,1,0:T(8,128)S(1)}, f32[6,24,384]{2,1,0:T(8,128)}, u32[]{:S(2)}, u32[]{:S(2)}) collective-permute-start(f32[6,24,384]{2,1,0:T(8,128)S(1)} %bitcast.73), channel_id=1, source_target_pairs={{0,0},{1,64},{4,16},{5,80},{8,32},{9,96},{12,48},{13,112},{16,4},{... | collective-permute-start | bytes 663560 | tf_op jit(solution)/shard_map/ppermute | solution.py:345
  14.3 2.6 %copy.18 = f32[12,8,24,384]{3,2,1,0:T(8,128)S(1)} copy(f32[12,8,24,384]{3,1,2,0:T(8,128)} %bitcast.66) | data formatting | bytes 7077888
  16.9 10.1 %collective-permute-done = f32[6,24,384]{2,1,0:T(8,128)} collective-permute-done((f32[6,24,384]{2,1,0:T(8,128)S(1)}, f32[6,24,384]{2,1,0:T(8,128)}, u32[]{:S(2)}, u32[]{:S(2)}) %collective-permute-start) | collective-permute-done | bytes 221216 | tf_op jit(solution)/shard_map/ppermute | solution.py:345
  27.0 2.0 copy.13
  29.1 7.6 %all-to-all-start = ((f32[16,6,24,384]{3,2,1,0:T(8,128)}), f32[16,6,24,384]{3,2,1,0:T(8,128)S(1)}, u32[]{:S(2)}, u32[]{:S(2)}) async-start(f32[16,6,24,384]{3,2,1,0:T(8,128)} %copy.13), calls=%async_computation | async-start | bytes 7077888 | tf_op jit(solution)/shard_map/all_to_all | solution.py:400
  36.8 0.7 all-gather.3.cloned.1.call-update
  37.5 0.6 fusion.6
  42.0 42.4 %all-to-all-done = f32[16,6,24,384]{3,2,1,0:T(8,128)S(1)} async-done(((f32[16,6,24,384]{3,2,1,0:T(8,128)}), f32[16,6,24,384]{3,2,1,0:T(8,128)S(1)}, u32[]{:S(2)}, u32[]{:S(2)}) %all-to-all-start) | async-done | bytes 3538976 | tf_op jit(solution)/shard_map/all_to_all | solution.py:400
  84.5 1.4 collective-permute-start.1
  85.9 0.7 collective-permute-start.2
  86.6 17.0 %collective-permute-done.1 = f32[2,2,6,24,384]{4,3,2,1,0:T(8,128)S(1)} collective-permute-done((f32[2,2,6,24,384]{4,3,2,1,0:T(8,128)S(1)}, f32[2,2,6,24,384]{4,3,2,1,0:T(8,128)S(1)}, u32[]{:S(2)}, u32[]{:S(2)}) %collective-permute-start.1) | collective-permute-done | bytes 884768 | tf_op jit(solution)/shard_map/ppermute | solution.py:358
  103.6 1.3 collective-permute-done.2
  104.9 0.2 pad_maximum_fusion.own
  105.2 0.5 collective-permute-start.4
  105.7 2.9 %collective-permute-start.5 = (f32[1,2,6,24,384]{4,3,2,1,0:T(8,128)S(1)}, f32[1,2,6,24,384]{4,3,2,1,0:T(8,128)S(1)}, u32[]{:S(2)}, u32[]{:S(2)}) collective-permute-start(f32[1,2,6,24,384]{4,3,2,1,0:T(8,128)S(1)} %slice.139), channel_id=1, source_target_pairs={{0,12},{4,0},{8,4},{12,8},{1,13},{5,1},{9,5},{13,9},{2,14},{6,2},{... | collective-permute-start | bytes 1327112 | tf_op jit(solution)/shard_map/ppermute | solution.py:358
  108.6 10.4 %collective-permute-done.4 = f32[1,2,6,24,384]{4,3,2,1,0:T(8,128)S(1)} collective-permute-done((f32[1,2,6,24,384]{4,3,2,1,0:T(8,128)S(1)}, f32[1,2,6,24,384]{4,3,2,1,0:T(8,128)S(1)}, u32[]{:S(2)}, u32[]{:S(2)}) %collective-permute-start.4) | collective-permute-done | bytes 442400 | tf_op jit(solution)/shard_map/ppermute | solution.py:358
  119.1 0.3 collective-permute-start.6
  119.5 2.5 collective-permute-done.6.other_far
  121.9 1.1 copy-done
  123.1 1.0 copy-done.1
  124.1 33.4 %shard_map.68 = (f32[4,2,2,6,24,384]{5,4,3,2,1,0:T(8,128)}, f32[4,2,2,6,24,384]{5,4,3,2,1,0:T(8,128)}, f32[4,4,6,24,384]{4,3,2,1,0:T(8,128)}) custom-call(s32[3]{0:T(128)S(1)} %pad_add_fusion.ids, f32[4,4,6,24,384]{4,3,2,1,0:T(8,128)} %bitcast.74, f32[3,2,2,6,24,384]{5,4,3,2,1,0:T(8,128)S(1)} %pad_maximum_fusion.own, ...), custom_call_target="tpu_custom_call" | custom-call | flops 12230590464 | bytes 35000000 | tf_op jit(solution)/shard_map/pallas_call | solution.py:304
  157.6 0.2 collective-permute-start.7
  157.8 6.3 %collective-permute-done.7 = f32[4,2,2,6,24,384]{5,4,3,2,1,0:T(8,128)S(1)} collective-permute-done((f32[4,2,2,6,24,384]{5,4,3,2,1,0:T(8,128)}, f32[4,2,2,6,24,384]{5,4,3,2,1,0:T(8,128)S(1)}, u32[]{:S(2)}, u32[]{:S(2)}) %collective-permute-start.7) | collective-permute-done | bytes 3538976 | tf_op jit(solution)/shard_map/ppermute | solution.py:349
  164.1 0.5 add.38
  164.8 3.2 %collective-permute-start.10 = (f32[1,2,6,24,384]{4,3,2,1,0:T(8,128)S(1)}, f32[1,2,6,24,384]{4,3,2,1,0:T(8,128)S(1)}, u32[]{:S(2)}, u32[]{:S(2)}) collective-permute-start(f32[1,2,6,24,384]{4,3,2,1,0:T(8,128)S(1)} %get-tuple-element.25), channel_id=1, source_target_pairs={{0,12},{4,0},{8,4},{12,8},{1,13},{5,1},{9,5},{13,9},{2,14},{6,2},{... | collective-permute-start | bytes 1327112 | tf_op jit(solution)/shard_map/ppermute | solution.py:358
  168.0 10.3 %collective-permute-done.8 = f32[1,2,6,24,384]{4,3,2,1,0:T(8,128)S(1)} collective-permute-done((f32[1,2,6,24,384]{4,3,2,1,0:T(8,128)S(1)}, f32[1,2,6,24,384]{4,3,2,1,0:T(8,128)S(1)}, u32[]{:S(2)}, u32[]{:S(2)}) %collective-permute-start.8) | collective-permute-done | bytes 442400 | tf_op jit(solution)/shard_map/ppermute | solution.py:358
  178.3 0.1 fusion.3
  178.5 3.1 %collective-permute-start.11 = (f32[2,2,6,24,384]{4,3,2,1,0:T(8,128)S(1)}, f32[2,2,6,24,384]{4,3,2,1,0:T(8,128)S(1)}, u32[]{:S(2)}, u32[]{:S(2)}) collective-permute-start(f32[2,2,6,24,384]{4,3,2,1,0:T(8,128)S(1)} %pad_maximum_fusion.3), channel_id=1, source_target_pairs={{0,12},{4,0},{8,4},{12,8},{1,13},{5,1},{9,5},{13,9},{2,14},{6,2},{... | collective-permute-start | bytes 2654216 | tf_op jit(solution)/shard_map/ppermute | solution.py:358
  181.7 18.1 %collective-permute-done.11 = f32[2,2,6,24,384]{4,3,2,1,0:T(8,128)S(1)} collective-permute-done((f32[2,2,6,24,384]{4,3,2,1,0:T(8,128)S(1)}, f32[2,2,6,24,384]{4,3,2,1,0:T(8,128)S(1)}, u32[]{:S(2)}, u32[]{:S(2)}) %collective-permute-start.11) | collective-permute-done | bytes 884768 | tf_op jit(solution)/shard_map/ppermute | solution.py:358
  199.8 3.6 %collective-permute-done.9 = f32[2,2,6,24,384]{4,3,2,1,0:T(8,128)S(1)} collective-permute-done((f32[2,2,6,24,384]{4,3,2,1,0:T(8,128)S(1)}, f32[2,2,6,24,384]{4,3,2,1,0:T(8,128)S(1)}, u32[]{:S(2)}, u32[]{:S(2)}) %collective-permute-start.9) | collective-permute-done | bytes 884768 | tf_op jit(solution)/shard_map/ppermute | solution.py:358
  203.5 0.1 reduce-scatter.2.cloned.1.call-done
  203.6 1.1 slice_bitcast_fusion.10
  204.7 3.3 %collective-permute-start.12 = (f32[3,24,384]{2,1,0:T(8,128)S(1)}, f32[3,24,384]{2,1,0:T(8,128)S(1)}, u32[]{:S(2)}, u32[]{:S(2)}) collective-permute-start(f32[3,24,384]{2,1,0:T(8,128)S(1)} %get-tuple-element.32), channel_id=1, source_target_pairs={{0,16},{16,32},{32,48},{48,0},{1,17},{17,33},{33,49},{49,1},{2,18}... | collective-permute-start | bytes 331784 | tf_op jit(solution)/shard_map/ppermute | solution.py:358
  208.0 1.5 collective-permute-start.14
  209.5 2.6 %collective-permute-done.12 = f32[3,24,384]{2,1,0:T(8,128)S(1)} collective-permute-done((f32[3,24,384]{2,1,0:T(8,128)S(1)}, f32[3,24,384]{2,1,0:T(8,128)S(1)}, u32[]{:S(2)}, u32[]{:S(2)}) %collective-permute-start.12) | collective-permute-done | bytes 110624 | tf_op jit(solution)/shard_map/ppermute | solution.py:358
  212.1 1.8 collective-permute-done.14
  213.9 1.0 bitcast_add_fusion.2
  214.9 0.4 collective-permute-start.15
  215.3 3.0 %collective-permute-start.13 = (f32[6,24,384]{2,1,0:T(8,128)S(1)}, f32[6,24,384]{2,1,0:T(8,128)S(1)}, u32[]{:S(2)}, u32[]{:S(2)}) collective-permute-start(f32[6,24,384]{2,1,0:T(8,128)S(1)} %pad_maximum_fusion.4), channel_id=1, source_target_pairs={{0,16},{16,32},{32,48},{48,0},{1,17},{17,33},{33,49},{49,1},{2,18}... | collective-permute-start | bytes 663560 | tf_op jit(solution)/shard_map/ppermute | solution.py:358
  218.3 1.0 copy.14
  219.3 5.7 %all-to-all-start.1 = ((f32[2,2,6,24,384]{4,3,2,0,1:T(8,128)}), f32[2,2,6,24,384]{4,3,2,0,1:T(8,128)S(1)}, u32[]{:S(2)}, u32[]{:S(2)}) async-start(f32[2,2,6,24,384]{4,3,2,0,1:T(8,128)} %copy.14), calls=%async_computation.2 | async-start | bytes 1769472 | tf_op jit(solution)/shard_map/all_to_all | solution.py:414
  225.0 1.0 fusion.4
  226.0 2.9 %collective-permute-start.16 = (f32[6,24,384]{2,1,0:T(8,128)S(1)}, f32[6,24,384]{2,1,0:T(8,128)S(1)}, u32[]{:S(2)}, u32[]{:S(2)}) collective-permute-start(f32[6,24,384]{2,1,0:T(8,128)S(1)} %fusion.4), channel_id=1, source_target_pairs={{0,0},{1,64},{4,16},{5,80},{8,32},{9,96},{12,48},{13,112},{16,4},{... | collective-permute-start | bytes 663560 | tf_op jit(solution)/shard_map/ppermute | solution.py:345
  228.9 4.6 %all-to-all-done.1 = f32[2,2,6,24,384]{4,3,2,0,1:T(8,128)S(1)} async-done(((f32[2,2,6,24,384]{4,3,2,0,1:T(8,128)}), f32[2,2,6,24,384]{4,3,2,0,1:T(8,128)S(1)}, u32[]{:S(2)}, u32[]{:S(2)}) %all-to-all-start.1) | async-done | bytes 884768 | tf_op jit(solution)/shard_map/all_to_all | solution.py:414
  233.6 1.4 reshape.39
  235.1 7.8 %collective-permute-done.16 = f32[6,24,384]{2,1,0:T(8,128)S(1)} collective-permute-done((f32[6,24,384]{2,1,0:T(8,128)S(1)}, f32[6,24,384]{2,1,0:T(8,128)S(1)}, u32[]{:S(2)}, u32[]{:S(2)}) %collective-permute-start.16) | collective-permute-done | bytes 221216 | tf_op jit(solution)/shard_map/ppermute | solution.py:345
  242.8 0.9 reshape.42
  (33 shorter events, 1.2 us)
Async XLA Ops:
  8.7 18.4 %collective-permute-start = (f32[6,24,384]{2,1,0:T(8,128)S(1)}, f32[6,24,384]{2,1,0:T(8,128)}, u32[]{:S(2)}, u32[]{:S(2)}) collective-permute-start(f32[6,24,384]{2,1,0:T(8,128)S(1)} %bitcast.73), channel_id=1, source_target_pairs={{0,0},{1,64},{4,16},{5,80},{8,32},{9,96},{12,48},{13,112},{16,4},{... | collective-permute-start | bytes 663560 | tf_op jit(solution)/shard_map/ppermute | solution.py:345
  29.1 8.4 %copy-start.3 = (s32[2]{0:T(128)S(1)}, s32[2]{0:T(128)}, u32[]{:S(2)}) copy-start(s32[2]{0:T(128)} %param.7) | copy-start | bytes 28
  29.1 55.2 %all-to-all-start = ((f32[16,6,24,384]{3,2,1,0:T(8,128)}), f32[16,6,24,384]{3,2,1,0:T(8,128)S(1)}, u32[]{:S(2)}, u32[]{:S(2)}) async-start(f32[16,6,24,384]{3,2,1,0:T(8,128)} %copy.13), calls=%async_computation | async-start | bytes 7077888 | tf_op jit(solution)/shard_map/all_to_all | solution.py:400
  36.7 85.2 %all-gather.3.cloned.1.call-start = ((), (), s32[]{:S(2)}) async-start(), calls=%async_computation.4 | async-start | bytes 3760128 | tf_op jit(solution)/shard_map/all_gather | solution.py:398
  37.4 166.2 %reduce-scatter.2.cloned.1.call-start = ((), (), s32[]{:S(2)}) async-start(), calls=%async_computation.3 | async-start | bytes 4423680 | tf_op jit(solution)/shard_map/reduce_scatter | solution.py:410
  84.5 19.1 %collective-permute-start.1 = (f32[2,2,6,24,384]{4,3,2,1,0:T(8,128)S(1)}, f32[2,2,6,24,384]{4,3,2,1,0:T(8,128)S(1)}, u32[]{:S(2)}, u32[]{:S(2)}) collective-permute-start(f32[2,2,6,24,384]{4,3,2,1,0:T(8,128)S(1)} %get-tuple-element.37), channel_id=1, source_target_pairs={{0,12},{4,0},{8,4},{12,8},{1,13},{5,1},{9,5},{13,9},{2,14},{6,2},{... | collective-permute-start | bytes 2654216 | tf_op jit(solution)/shard_map/ppermute | solution.py:358
  85.9 19.0 %collective-permute-start.2 = (f32[2,2,6,24,384]{4,3,2,1,0:T(8,128)S(1)}, f32[2,2,6,24,384]{4,3,2,1,0:T(8,128)S(1)}, u32[]{:S(2)}, u32[]{:S(2)}) collective-permute-start(f32[2,2,6,24,384]{4,3,2,1,0:T(8,128)S(1)} %get-tuple-element.37), channel_id=1, source_target_pairs={{0,4},{4,8},{8,12},{12,0},{1,5},{5,9},{9,13},{13,1},{2,6},{6,10},{... | collective-permute-start | bytes 2654216 | tf_op jit(solution)/shard_map/ppermute | solution.py:358
  105.1 16.9 %collective-permute-start.3 = (f32[3,2,2,6,24,384]{5,4,3,2,1,0:T(8,128)S(1)}, f32[3,2,2,6,24,384]{5,4,3,2,1,0:T(8,128)}, u32[]{:S(2)}, u32[]{:S(2)}) collective-permute-start(f32[3,2,2,6,24,384]{5,4,3,2,1,0:T(8,128)S(1)} %pad_maximum_fusion.own), channel_id=1, source_target_pairs={{0,1},{1,0},{2,3},{3,2},{4,5},{5,4},{6,7},{7,6},{8,9},{9,8},{10,11... | collective-permute-start | bytes 7962632 | tf_op jit(solution)/shard_map/ppermute | solution.py:349
  105.2 13.8 %collective-permute-start.4 = (f32[1,2,6,24,384]{4,3,2,1,0:T(8,128)S(1)}, f32[1,2,6,24,384]{4,3,2,1,0:T(8,128)S(1)}, u32[]{:S(2)}, u32[]{:S(2)}) collective-permute-start(f32[1,2,6,24,384]{4,3,2,1,0:T(8,128)S(1)} %slice.138), channel_id=1, source_target_pairs={{0,4},{4,8},{8,12},{12,0},{1,5},{5,9},{9,13},{13,1},{2,6},{6,10},{... | collective-permute-start | bytes 1327112 | tf_op jit(solution)/shard_map/ppermute | solution.py:358
  105.7 13.3 %collective-permute-start.5 = (f32[1,2,6,24,384]{4,3,2,1,0:T(8,128)S(1)}, f32[1,2,6,24,384]{4,3,2,1,0:T(8,128)S(1)}, u32[]{:S(2)}, u32[]{:S(2)}) collective-permute-start(f32[1,2,6,24,384]{4,3,2,1,0:T(8,128)S(1)} %slice.139), channel_id=1, source_target_pairs={{0,12},{4,0},{8,4},{12,8},{1,13},{5,1},{9,5},{13,9},{2,14},{6,2},{... | collective-permute-start | bytes 1327112 | tf_op jit(solution)/shard_map/ppermute | solution.py:358
  119.1 2.8 %collective-permute-start.6 = (f32[2,2,6,24,384]{4,3,2,1,0:T(8,128)S(1)}, f32[2,2,6,24,384]{4,3,2,1,0:T(8,128)}, u32[]{:S(2)}, u32[]{:S(2)}) collective-permute-start(f32[2,2,6,24,384]{4,3,2,1,0:T(8,128)S(1)} %constant_dynamic-update-slice_fusion.own_far), channel_id=1, source_target_pairs={{0,1},{1,0},{2,3},{3,2},{4,5},{5,4},{6,7},{7,6},{8,9},{9,8},{10,11... | collective-permute-start | bytes 2654216 | tf_op jit(solution)/shard_map/ppermute | solution.py:349
  121.9 1.1 copy-start
  123.1 1.0 copy-start.1
  157.5 6.5 %copy-start.2 = (f32[4,2,2,6,24,384]{5,4,3,2,1,0:T(8,128)S(1)}, f32[4,2,2,6,24,384]{5,4,3,2,1,0:T(8,128)}, u32[]{:S(2)}) copy-start(f32[4,2,2,6,24,384]{5,4,3,2,1,0:T(8,128)} %get-tuple-element.11) | copy-start | bytes 10616836
  157.6 6.5 %collective-permute-start.7 = (f32[4,2,2,6,24,384]{5,4,3,2,1,0:T(8,128)}, f32[4,2,2,6,24,384]{5,4,3,2,1,0:T(8,128)S(1)}, u32[]{:S(2)}, u32[]{:S(2)}) collective-permute-start(f32[4,2,2,6,24,384]{5,4,3,2,1,0:T(8,128)} %get-tuple-element.12), channel_id=1, source_target_pairs={{0,1},{1,0},{2,3},{3,2},{4,5},{5,4},{6,7},{7,6},{8,9},{9,8},{10,11... | collective-permute-start | bytes 10616840 | tf_op jit(solution)/shard_map/ppermute | solution.py:349
  164.7 13.6 %collective-permute-start.8 = (f32[1,2,6,24,384]{4,3,2,1,0:T(8,128)S(1)}, f32[1,2,6,24,384]{4,3,2,1,0:T(8,128)S(1)}, u32[]{:S(2)}, u32[]{:S(2)}) collective-permute-start(f32[1,2,6,24,384]{4,3,2,1,0:T(8,128)S(1)} %get-tuple-element.24), channel_id=1, source_target_pairs={{0,4},{4,8},{8,12},{12,0},{1,5},{5,9},{9,13},{13,1},{2,6},{6,10},{... | collective-permute-start | bytes 1327112 | tf_op jit(solution)/shard_map/ppermute | solution.py:358
  164.8 13.5 %collective-permute-start.10 = (f32[1,2,6,24,384]{4,3,2,1,0:T(8,128)S(1)}, f32[1,2,6,24,384]{4,3,2,1,0:T(8,128)S(1)}, u32[]{:S(2)}, u32[]{:S(2)}) collective-permute-start(f32[1,2,6,24,384]{4,3,2,1,0:T(8,128)S(1)} %get-tuple-element.25), channel_id=1, source_target_pairs={{0,12},{4,0},{8,4},{12,8},{1,13},{5,1},{9,5},{13,9},{2,14},{6,2},{... | collective-permute-start | bytes 1327112 | tf_op jit(solution)/shard_map/ppermute | solution.py:358
  178.5 21.3 %collective-permute-start.11 = (f32[2,2,6,24,384]{4,3,2,1,0:T(8,128)S(1)}, f32[2,2,6,24,384]{4,3,2,1,0:T(8,128)S(1)}, u32[]{:S(2)}, u32[]{:S(2)}) collective-permute-start(f32[2,2,6,24,384]{4,3,2,1,0:T(8,128)S(1)} %pad_maximum_fusion.3), channel_id=1, source_target_pairs={{0,12},{4,0},{8,4},{12,8},{1,13},{5,1},{9,5},{13,9},{2,14},{6,2},{... | collective-permute-start | bytes 2654216 | tf_op jit(solution)/shard_map/ppermute | solution.py:358
  181.6 21.7 %collective-permute-start.9 = (f32[2,2,6,24,384]{4,3,2,1,0:T(8,128)S(1)}, f32[2,2,6,24,384]{4,3,2,1,0:T(8,128)S(1)}, u32[]{:S(2)}, u32[]{:S(2)}) collective-permute-start(f32[2,2,6,24,384]{4,3,2,1,0:T(8,128)S(1)} %pad_maximum_fusion.2), channel_id=1, source_target_pairs={{0,4},{4,8},{8,12},{12,0},{1,5},{5,9},{9,13},{13,1},{2,6},{6,10},{... | collective-permute-start | bytes 2654216 | tf_op jit(solution)/shard_map/ppermute | solution.py:358
  204.7 7.4 %collective-permute-start.12 = (f32[3,24,384]{2,1,0:T(8,128)S(1)}, f32[3,24,384]{2,1,0:T(8,128)S(1)}, u32[]{:S(2)}, u32[]{:S(2)}) collective-permute-start(f32[3,24,384]{2,1,0:T(8,128)S(1)} %get-tuple-element.32), channel_id=1, source_target_pairs={{0,16},{16,32},{32,48},{48,0},{1,17},{17,33},{33,49},{49,1},{2,18}... | collective-permute-start | bytes 331784 | tf_op jit(solution)/shard_map/ppermute | solution.py:358
  208.0 6.0 %collective-permute-start.14 = (f32[3,24,384]{2,1,0:T(8,128)S(1)}, f32[3,24,384]{2,1,0:T(8,128)S(1)}, u32[]{:S(2)}, u32[]{:S(2)}) collective-permute-start(f32[3,24,384]{2,1,0:T(8,128)S(1)} %get-tuple-element.33), channel_id=1, source_target_pairs={{0,48},{16,0},{32,16},{48,32},{1,49},{17,1},{33,17},{49,33},{2,50}... | collective-permute-start | bytes 331784 | tf_op jit(solution)/shard_map/ppermute | solution.py:358
  214.9 10.1 %collective-permute-start.15 = (f32[6,24,384]{2,1,0:T(8,128)S(1)}, f32[6,24,384]{2,1,0:T(8,128)S(1)}, u32[]{:S(2)}, u32[]{:S(2)}) collective-permute-start(f32[6,24,384]{2,1,0:T(8,128)S(1)} %pad_maximum_fusion.5), channel_id=1, source_target_pairs={{0,48},{16,0},{32,16},{48,32},{1,49},{17,1},{33,17},{49,33},{2,50}... | collective-permute-start | bytes 663560 | tf_op jit(solution)/shard_map/ppermute | solution.py:358
  215.3 9.7 %collective-permute-start.13 = (f32[6,24,384]{2,1,0:T(8,128)S(1)}, f32[6,24,384]{2,1,0:T(8,128)S(1)}, u32[]{:S(2)}, u32[]{:S(2)}) collective-permute-start(f32[6,24,384]{2,1,0:T(8,128)S(1)} %pad_maximum_fusion.4), channel_id=1, source_target_pairs={{0,16},{16,32},{32,48},{48,0},{1,17},{17,33},{33,49},{49,1},{2,18}... | collective-permute-start | bytes 663560 | tf_op jit(solution)/shard_map/ppermute | solution.py:358
  219.3 14.3 %all-to-all-start.1 = ((f32[2,2,6,24,384]{4,3,2,0,1:T(8,128)}), f32[2,2,6,24,384]{4,3,2,0,1:T(8,128)S(1)}, u32[]{:S(2)}, u32[]{:S(2)}) async-start(f32[2,2,6,24,384]{4,3,2,0,1:T(8,128)} %copy.14), calls=%async_computation.2 | async-start | bytes 1769472 | tf_op jit(solution)/shard_map/all_to_all | solution.py:414
  226.0 16.8 %collective-permute-start.16 = (f32[6,24,384]{2,1,0:T(8,128)S(1)}, f32[6,24,384]{2,1,0:T(8,128)S(1)}, u32[]{:S(2)}, u32[]{:S(2)}) collective-permute-start(f32[6,24,384]{2,1,0:T(8,128)S(1)} %fusion.4), channel_id=1, source_target_pairs={{0,0},{1,64},{4,16},{5,80},{8,32},{9,96},{12,48},{13,112},{16,4},{... | collective-permute-start | bytes 663560 | tf_op jit(solution)/shard_map/ppermute | solution.py:345
Sparse Core Ops, SparseCore 0:
  39.7 71.9 all-gather.2
  157.7 45.8 reduce-scatter.1

commit v5 on v4

--- a/solution.py
+++ b/solution.py
@@ -410,7 +410,7 @@
     local = lax.psum_scatter(local, ("x_hi", "x_lo"), scatter_dimension=0)
     total = scatter_ring(keep + other_core(send), "z")
     total, local = lax.optimization_barrier((total, local))
-    local = scatter_ring(local, "y")
+    local = local[0] + sum(shifted(local[k], "y", k) for k in (1, 2, 3))
     total = lax.all_to_all(total, "x_hi", 1, 1, tiled=True)
     local = turn(local)
     return (

time: 251 us -> 250 us (level)
  waiting for transfers between devices: 140 us -> 136 us
    ppermute x2, waiting for transfers between devices: 17.9 us -> 23.8 us  [turn(): return lax.ppermute(value, TURN_AXES, pairs)]
    all_to_all x1, waiting for transfers between devices: 4.63 us -> 0.01 us  [per_device(): total = lax.all_to_all(total, 'x_hi', 1, 1, tiled=True)]
    ppermute x12 -> x11, waiting for transfers between devices: 65.1 us -> 60.6 us  [shifted(): lax.ppermute(value, axis, [(ring[i], ring[(i + step) % 4]) for i in range...]
    ppermute x12 -> x11, starting transfers between devices: 20.1 us -> 19.3 us  [shifted(): lax.ppermute(value, axis, [(ring[i], ring[(i + step) % 4]) for i in range...]
  transfers between devices with their start and end apart: 21 -> 20, of which waited for: 15 -> 12; matrix products, arithmetic and copies ran while one was open for 3% -> 3% of each run, Pallas kernels for 0% -> 0%
where the time goes in v5:
time: 250 us; the launch traced here: 248 us
  waiting for transfers between devices  136 us (54%)
  starting transfers between devices  44.2 us (18%)
  Pallas kernels  33.5 us (13%)
  between operations  18.1 us (7%)
  local copies, waits for them, and re-layouts  12.3 us (5%)
  other arithmetic  3.7 us (1%)
    ppermute x11, waiting for transfers between devices, shifted(): lax.ppermute(value, axis, [(ring[i], ring[(i + step) % 4]) for i in range...  60.6 us
    all_to_all x1, waiting for transfers between devices, per_device(): blocks = lax.all_to_all(blocks, ('x_lo', 'y', 'x_hi'), 0, 0, tiled=True)  42.4 us
    pallas_call x1, Pallas kernels, solve(): pl.pallas_call(field_kernel, grid_spec=pltpu.PrefetchScalarGridSpec(num_s...  33.5 us
    ppermute x2, waiting for transfers between devices, turn(): return lax.ppermute(value, TURN_AXES, pairs)  23.8 us
    ppermute x11, starting transfers between devices, shifted(): lax.ppermute(value, axis, [(ring[i], ring[(i + step) % 4]) for i in range...  19.3 us
    ppermute x2, starting transfers between devices, turn(): return lax.ppermute(value, TURN_AXES, pairs)  9.11 us
    ppermute x3, waiting for transfers between devices, other_core(): return lax.ppermute(value, 'core', [(0, 1), (1, 0)])  8.76 us
    all_to_all x1, starting transfers between devices, per_device(): blocks = lax.all_to_all(blocks, ('x_lo', 'y', 'x_hi'), 0, 0, tiled=True)  7.61 us
  transfers between devices with their start and end apart: 20, of which 12 were waited for; matrix products, arithmetic and copies ran while one was open for 3% of the time, Pallas kernels for 0%

profile of v5, /device:TPU:28, one launch (start us, length us, event | category | flops | bytes accessed | tf_op | source)
XLA Modules:
  0.0 248.2 jit_solution(8504802833233998434)
XLA Ops:
  7.2 1.5 reduce
  8.7 5.6 %collective-permute-start = (f32[6,24,384]{2,1,0:T(8,128)S(1)}, f32[6,24,384]{2,1,0:T(8,128)}, u32[]{:S(2)}, u32[]{:S(2)}) collective-permute-start(f32[6,24,384]{2,1,0:T(8,128)S(1)} %bitcast.64), channel_id=1, source_target_pairs={{0,0},{1,64},{4,16},{5,80},{8,32},{9,96},{12,48},{13,112},{16,4},{... | collective-permute-start | bytes 663560 | tf_op jit(solution)/shard_map/ppermute | solution.py:345
  14.3 2.6 %copy.18 = f32[12,8,24,384]{3,2,1,0:T(8,128)S(1)} copy(f32[12,8,24,384]{3,1,2,0:T(8,128)} %bitcast.58) | data formatting | bytes 7077888
  16.9 10.1 %collective-permute-done = f32[6,24,384]{2,1,0:T(8,128)} collective-permute-done((f32[6,24,384]{2,1,0:T(8,128)S(1)}, f32[6,24,384]{2,1,0:T(8,128)}, u32[]{:S(2)}, u32[]{:S(2)}) %collective-permute-start) | collective-permute-done | bytes 221216 | tf_op jit(solution)/shard_map/ppermute | solution.py:345
  27.0 2.0 copy.13
  29.1 7.6 %all-to-all-start = ((f32[16,6,24,384]{3,2,1,0:T(8,128)}), f32[16,6,24,384]{3,2,1,0:T(8,128)S(1)}, u32[]{:S(2)}, u32[]{:S(2)}) async-start(f32[16,6,24,384]{3,2,1,0:T(8,128)} %copy.13), calls=%async_computation | async-start | bytes 7077888 | tf_op jit(solution)/shard_map/all_to_all | solution.py:400
  36.7 0.7 all-gather.3.cloned.1.call-update
  37.5 0.6 fusion.5
  42.0 42.4 %all-to-all-done = f32[16,6,24,384]{3,2,1,0:T(8,128)S(1)} async-done(((f32[16,6,24,384]{3,2,1,0:T(8,128)}), f32[16,6,24,384]{3,2,1,0:T(8,128)S(1)}, u32[]{:S(2)}, u32[]{:S(2)}) %all-to-all-start) | async-done | bytes 3538976 | tf_op jit(solution)/shard_map/all_to_all | solution.py:400
  84.4 0.1 fusion.4
  84.5 1.4 collective-permute-start.1
  85.9 0.7 collective-permute-start.2
  86.6 17.0 %collective-permute-done.1 = f32[2,2,6,24,384]{4,3,2,1,0:T(8,128)S(1)} collective-permute-done((f32[2,2,6,24,384]{4,3,2,1,0:T(8,128)S(1)}, f32[2,2,6,24,384]{4,3,2,1,0:T(8,128)S(1)}, u32[]{:S(2)}, u32[]{:S(2)}) %collective-permute-start.1) | collective-permute-done | bytes 884768 | tf_op jit(solution)/shard_map/ppermute | solution.py:358
  103.6 1.3 collective-permute-done.2
  104.9 0.2 pad_maximum_fusion.own
  105.0 0.1 collective-permute-start.3
  105.2 0.5 collective-permute-start.4
  105.7 2.9 %collective-permute-start.5 = (f32[1,2,6,24,384]{4,3,2,1,0:T(8,128)S(1)}, f32[1,2,6,24,384]{4,3,2,1,0:T(8,128)S(1)}, u32[]{:S(2)}, u32[]{:S(2)}) collective-permute-start(f32[1,2,6,24,384]{4,3,2,1,0:T(8,128)S(1)} %slice.94), channel_id=1, source_target_pairs={{0,12},{4,0},{8,4},{12,8},{1,13},{5,1},{9,5},{13,9},{2,14},{6,2},{... | collective-permute-start | bytes 1327112 | tf_op jit(solution)/shard_map/ppermute | solution.py:358
  108.6 10.4 %collective-permute-done.4 = f32[1,2,6,24,384]{4,3,2,1,0:T(8,128)S(1)} collective-permute-done((f32[1,2,6,24,384]{4,3,2,1,0:T(8,128)S(1)}, f32[1,2,6,24,384]{4,3,2,1,0:T(8,128)S(1)}, u32[]{:S(2)}, u32[]{:S(2)}) %collective-permute-start.4) | collective-permute-done | bytes 442400 | tf_op jit(solution)/shard_map/ppermute | solution.py:358
  119.1 0.3 collective-permute-start.6
  119.5 2.5 collective-permute-done.6.other_far
  121.9 1.1 copy-done
  123.1 1.0 copy-done.1
  124.1 33.5 %shard_map.68 = (f32[4,2,2,6,24,384]{5,4,3,2,1,0:T(8,128)}, f32[4,2,2,6,24,384]{5,4,3,2,1,0:T(8,128)}, f32[4,4,6,24,384]{4,3,2,1,0:T(8,128)}) custom-call(s32[3]{0:T(128)S(1)} %pad_add_fusion.ids, f32[4,4,6,24,384]{4,3,2,1,0:T(8,128)} %bitcast.65, f32[3,2,2,6,24,384]{5,4,3,2,1,0:T(8,128)S(1)} %pad_maximum_fusion.own, ...), custom_call_target="tpu_custom_call" | custom-call | flops 12230590464 | bytes 35000000 | tf_op jit(solution)/shard_map/pallas_call | solution.py:304
  157.6 0.2 collective-permute-start.7
  157.8 6.3 %collective-permute-done.7 = f32[4,2,2,6,24,384]{5,4,3,2,1,0:T(8,128)S(1)} collective-permute-done((f32[4,2,2,6,24,384]{5,4,3,2,1,0:T(8,128)}, f32[4,2,2,6,24,384]{5,4,3,2,1,0:T(8,128)S(1)}, u32[]{:S(2)}, u32[]{:S(2)}) %collective-permute-start.7) | collective-permute-done | bytes 3538976 | tf_op jit(solution)/shard_map/ppermute | solution.py:349
  164.1 0.5 add.35
  164.6 0.1 slice_bitcast_fusion.5
  164.8 3.2 %collective-permute-start.10 = (f32[1,2,6,24,384]{4,3,2,1,0:T(8,128)S(1)}, f32[1,2,6,24,384]{4,3,2,1,0:T(8,128)S(1)}, u32[]{:S(2)}, u32[]{:S(2)}) collective-permute-start(f32[1,2,6,24,384]{4,3,2,1,0:T(8,128)S(1)} %get-tuple-element.25), channel_id=1, source_target_pairs={{0,12},{4,0},{8,4},{12,8},{1,13},{5,1},{9,5},{13,9},{2,14},{6,2},{... | collective-permute-start | bytes 1327112 | tf_op jit(solution)/shard_map/ppermute | solution.py:358
  168.0 10.2 %collective-permute-done.8 = f32[1,2,6,24,384]{4,3,2,1,0:T(8,128)S(1)} collective-permute-done((f32[1,2,6,24,384]{4,3,2,1,0:T(8,128)S(1)}, f32[1,2,6,24,384]{4,3,2,1,0:T(8,128)S(1)}, u32[]{:S(2)}, u32[]{:S(2)}) %collective-permute-start.8) | collective-permute-done | bytes 442400 | tf_op jit(solution)/shard_map/ppermute | solution.py:358
  178.3 0.1 fusion.3
  178.4 3.1 %collective-permute-start.11 = (f32[2,2,6,24,384]{4,3,2,1,0:T(8,128)S(1)}, f32[2,2,6,24,384]{4,3,2,1,0:T(8,128)S(1)}, u32[]{:S(2)}, u32[]{:S(2)}) collective-permute-start(f32[2,2,6,24,384]{4,3,2,1,0:T(8,128)S(1)} %pad_maximum_fusion.3), channel_id=1, source_target_pairs={{0,12},{4,0},{8,4},{12,8},{1,13},{5,1},{9,5},{13,9},{2,14},{6,2},{... | collective-permute-start | bytes 2654216 | tf_op jit(solution)/shard_map/ppermute | solution.py:358
  181.5 0.1 pad_maximum_fusion.2
  181.7 18.0 %collective-permute-done.11 = f32[2,2,6,24,384]{4,3,2,1,0:T(8,128)S(1)} collective-permute-done((f32[2,2,6,24,384]{4,3,2,1,0:T(8,128)S(1)}, f32[2,2,6,24,384]{4,3,2,1,0:T(8,128)S(1)}, u32[]{:S(2)}, u32[]{:S(2)}) %collective-permute-start.11) | collective-permute-done | bytes 884768 | tf_op jit(solution)/shard_map/ppermute | solution.py:358
  199.7 3.6 %collective-permute-done.9 = f32[2,2,6,24,384]{4,3,2,1,0:T(8,128)S(1)} collective-permute-done((f32[2,2,6,24,384]{4,3,2,1,0:T(8,128)S(1)}, f32[2,2,6,24,384]{4,3,2,1,0:T(8,128)S(1)}, u32[]{:S(2)}, u32[]{:S(2)}) %collective-permute-start.9) | collective-permute-done | bytes 884768 | tf_op jit(solution)/shard_map/ppermute | solution.py:358
  203.3 0.1 fusion.1
  203.4 0.2 reduce-scatter.2.cloned.1.call-done
  203.6 1.2 slice_bitcast_fusion.8
  204.8 3.9 %collective-permute-start.13 = (f32[6,24,384]{2,1,0:T(8,128)S(1)}, f32[6,24,384]{2,1,0:T(8,128)S(1)}, u32[]{:S(2)}, u32[]{:S(2)}) collective-permute-start(f32[6,24,384]{2,1,0:T(8,128)S(1)} %get-tuple-element.30), channel_id=1, source_target_pairs={{0,32},{16,48},{32,0},{48,16},{1,33},{17,49},{33,1},{49,17},{2,34}... | collective-permute-start | bytes 663560 | tf_op jit(solution)/shard_map/ppermute | solution.py:358
  208.7 0.9 collective-permute-start.14
  209.6 2.6 %collective-permute-start.12 = (f32[6,24,384]{2,1,0:T(8,128)S(1)}, f32[6,24,384]{2,1,0:T(8,128)S(1)}, u32[]{:S(2)}, u32[]{:S(2)}) collective-permute-start(f32[6,24,384]{2,1,0:T(8,128)S(1)} %get-tuple-element.32), channel_id=1, source_target_pairs={{0,16},{16,32},{32,48},{48,0},{1,17},{17,33},{33,49},{49,1},{2,18}... | collective-permute-start | bytes 663560 | tf_op jit(solution)/shard_map/ppermute | solution.py:358
  212.2 1.0 copy.14
  213.2 7.5 %all-to-all-start.1 = ((f32[2,2,6,24,384]{4,3,2,0,1:T(8,128)}), f32[2,2,6,24,384]{4,3,2,0,1:T(8,128)S(1)}, u32[]{:S(2)}, u32[]{:S(2)}) async-start(f32[2,2,6,24,384]{4,3,2,0,1:T(8,128)} %copy.14), calls=%async_computation.2 | async-start | bytes 1769472 | tf_op jit(solution)/shard_map/all_to_all | solution.py:414
  220.7 1.0 bitcast_add_fusion
  221.7 3.5 %collective-permute-start.15 = (f32[6,24,384]{2,1,0:T(8,128)S(1)}, f32[6,24,384]{2,1,0:T(8,128)S(1)}, u32[]{:S(2)}, u32[]{:S(2)}) collective-permute-start(f32[6,24,384]{2,1,0:T(8,128)S(1)} %bitcast_add_fusion), channel_id=1, source_target_pairs={{0,0},{1,64},{4,16},{5,80},{8,32},{9,96},{12,48},{13,112},{16,4},{... | collective-permute-start | bytes 663560 | tf_op jit(solution)/shard_map/ppermute | solution.py:345
  225.2 13.7 %collective-permute-done.15 = f32[6,24,384]{2,1,0:T(8,128)S(1)} collective-permute-done((f32[6,24,384]{2,1,0:T(8,128)S(1)}, f32[6,24,384]{2,1,0:T(8,128)S(1)}, u32[]{:S(2)}, u32[]{:S(2)}) %collective-permute-start.15) | collective-permute-done | bytes 221216 | tf_op jit(solution)/shard_map/ppermute | solution.py:345
  238.9 0.9 reshape.36
  239.9 1.4 reshape.33
  (28 shorter events, 0.7 us)
Async XLA Ops:
  8.7 18.4 %collective-permute-start = (f32[6,24,384]{2,1,0:T(8,128)S(1)}, f32[6,24,384]{2,1,0:T(8,128)}, u32[]{:S(2)}, u32[]{:S(2)}) collective-permute-start(f32[6,24,384]{2,1,0:T(8,128)S(1)} %bitcast.64), channel_id=1, source_target_pairs={{0,0},{1,64},{4,16},{5,80},{8,32},{9,96},{12,48},{13,112},{16,4},{... | collective-permute-start | bytes 663560 | tf_op jit(solution)/shard_map/ppermute | solution.py:345
  29.1 8.4 %copy-start.3 = (s32[2]{0:T(128)S(1)}, s32[2]{0:T(128)}, u32[]{:S(2)}) copy-start(s32[2]{0:T(128)} %param.7) | copy-start | bytes 28
  29.1 55.2 %all-to-all-start = ((f32[16,6,24,384]{3,2,1,0:T(8,128)}), f32[16,6,24,384]{3,2,1,0:T(8,128)S(1)}, u32[]{:S(2)}, u32[]{:S(2)}) async-start(f32[16,6,24,384]{3,2,1,0:T(8,128)} %copy.13), calls=%async_computation | async-start | bytes 7077888 | tf_op jit(solution)/shard_map/all_to_all | solution.py:400
  36.7 85.2 %all-gather.3.cloned.1.call-start = ((), (), s32[]{:S(2)}) async-start(), calls=%async_computation.4 | async-start | bytes 3760128 | tf_op jit(solution)/shard_map/all_gather | solution.py:398
  37.4 166.2 %reduce-scatter.2.cloned.1.call-start = ((), (), s32[]{:S(2)}) async-start(), calls=%async_computation.3 | async-start | bytes 4423680 | tf_op jit(solution)/shard_map/reduce_scatter | solution.py:410
  84.5 19.1 %collective-permute-start.1 = (f32[2,2,6,24,384]{4,3,2,1,0:T(8,128)S(1)}, f32[2,2,6,24,384]{4,3,2,1,0:T(8,128)S(1)}, u32[]{:S(2)}, u32[]{:S(2)}) collective-permute-start(f32[2,2,6,24,384]{4,3,2,1,0:T(8,128)S(1)} %get-tuple-element.34), channel_id=1, source_target_pairs={{0,12},{4,0},{8,4},{12,8},{1,13},{5,1},{9,5},{13,9},{2,14},{6,2},{... | collective-permute-start | bytes 2654216 | tf_op jit(solution)/shard_map/ppermute | solution.py:358
  85.9 19.0 %collective-permute-start.2 = (f32[2,2,6,24,384]{4,3,2,1,0:T(8,128)S(1)}, f32[2,2,6,24,384]{4,3,2,1,0:T(8,128)S(1)}, u32[]{:S(2)}, u32[]{:S(2)}) collective-permute-start(f32[2,2,6,24,384]{4,3,2,1,0:T(8,128)S(1)} %get-tuple-element.34), channel_id=1, source_target_pairs={{0,4},{4,8},{8,12},{12,0},{1,5},{5,9},{9,13},{13,1},{2,6},{6,10},{... | collective-permute-start | bytes 2654216 | tf_op jit(solution)/shard_map/ppermute | solution.py:358
  105.0 16.9 %collective-permute-start.3 = (f32[3,2,2,6,24,384]{5,4,3,2,1,0:T(8,128)S(1)}, f32[3,2,2,6,24,384]{5,4,3,2,1,0:T(8,128)}, u32[]{:S(2)}, u32[]{:S(2)}) collective-permute-start(f32[3,2,2,6,24,384]{5,4,3,2,1,0:T(8,128)S(1)} %pad_maximum_fusion.own), channel_id=1, source_target_pairs={{0,1},{1,0},{2,3},{3,2},{4,5},{5,4},{6,7},{7,6},{8,9},{9,8},{10,11... | collective-permute-start | bytes 7962632 | tf_op jit(solution)/shard_map/ppermute | solution.py:349
  105.2 13.8 %collective-permute-start.4 = (f32[1,2,6,24,384]{4,3,2,1,0:T(8,128)S(1)}, f32[1,2,6,24,384]{4,3,2,1,0:T(8,128)S(1)}, u32[]{:S(2)}, u32[]{:S(2)}) collective-permute-start(f32[1,2,6,24,384]{4,3,2,1,0:T(8,128)S(1)} %slice.93), channel_id=1, source_target_pairs={{0,4},{4,8},{8,12},{12,0},{1,5},{5,9},{9,13},{13,1},{2,6},{6,10},{... | collective-permute-start | bytes 1327112 | tf_op jit(solution)/shard_map/ppermute | solution.py:358
  105.7 13.3 %collective-permute-start.5 = (f32[1,2,6,24,384]{4,3,2,1,0:T(8,128)S(1)}, f32[1,2,6,24,384]{4,3,2,1,0:T(8,128)S(1)}, u32[]{:S(2)}, u32[]{:S(2)}) collective-permute-start(f32[1,2,6,24,384]{4,3,2,1,0:T(8,128)S(1)} %slice.94), channel_id=1, source_target_pairs={{0,12},{4,0},{8,4},{12,8},{1,13},{5,1},{9,5},{13,9},{2,14},{6,2},{... | collective-permute-start | bytes 1327112 | tf_op jit(solution)/shard_map/ppermute | solution.py:358
  119.1 2.8 %collective-permute-start.6 = (f32[2,2,6,24,384]{4,3,2,1,0:T(8,128)S(1)}, f32[2,2,6,24,384]{4,3,2,1,0:T(8,128)}, u32[]{:S(2)}, u32[]{:S(2)}) collective-permute-start(f32[2,2,6,24,384]{4,3,2,1,0:T(8,128)S(1)} %constant_dynamic-update-slice_fusion.own_far), channel_id=1, source_target_pairs={{0,1},{1,0},{2,3},{3,2},{4,5},{5,4},{6,7},{7,6},{8,9},{9,8},{10,11... | collective-permute-start | bytes 2654216 | tf_op jit(solution)/shard_map/ppermute | solution.py:349
  121.9 1.1 copy-start
  123.1 1.0 copy-start.1
  157.6 6.5 %copy-start.2 = (f32[4,2,2,6,24,384]{5,4,3,2,1,0:T(8,128)S(1)}, f32[4,2,2,6,24,384]{5,4,3,2,1,0:T(8,128)}, u32[]{:S(2)}) copy-start(f32[4,2,2,6,24,384]{5,4,3,2,1,0:T(8,128)} %get-tuple-element.11) | copy-start | bytes 10616836
  157.6 6.5 %collective-permute-start.7 = (f32[4,2,2,6,24,384]{5,4,3,2,1,0:T(8,128)}, f32[4,2,2,6,24,384]{5,4,3,2,1,0:T(8,128)S(1)}, u32[]{:S(2)}, u32[]{:S(2)}) collective-permute-start(f32[4,2,2,6,24,384]{5,4,3,2,1,0:T(8,128)} %get-tuple-element.12), channel_id=1, source_target_pairs={{0,1},{1,0},{2,3},{3,2},{4,5},{5,4},{6,7},{7,6},{8,9},{9,8},{10,11... | collective-permute-start | bytes 10616840 | tf_op jit(solution)/shard_map/ppermute | solution.py:349
  164.7 13.5 %collective-permute-start.8 = (f32[1,2,6,24,384]{4,3,2,1,0:T(8,128)S(1)}, f32[1,2,6,24,384]{4,3,2,1,0:T(8,128)S(1)}, u32[]{:S(2)}, u32[]{:S(2)}) collective-permute-start(f32[1,2,6,24,384]{4,3,2,1,0:T(8,128)S(1)} %get-tuple-element.24), channel_id=1, source_target_pairs={{0,4},{4,8},{8,12},{12,0},{1,5},{5,9},{9,13},{13,1},{2,6},{6,10},{... | collective-permute-start | bytes 1327112 | tf_op jit(solution)/shard_map/ppermute | solution.py:358
  164.8 13.5 %collective-permute-start.10 = (f32[1,2,6,24,384]{4,3,2,1,0:T(8,128)S(1)}, f32[1,2,6,24,384]{4,3,2,1,0:T(8,128)S(1)}, u32[]{:S(2)}, u32[]{:S(2)}) collective-permute-start(f32[1,2,6,24,384]{4,3,2,1,0:T(8,128)S(1)} %get-tuple-element.25), channel_id=1, source_target_pairs={{0,12},{4,0},{8,4},{12,8},{1,13},{5,1},{9,5},{13,9},{2,14},{6,2},{... | collective-permute-start | bytes 1327112 | tf_op jit(solution)/shard_map/ppermute | solution.py:358
  178.4 21.3 %collective-permute-start.11 = (f32[2,2,6,24,384]{4,3,2,1,0:T(8,128)S(1)}, f32[2,2,6,24,384]{4,3,2,1,0:T(8,128)S(1)}, u32[]{:S(2)}, u32[]{:S(2)}) collective-permute-start(f32[2,2,6,24,384]{4,3,2,1,0:T(8,128)S(1)} %pad_maximum_fusion.3), channel_id=1, source_target_pairs={{0,12},{4,0},{8,4},{12,8},{1,13},{5,1},{9,5},{13,9},{2,14},{6,2},{... | collective-permute-start | bytes 2654216 | tf_op jit(solution)/shard_map/ppermute | solution.py:358
  181.6 21.7 %collective-permute-start.9 = (f32[2,2,6,24,384]{4,3,2,1,0:T(8,128)S(1)}, f32[2,2,6,24,384]{4,3,2,1,0:T(8,128)S(1)}, u32[]{:S(2)}, u32[]{:S(2)}) collective-permute-start(f32[2,2,6,24,384]{4,3,2,1,0:T(8,128)S(1)} %pad_maximum_fusion.2), channel_id=1, source_target_pairs={{0,4},{4,8},{8,12},{12,0},{1,5},{5,9},{9,13},{13,1},{2,6},{6,10},{... | collective-permute-start | bytes 2654216 | tf_op jit(solution)/shard_map/ppermute | solution.py:358
  204.8 15.9 %collective-permute-start.13 = (f32[6,24,384]{2,1,0:T(8,128)S(1)}, f32[6,24,384]{2,1,0:T(8,128)S(1)}, u32[]{:S(2)}, u32[]{:S(2)}) collective-permute-start(f32[6,24,384]{2,1,0:T(8,128)S(1)} %get-tuple-element.30), channel_id=1, source_target_pairs={{0,32},{16,48},{32,0},{48,16},{1,33},{17,49},{33,1},{49,17},{2,34}... | collective-permute-start | bytes 663560 | tf_op jit(solution)/shard_map/ppermute | solution.py:358
  208.7 12.0 %collective-permute-start.14 = (f32[6,24,384]{2,1,0:T(8,128)S(1)}, f32[6,24,384]{2,1,0:T(8,128)S(1)}, u32[]{:S(2)}, u32[]{:S(2)}) collective-permute-start(f32[6,24,384]{2,1,0:T(8,128)S(1)} %get-tuple-element.31), channel_id=1, source_target_pairs={{0,48},{16,0},{32,16},{48,32},{1,49},{17,1},{33,17},{49,33},{2,50}... | collective-permute-start | bytes 663560 | tf_op jit(solution)/shard_map/ppermute | solution.py:358
  209.6 11.1 %collective-permute-start.12 = (f32[6,24,384]{2,1,0:T(8,128)S(1)}, f32[6,24,384]{2,1,0:T(8,128)S(1)}, u32[]{:S(2)}, u32[]{:S(2)}) collective-permute-start(f32[6,24,384]{2,1,0:T(8,128)S(1)} %get-tuple-element.32), channel_id=1, source_target_pairs={{0,16},{16,32},{32,48},{48,0},{1,17},{17,33},{33,49},{49,1},{2,18}... | collective-permute-start | bytes 663560 | tf_op jit(solution)/shard_map/ppermute | solution.py:358
  213.2 26.7 %all-to-all-start.1 = ((f32[2,2,6,24,384]{4,3,2,0,1:T(8,128)}), f32[2,2,6,24,384]{4,3,2,0,1:T(8,128)S(1)}, u32[]{:S(2)}, u32[]{:S(2)}) async-start(f32[2,2,6,24,384]{4,3,2,0,1:T(8,128)} %copy.14), calls=%async_computation.2 | async-start | bytes 1769472 | tf_op jit(solution)/shard_map/all_to_all | solution.py:414
  221.7 17.2 %collective-permute-start.15 = (f32[6,24,384]{2,1,0:T(8,128)S(1)}, f32[6,24,384]{2,1,0:T(8,128)S(1)}, u32[]{:S(2)}, u32[]{:S(2)}) collective-permute-start(f32[6,24,384]{2,1,0:T(8,128)S(1)} %bitcast_add_fusion), channel_id=1, source_target_pairs={{0,0},{1,64},{4,16},{5,80},{8,32},{9,96},{12,48},{13,112},{16,4},{... | collective-permute-start | bytes 663560 | tf_op jit(solution)/shard_map/ppermute | solution.py:345
Sparse Core Ops, SparseCore 0:
  39.7 71.9 all-gather.2
  157.7 45.8 reduce-scatter.1

commit v6 on v5

--- a/solution.py
+++ b/solution.py
@@ -411,7 +411,13 @@
     total = scatter_ring(keep + other_core(send), "z")
     total, local = lax.optimization_barrier((total, local))
     local = local[0] + sum(shifted(local[k], "y", k) for k in (1, 2, 3))
-    total = lax.all_to_all(total, "x_hi", 1, 1, tiled=True)
+    half = lax.axis_index("x_hi")
+    mine = lax.dynamic_index_in_dim(total, half, 1)
+    theirs = lax.dynamic_index_in_dim(total, 1 - half, 1)
+    theirs = lax.ppermute(theirs, "x_hi", [(0, 1), (1, 0)])
+    total = jnp.concatenate(
+        [jnp.where(half == 0, mine, theirs), jnp.where(half == 0, theirs, mine)], axis=1
+    )
     local = turn(local)
     return (
         local.reshape(1, planes, N * N),

time: 250 us -> 250 us (level)
  waiting for transfers between devices: 136 us -> 141 us
  starting transfers between devices: 44.2 us -> 41 us
    all_to_all x1 -> x0, starting transfers between devices: 7.52 us -> none  [per_device(): total = lax.all_to_all(total, 'x_hi', 1, 1, tiled=True)]
    ppermute x0 -> x1, starting transfers between devices: none -> 4.06 us  [per_device(): theirs = lax.ppermute(theirs, 'x_hi', [(0, 1), (1, 0)])]
    ppermute x11, waiting for transfers between devices: 60.6 us -> 64.6 us  [shifted(): lax.ppermute(value, axis, [(ring[i], ring[(i + step) % 4]) for i in range...]
  transfers between devices with their start and end apart: 20 -> 20, of which waited for: 12 -> 14; matrix products, arithmetic and copies ran while one was open for 3% -> 3% of each run, Pallas kernels for 0% -> 0%
where the time goes in v6:
time: 250 us; the launch traced here: 248 us
  waiting for transfers between devices  141 us (56%)
  starting transfers between devices  41 us (16%)
  Pallas kernels  33.5 us (13%)
  between operations  18.1 us (7%)
  local copies, waits for them, and re-layouts  11.4 us (5%)
  other arithmetic  3.79 us (2%)
    ppermute x11, waiting for transfers between devices, shifted(): lax.ppermute(value, axis, [(ring[i], ring[(i + step) % 4]) for i in range...  64.6 us
    all_to_all x1, waiting for transfers between devices, per_device(): blocks = lax.all_to_all(blocks, ('x_lo', 'y', 'x_hi'), 0, 0, tiled=True)  42.4 us
    pallas_call x1, Pallas kernels, solve(): pl.pallas_call(field_kernel, grid_spec=pltpu.PrefetchScalarGridSpec(num_s...  33.5 us
    ppermute x2, waiting for transfers between devices, turn(): return lax.ppermute(value, TURN_AXES, pairs)  23.6 us
    ppermute x11, starting transfers between devices, shifted(): lax.ppermute(value, axis, [(ring[i], ring[(i + step) % 4]) for i in range...  18.3 us
    ppermute x2, starting transfers between devices, turn(): return lax.ppermute(value, TURN_AXES, pairs)  10.3 us
    ppermute x3, waiting for transfers between devices, other_core(): return lax.ppermute(value, 'core', [(0, 1), (1, 0)])  8.76 us
    all_to_all x1, starting transfers between devices, per_device(): blocks = lax.all_to_all(blocks, ('x_lo', 'y', 'x_hi'), 0, 0, tiled=True)  7.61 us
  transfers between devices with their start and end apart: 20, of which 14 were waited for; matrix products, arithmetic and copies ran while one was open for 3% of the time, Pallas kernels for 0%

profile of v6, /device:TPU:28, one launch (start us, length us, event | category | flops | bytes accessed | tf_op | source)
XLA Modules:
  0.0 248.3 jit_solution(7271126015232534381)
XLA Ops:
  7.2 1.5 reduce
  8.7 5.6 %collective-permute-start = (f32[6,24,384]{2,1,0:T(8,128)S(1)}, f32[6,24,384]{2,1,0:T(8,128)}, u32[]{:S(2)}, u32[]{:S(2)}) collective-permute-start(f32[6,24,384]{2,1,0:T(8,128)S(1)} %bitcast.64), channel_id=1, source_target_pairs={{0,0},{1,64},{4,16},{5,80},{8,32},{9,96},{12,48},{13,112},{16,4},{... | collective-permute-start | bytes 663560 | tf_op jit(solution)/shard_map/ppermute | solution.py:345
  14.3 2.6 %copy.17 = f32[12,8,24,384]{3,2,1,0:T(8,128)S(1)} copy(f32[12,8,24,384]{3,1,2,0:T(8,128)} %bitcast.58) | data formatting | bytes 7077888
  16.9 10.1 %collective-permute-done = f32[6,24,384]{2,1,0:T(8,128)} collective-permute-done((f32[6,24,384]{2,1,0:T(8,128)S(1)}, f32[6,24,384]{2,1,0:T(8,128)}, u32[]{:S(2)}, u32[]{:S(2)}) %collective-permute-start) | collective-permute-done | bytes 221216 | tf_op jit(solution)/shard_map/ppermute | solution.py:345
  27.0 2.0 copy.13
  29.1 7.6 %all-to-all-start = ((f32[16,6,24,384]{3,2,1,0:T(8,128)}), f32[16,6,24,384]{3,2,1,0:T(8,128)S(1)}, u32[]{:S(2)}, u32[]{:S(2)}) async-start(f32[16,6,24,384]{3,2,1,0:T(8,128)} %copy.13), calls=%async_computation | async-start | bytes 7077888 | tf_op jit(solution)/shard_map/all_to_all | solution.py:400
  36.7 0.7 all-gather.3.cloned.1.call-update
  37.5 0.6 fusion.5
  42.0 42.4 %all-to-all-done = f32[16,6,24,384]{3,2,1,0:T(8,128)S(1)} async-done(((f32[16,6,24,384]{3,2,1,0:T(8,128)}), f32[16,6,24,384]{3,2,1,0:T(8,128)S(1)}, u32[]{:S(2)}, u32[]{:S(2)}) %all-to-all-start) | async-done | bytes 3538976 | tf_op jit(solution)/shard_map/all_to_all | solution.py:400
  84.4 0.1 fusion.4
  84.5 1.4 collective-permute-start.1
  85.9 0.7 collective-permute-start.2
  86.6 17.0 %collective-permute-done.1 = f32[2,2,6,24,384]{4,3,2,1,0:T(8,128)S(1)} collective-permute-done((f32[2,2,6,24,384]{4,3,2,1,0:T(8,128)S(1)}, f32[2,2,6,24,384]{4,3,2,1,0:T(8,128)S(1)}, u32[]{:S(2)}, u32[]{:S(2)}) %collective-permute-start.1) | collective-permute-done | bytes 884768 | tf_op jit(solution)/shard_map/ppermute | solution.py:358
  103.6 1.3 collective-permute-done.2
  104.9 0.2 pad_maximum_fusion.own
  105.0 0.1 collective-permute-start.3
  105.2 0.5 collective-permute-start.4
  105.7 2.9 %collective-permute-start.5 = (f32[1,2,6,24,384]{4,3,2,1,0:T(8,128)S(1)}, f32[1,2,6,24,384]{4,3,2,1,0:T(8,128)S(1)}, u32[]{:S(2)}, u32[]{:S(2)}) collective-permute-start(f32[1,2,6,24,384]{4,3,2,1,0:T(8,128)S(1)} %slice.94), channel_id=1, source_target_pairs={{0,12},{4,0},{8,4},{12,8},{1,13},{5,1},{9,5},{13,9},{2,14},{6,2},{... | collective-permute-start | bytes 1327112 | tf_op jit(solution)/shard_map/ppermute | solution.py:358
  108.6 10.4 %collective-permute-done.4 = f32[1,2,6,24,384]{4,3,2,1,0:T(8,128)S(1)} collective-permute-done((f32[1,2,6,24,384]{4,3,2,1,0:T(8,128)S(1)}, f32[1,2,6,24,384]{4,3,2,1,0:T(8,128)S(1)}, u32[]{:S(2)}, u32[]{:S(2)}) %collective-permute-start.4) | collective-permute-done | bytes 442400 | tf_op jit(solution)/shard_map/ppermute | solution.py:358
  119.1 0.3 collective-permute-start.6
  119.4 0.1 pad_add_fusion.ids
  119.5 2.5 collective-permute-done.6.other_far
  121.9 1.1 copy-done
  123.1 1.0 copy-done.1
  124.1 33.5 %shard_map.68 = (f32[4,2,2,6,24,384]{5,4,3,2,1,0:T(8,128)}, f32[4,2,2,6,24,384]{5,4,3,2,1,0:T(8,128)}, f32[4,4,6,24,384]{4,3,2,1,0:T(8,128)}) custom-call(s32[3]{0:T(128)S(1)} %pad_add_fusion.ids, f32[4,4,6,24,384]{4,3,2,1,0:T(8,128)} %bitcast.65, f32[3,2,2,6,24,384]{5,4,3,2,1,0:T(8,128)S(1)} %pad_maximum_fusion.own, ...), custom_call_target="tpu_custom_call" | custom-call | flops 12230590464 | bytes 35000000 | tf_op jit(solution)/shard_map/pallas_call | solution.py:304
  157.6 0.2 collective-permute-start.7
  157.8 6.3 %collective-permute-done.7 = f32[4,2,2,6,24,384]{5,4,3,2,1,0:T(8,128)S(1)} collective-permute-done((f32[4,2,2,6,24,384]{5,4,3,2,1,0:T(8,128)}, f32[4,2,2,6,24,384]{5,4,3,2,1,0:T(8,128)S(1)}, u32[]{:S(2)}, u32[]{:S(2)}) %collective-permute-start.7) | collective-permute-done | bytes 3538976 | tf_op jit(solution)/shard_map/ppermute | solution.py:349
  164.1 0.5 add.43
  164.6 0.1 slice_bitcast_fusion.5
  164.7 3.1 %collective-permute-start.10 = (f32[1,2,6,24,384]{4,3,2,1,0:T(8,128)S(1)}, f32[1,2,6,24,384]{4,3,2,1,0:T(8,128)S(1)}, u32[]{:S(2)}, u32[]{:S(2)}) collective-permute-start(f32[1,2,6,24,384]{4,3,2,1,0:T(8,128)S(1)} %get-tuple-element.25), channel_id=1, source_target_pairs={{0,12},{4,0},{8,4},{12,8},{1,13},{5,1},{9,5},{13,9},{2,14},{6,2},{... | collective-permute-start | bytes 1327112 | tf_op jit(solution)/shard_map/ppermute | solution.py:358
  167.8 9.7 %collective-permute-done.10 = f32[1,2,6,24,384]{4,3,2,1,0:T(8,128)S(1)} collective-permute-done((f32[1,2,6,24,384]{4,3,2,1,0:T(8,128)S(1)}, f32[1,2,6,24,384]{4,3,2,1,0:T(8,128)S(1)}, u32[]{:S(2)}, u32[]{:S(2)}) %collective-permute-start.10) | collective-permute-done | bytes 442400 | tf_op jit(solution)/shard_map/ppermute | solution.py:358
  177.5 3.4 %collective-permute-done.8 = f32[1,2,6,24,384]{4,3,2,1,0:T(8,128)S(1)} collective-permute-done((f32[1,2,6,24,384]{4,3,2,1,0:T(8,128)S(1)}, f32[1,2,6,24,384]{4,3,2,1,0:T(8,128)S(1)}, u32[]{:S(2)}, u32[]{:S(2)}) %collective-permute-start.8) | collective-permute-done | bytes 442400 | tf_op jit(solution)/shard_map/ppermute | solution.py:358
  180.9 0.1 fusion.3
  181.3 3.3 %collective-permute-start.11 = (f32[2,2,6,24,384]{4,3,2,1,0:T(8,128)S(1)}, f32[2,2,6,24,384]{4,3,2,1,0:T(8,128)S(1)}, u32[]{:S(2)}, u32[]{:S(2)}) collective-permute-start(f32[2,2,6,24,384]{4,3,2,1,0:T(8,128)S(1)} %pad_maximum_fusion.3), channel_id=1, source_target_pairs={{0,12},{4,0},{8,4},{12,8},{1,13},{5,1},{9,5},{13,9},{2,14},{6,2},{... | collective-permute-start | bytes 2654216 | tf_op jit(solution)/shard_map/ppermute | solution.py:358
  184.6 18.4 %collective-permute-done.9 = f32[2,2,6,24,384]{4,3,2,1,0:T(8,128)S(1)} collective-permute-done((f32[2,2,6,24,384]{4,3,2,1,0:T(8,128)S(1)}, f32[2,2,6,24,384]{4,3,2,1,0:T(8,128)S(1)}, u32[]{:S(2)}, u32[]{:S(2)}) %collective-permute-start.9) | collective-permute-done | bytes 884768 | tf_op jit(solution)/shard_map/ppermute | solution.py:358
  202.9 0.1 fusion.1
  203.1 0.6 reduce-scatter.2.cloned.1.call-done
  203.6 1.2 slice_bitcast_fusion.8
  204.8 2.9 %collective-permute-start.12 = (f32[6,24,384]{2,1,0:T(8,128)S(1)}, f32[6,24,384]{2,1,0:T(8,128)S(1)}, u32[]{:S(2)}, u32[]{:S(2)}) collective-permute-start(f32[6,24,384]{2,1,0:T(8,128)S(1)} %get-tuple-element.34), channel_id=1, source_target_pairs={{0,16},{16,32},{32,48},{48,0},{1,17},{17,33},{33,49},{49,1},{2,18}... | collective-permute-start | bytes 663560 | tf_op jit(solution)/shard_map/ppermute | solution.py:358
  207.7 3.5 %collective-permute-start.13 = (f32[6,24,384]{2,1,0:T(8,128)S(1)}, f32[6,24,384]{2,1,0:T(8,128)S(1)}, u32[]{:S(2)}, u32[]{:S(2)}) collective-permute-start(f32[6,24,384]{2,1,0:T(8,128)S(1)} %get-tuple-element.32), channel_id=1, source_target_pairs={{0,32},{16,48},{32,0},{48,16},{1,33},{17,49},{33,1},{49,17},{2,34}... | collective-permute-start | bytes 663560 | tf_op jit(solution)/shard_map/ppermute | solution.py:358
  211.3 4.1 %collective-permute-start.16 = (f32[2,1,6,24,384]{4,3,2,1,0:T(8,128)S(1)}, f32[2,1,6,24,384]{4,3,2,1,0:T(8,128)S(1)}, u32[]{:S(2)}, u32[]{:S(2)}) collective-permute-start(f32[2,1,6,24,384]{4,3,2,1,0:T(8,128)S(1)} %constant_dynamic-slice_fusion), channel_id=1, source_target_pairs={{0,2},{2,0},{1,3},{3,1},{4,6},{6,4},{5,7},{7,5},{8,10},{10,8},{9,1... | collective-permute-start | bytes 1327112 | tf_op jit(solution)/shard_map/ppermute | solution.py:417
  215.3 1.7 collective-permute-done.13
  217.1 2.6 %collective-permute-done.14 = f32[6,24,384]{2,1,0:T(8,128)S(1)} collective-permute-done((f32[6,24,384]{2,1,0:T(8,128)S(1)}, f32[6,24,384]{2,1,0:T(8,128)S(1)}, u32[]{:S(2)}, u32[]{:S(2)}) %collective-permute-start.14) | collective-permute-done | bytes 221216 | tf_op jit(solution)/shard_map/ppermute | solution.py:358
  219.6 1.0 bitcast_add_fusion
  220.6 4.7 %collective-permute-start.15 = (f32[6,24,384]{2,1,0:T(8,128)S(1)}, f32[6,24,384]{2,1,0:T(8,128)S(1)}, u32[]{:S(2)}, u32[]{:S(2)}) collective-permute-start(f32[6,24,384]{2,1,0:T(8,128)S(1)} %bitcast_add_fusion), channel_id=1, source_target_pairs={{0,0},{1,64},{4,16},{5,80},{8,32},{9,96},{12,48},{13,112},{16,4},{... | collective-permute-start | bytes 663560 | tf_op jit(solution)/shard_map/ppermute | solution.py:345
  225.4 13.5 %collective-permute-done.15 = f32[6,24,384]{2,1,0:T(8,128)S(1)} collective-permute-done((f32[6,24,384]{2,1,0:T(8,128)S(1)}, f32[6,24,384]{2,1,0:T(8,128)S(1)}, u32[]{:S(2)}, u32[]{:S(2)}) %collective-permute-start.15) | collective-permute-done | bytes 221216 | tf_op jit(solution)/shard_map/ppermute | solution.py:345
  238.9 0.9 reshape.36
  240.0 1.4 reshape.33
  (30 shorter events, 0.8 us)
Async XLA Ops:
  8.7 18.4 %collective-permute-start = (f32[6,24,384]{2,1,0:T(8,128)S(1)}, f32[6,24,384]{2,1,0:T(8,128)}, u32[]{:S(2)}, u32[]{:S(2)}) collective-permute-start(f32[6,24,384]{2,1,0:T(8,128)S(1)} %bitcast.64), channel_id=1, source_target_pairs={{0,0},{1,64},{4,16},{5,80},{8,32},{9,96},{12,48},{13,112},{16,4},{... | collective-permute-start | bytes 663560 | tf_op jit(solution)/shard_map/ppermute | solution.py:345
  29.1 8.4 %copy-start.3 = (s32[2]{0:T(128)S(1)}, s32[2]{0:T(128)}, u32[]{:S(2)}) copy-start(s32[2]{0:T(128)} %param.7) | copy-start | bytes 28
  29.1 55.2 %all-to-all-start = ((f32[16,6,24,384]{3,2,1,0:T(8,128)}), f32[16,6,24,384]{3,2,1,0:T(8,128)S(1)}, u32[]{:S(2)}, u32[]{:S(2)}) async-start(f32[16,6,24,384]{3,2,1,0:T(8,128)} %copy.13), calls=%async_computation | async-start | bytes 7077888 | tf_op jit(solution)/shard_map/all_to_all | solution.py:400
  36.7 85.2 %all-gather.3.cloned.1.call-start = ((), (), s32[]{:S(2)}) async-start(), calls=%async_computation.3 | async-start | bytes 3760128 | tf_op jit(solution)/shard_map/all_gather | solution.py:398
  37.4 166.2 %reduce-scatter.2.cloned.1.call-start = ((), (), s32[]{:S(2)}) async-start(), calls=%async_computation.2 | async-start | bytes 4423680 | tf_op jit(solution)/shard_map/reduce_scatter | solution.py:410
  84.5 19.1 %collective-permute-start.1 = (f32[2,2,6,24,384]{4,3,2,1,0:T(8,128)S(1)}, f32[2,2,6,24,384]{4,3,2,1,0:T(8,128)S(1)}, u32[]{:S(2)}, u32[]{:S(2)}) collective-permute-start(f32[2,2,6,24,384]{4,3,2,1,0:T(8,128)S(1)} %get-tuple-element.36), channel_id=1, source_target_pairs={{0,12},{4,0},{8,4},{12,8},{1,13},{5,1},{9,5},{13,9},{2,14},{6,2},{... | collective-permute-start | bytes 2654216 | tf_op jit(solution)/shard_map/ppermute | solution.py:358
  85.9 19.0 %collective-permute-start.2 = (f32[2,2,6,24,384]{4,3,2,1,0:T(8,128)S(1)}, f32[2,2,6,24,384]{4,3,2,1,0:T(8,128)S(1)}, u32[]{:S(2)}, u32[]{:S(2)}) collective-permute-start(f32[2,2,6,24,384]{4,3,2,1,0:T(8,128)S(1)} %get-tuple-element.36), channel_id=1, source_target_pairs={{0,4},{4,8},{8,12},{12,0},{1,5},{5,9},{9,13},{13,1},{2,6},{6,10},{... | collective-permute-start | bytes 2654216 | tf_op jit(solution)/shard_map/ppermute | solution.py:358
  105.0 16.9 %collective-permute-start.3 = (f32[3,2,2,6,24,384]{5,4,3,2,1,0:T(8,128)S(1)}, f32[3,2,2,6,24,384]{5,4,3,2,1,0:T(8,128)}, u32[]{:S(2)}, u32[]{:S(2)}) collective-permute-start(f32[3,2,2,6,24,384]{5,4,3,2,1,0:T(8,128)S(1)} %pad_maximum_fusion.own), channel_id=1, source_target_pairs={{0,1},{1,0},{2,3},{3,2},{4,5},{5,4},{6,7},{7,6},{8,9},{9,8},{10,11... | collective-permute-start | bytes 7962632 | tf_op jit(solution)/shard_map/ppermute | solution.py:349
  105.2 13.8 %collective-permute-start.4 = (f32[1,2,6,24,384]{4,3,2,1,0:T(8,128)S(1)}, f32[1,2,6,24,384]{4,3,2,1,0:T(8,128)S(1)}, u32[]{:S(2)}, u32[]{:S(2)}) collective-permute-start(f32[1,2,6,24,384]{4,3,2,1,0:T(8,128)S(1)} %slice.93), channel_id=1, source_target_pairs={{0,4},{4,8},{8,12},{12,0},{1,5},{5,9},{9,13},{13,1},{2,6},{6,10},{... | collective-permute-start | bytes 1327112 | tf_op jit(solution)/shard_map/ppermute | solution.py:358
  105.7 13.3 %collective-permute-start.5 = (f32[1,2,6,24,384]{4,3,2,1,0:T(8,128)S(1)}, f32[1,2,6,24,384]{4,3,2,1,0:T(8,128)S(1)}, u32[]{:S(2)}, u32[]{:S(2)}) collective-permute-start(f32[1,2,6,24,384]{4,3,2,1,0:T(8,128)S(1)} %slice.94), channel_id=1, source_target_pairs={{0,12},{4,0},{8,4},{12,8},{1,13},{5,1},{9,5},{13,9},{2,14},{6,2},{... | collective-permute-start | bytes 1327112 | tf_op jit(solution)/shard_map/ppermute | solution.py:358
  119.1 2.8 %collective-permute-start.6 = (f32[2,2,6,24,384]{4,3,2,1,0:T(8,128)S(1)}, f32[2,2,6,24,384]{4,3,2,1,0:T(8,128)}, u32[]{:S(2)}, u32[]{:S(2)}) collective-permute-start(f32[2,2,6,24,384]{4,3,2,1,0:T(8,128)S(1)} %constant_dynamic-update-slice_fusion.own_far), channel_id=1, source_target_pairs={{0,1},{1,0},{2,3},{3,2},{4,5},{5,4},{6,7},{7,6},{8,9},{9,8},{10,11... | collective-permute-start | bytes 2654216 | tf_op jit(solution)/shard_map/ppermute | solution.py:349
  121.9 1.1 copy-start
  123.1 1.0 copy-start.1
  157.6 6.5 %copy-start.2 = (f32[4,2,2,6,24,384]{5,4,3,2,1,0:T(8,128)S(1)}, f32[4,2,2,6,24,384]{5,4,3,2,1,0:T(8,128)}, u32[]{:S(2)}) copy-start(f32[4,2,2,6,24,384]{5,4,3,2,1,0:T(8,128)} %get-tuple-element.11) | copy-start | bytes 10616836
  157.6 6.5 %collective-permute-start.7 = (f32[4,2,2,6,24,384]{5,4,3,2,1,0:T(8,128)}, f32[4,2,2,6,24,384]{5,4,3,2,1,0:T(8,128)S(1)}, u32[]{:S(2)}, u32[]{:S(2)}) collective-permute-start(f32[4,2,2,6,24,384]{5,4,3,2,1,0:T(8,128)} %get-tuple-element.12), channel_id=1, source_target_pairs={{0,1},{1,0},{2,3},{3,2},{4,5},{5,4},{6,7},{7,6},{8,9},{9,8},{10,11... | collective-permute-start | bytes 10616840 | tf_op jit(solution)/shard_map/ppermute | solution.py:349
  164.7 12.8 %collective-permute-start.10 = (f32[1,2,6,24,384]{4,3,2,1,0:T(8,128)S(1)}, f32[1,2,6,24,384]{4,3,2,1,0:T(8,128)S(1)}, u32[]{:S(2)}, u32[]{:S(2)}) collective-permute-start(f32[1,2,6,24,384]{4,3,2,1,0:T(8,128)S(1)} %get-tuple-element.25), channel_id=1, source_target_pairs={{0,12},{4,0},{8,4},{12,8},{1,13},{5,1},{9,5},{13,9},{2,14},{6,2},{... | collective-permute-start | bytes 1327112 | tf_op jit(solution)/shard_map/ppermute | solution.py:358
  167.8 13.1 %collective-permute-start.8 = (f32[1,2,6,24,384]{4,3,2,1,0:T(8,128)S(1)}, f32[1,2,6,24,384]{4,3,2,1,0:T(8,128)S(1)}, u32[]{:S(2)}, u32[]{:S(2)}) collective-permute-start(f32[1,2,6,24,384]{4,3,2,1,0:T(8,128)S(1)} %get-tuple-element.24), channel_id=1, source_target_pairs={{0,4},{4,8},{8,12},{12,0},{1,5},{5,9},{9,13},{13,1},{2,6},{6,10},{... | collective-permute-start | bytes 1327112 | tf_op jit(solution)/shard_map/ppermute | solution.py:358
  181.1 21.8 %collective-permute-start.9 = (f32[2,2,6,24,384]{4,3,2,1,0:T(8,128)S(1)}, f32[2,2,6,24,384]{4,3,2,1,0:T(8,128)S(1)}, u32[]{:S(2)}, u32[]{:S(2)}) collective-permute-start(f32[2,2,6,24,384]{4,3,2,1,0:T(8,128)S(1)} %pad_maximum_fusion.2), channel_id=1, source_target_pairs={{0,4},{4,8},{8,12},{12,0},{1,5},{5,9},{9,13},{13,1},{2,6},{6,10},{... | collective-permute-start | bytes 2654216 | tf_op jit(solution)/shard_map/ppermute | solution.py:358
  181.3 21.7 %collective-permute-start.11 = (f32[2,2,6,24,384]{4,3,2,1,0:T(8,128)S(1)}, f32[2,2,6,24,384]{4,3,2,1,0:T(8,128)S(1)}, u32[]{:S(2)}, u32[]{:S(2)}) collective-permute-start(f32[2,2,6,24,384]{4,3,2,1,0:T(8,128)S(1)} %pad_maximum_fusion.3), channel_id=1, source_target_pairs={{0,12},{4,0},{8,4},{12,8},{1,13},{5,1},{9,5},{13,9},{2,14},{6,2},{... | collective-permute-start | bytes 2654216 | tf_op jit(solution)/shard_map/ppermute | solution.py:358
  204.8 10.5 %collective-permute-start.12 = (f32[6,24,384]{2,1,0:T(8,128)S(1)}, f32[6,24,384]{2,1,0:T(8,128)S(1)}, u32[]{:S(2)}, u32[]{:S(2)}) collective-permute-start(f32[6,24,384]{2,1,0:T(8,128)S(1)} %get-tuple-element.34), channel_id=1, source_target_pairs={{0,16},{16,32},{32,48},{48,0},{1,17},{17,33},{33,49},{49,1},{2,18}... | collective-permute-start | bytes 663560 | tf_op jit(solution)/shard_map/ppermute | solution.py:358
  207.7 9.3 %collective-permute-start.13 = (f32[6,24,384]{2,1,0:T(8,128)S(1)}, f32[6,24,384]{2,1,0:T(8,128)S(1)}, u32[]{:S(2)}, u32[]{:S(2)}) collective-permute-start(f32[6,24,384]{2,1,0:T(8,128)S(1)} %get-tuple-element.32), channel_id=1, source_target_pairs={{0,32},{16,48},{32,0},{48,16},{1,33},{17,49},{33,1},{49,17},{2,34}... | collective-permute-start | bytes 663560 | tf_op jit(solution)/shard_map/ppermute | solution.py:358
  211.2 8.4 %collective-permute-start.14 = (f32[6,24,384]{2,1,0:T(8,128)S(1)}, f32[6,24,384]{2,1,0:T(8,128)S(1)}, u32[]{:S(2)}, u32[]{:S(2)}) collective-permute-start(f32[6,24,384]{2,1,0:T(8,128)S(1)} %get-tuple-element.33), channel_id=1, source_target_pairs={{0,48},{16,0},{32,16},{48,32},{1,49},{17,1},{33,17},{49,33},{2,50}... | collective-permute-start | bytes 663560 | tf_op jit(solution)/shard_map/ppermute | solution.py:358
  211.3 28.5 %collective-permute-start.16 = (f32[2,1,6,24,384]{4,3,2,1,0:T(8,128)S(1)}, f32[2,1,6,24,384]{4,3,2,1,0:T(8,128)S(1)}, u32[]{:S(2)}, u32[]{:S(2)}) collective-permute-start(f32[2,1,6,24,384]{4,3,2,1,0:T(8,128)S(1)} %constant_dynamic-slice_fusion), channel_id=1, source_target_pairs={{0,2},{2,0},{1,3},{3,1},{4,6},{6,4},{5,7},{7,5},{8,10},{10,8},{9,1... | collective-permute-start | bytes 1327112 | tf_op jit(solution)/shard_map/ppermute | solution.py:417
  220.6 18.3 %collective-permute-start.15 = (f32[6,24,384]{2,1,0:T(8,128)S(1)}, f32[6,24,384]{2,1,0:T(8,128)S(1)}, u32[]{:S(2)}, u32[]{:S(2)}) collective-permute-start(f32[6,24,384]{2,1,0:T(8,128)S(1)} %bitcast_add_fusion), channel_id=1, source_target_pairs={{0,0},{1,64},{4,16},{5,80},{8,32},{9,96},{12,48},{13,112},{16,4},{... | collective-permute-start | bytes 663560 | tf_op jit(solution)/shard_map/ppermute | solution.py:345
Sparse Core Ops, SparseCore 0:
  39.7 71.9 all-gather.2
  157.7 45.8 reduce-scatter.1
